TPU v7x, 32 devices: a whole 2x2x4 slice. The times are simulated.
32 devices in a mesh: seq: 4 (over z), batch: 4 (over y, x), head: 2 (over core).
Axes of the slice: x: 2, y: 2, z: 4, core: 2. Of those that a mesh axis runs over, the one named last changes fastest.
Arguments:
- tokens: bfloat16 [4, 2048, 2048], P('batch', 'seq'), may hold values from -6 to 6
- prescale: float32 [2048], replicated, may hold values from 0.25 to 1.75
- query_weight: bfloat16 [2048, 2048], P('seq', 'head'), may hold values from -0.125 to 0.125
- key_weight: bfloat16 [2048, 2048], P('seq', 'head'), may hold values from -0.125 to 0.125
- value_weight: bfloat16 [2048, 4096], P('seq', 'head'), may hold values from -0.125 to 0.125
- gate_weight: bfloat16 [2048, 4096], P('seq', 'head'), may hold values from -0.125 to 0.125
- groupscale: float32 [4096], P('head'), may hold values from 0.25 to 1.75
- groupshift: float32 [4096], P('head'), may hold values from -3 to 3
- output_weight: bfloat16 [4096, 2048], P('head', 'seq'), may hold values from -0.09375 to 0.09375
- postscale: float32 [2048], replicated, may hold values from 0.25 to 1.75
- postshift: float32 [2048], replicated, may hold values from -3 to 3
- expand_weight: bfloat16 [2048, 4096], P('seq', 'head'), may hold values from -0.125 to 0.125
- hiddenbias: float32 [4096], P('head'), may hold values from -3 to 3
- reduce_weight: bfloat16 [4096, 2048], P('head', 'seq'), may hold values from -0.09375 to 0.09375
- outputbias: float32 [2048], replicated, may hold values from -3 to 3
- cotangent: bfloat16 [4, 2048, 2048], P('batch', 'seq'), may hold values from -6 to 6
- doc_lengths: int32 [4, 8], P('batch'), may hold values from 1 to 512, 2048 in all within a row
- segments: int32 [4, 2048], P('batch', 'seq'), may hold values from 0 to 2, as said below
Outputs:
- layer_output: bfloat16 [4, 2048, 2048], P('batch', 'seq')
- tokens_grad: float32 [4, 2048, 2048], P('batch', 'seq')
- prescale_grad: float32 [2048], replicated
- query_grad: float32 [2048, 2048], P('seq', 'head')
- key_grad: float32 [2048, 2048], P('seq', 'head')
- value_grad: float32 [2048, 4096], P('seq', 'head')
- gate_grad: float32 [2048, 4096], P('seq', 'head')
- groupscale_grad: float32 [4096], P('head')
- groupshift_grad: float32 [4096], P('head')
- output_grad: float32 [4096, 2048], P('head', 'seq')
- postscale_grad: float32 [2048], replicated
- postshift_grad: float32 [2048], replicated
- expand_grad: float32 [2048, 4096], P('seq', 'head')
- hiddenbias_grad: float32 [4096], P('head')
- reduce_grad: float32 [4096, 2048], P('head', 'seq')
- outputbias_grad: float32 [2048], replicated
Inputs may be any that keep to these rules, and one draw needn't show every extreme that they name: segments are non-decreasing along each stream, 0 at its first token and 2 at its last; the id rises by one or more at each reset.
All inputs are finite; a program needn't handle non-finite values.
Results may differ from a plain program's by a relative error of at most 0.019.
Values may be sent and summed in bfloat16 or wider, within the bound.
No kernel may reach another device: no remote copies, remote signals or barrier semaphores. Data moves between devices by JAX's collectives and lax.ppermute only.
A program may use at most 384 MiB of HBM per device.

v0:
```python
import math

import jax
import jax.numpy as jnp
from jax import lax
from jax.sharding import PartitionSpec as P

HEADS = 8
KEY = 256
VAL = 512


def from_behind(value, axis, steps):
    count = lax.axis_size(axis)
    leading, last = (max(0, -steps), min(count, count - steps))
    return lax.ppermute(value, axis, [(source, source + steps) for source in range(leading, last)])


def entering(part, axis, combine, identity):
    place = lax.axis_index(axis)
    gathered = jax.tree.map(lambda a: lax.all_gather(a, axis), part)
    state = jax.tree.map(lambda a, e: jnp.zeros_like(a) + jnp.asarray(e, a.dtype), part, identity)

    def one(hop, state):
        return combine(
            state, jax.tree.map(lambda a: lax.dynamic_index_in_dim(a, hop, 0, False), gathered)
        )

    return lax.fori_loop(0, place, one, state)


def entering_2(array, axis, join, neutral):
    count = lax.axis_size(axis)
    place = lax.axis_index(axis)
    ahead = count - 1 - place
    gathered = jax.tree.map(
        lambda a, kind: lax.all_gather(a.astype(kind), axis), array, (jnp.bfloat16, jnp.bfloat16)
    )
    state = jax.tree.map(lambda a, e: jnp.zeros_like(a) + jnp.asarray(e, a.dtype), array, neutral)

    def one(hop, state):
        source = count - 1 - hop
        return join(
            state,
            jax.tree.map(
                lambda a, own: lax.dynamic_index_in_dim(a, source, 0, False).astype(own.dtype),
                gathered,
                array,
            ),
        )

    return lax.fori_loop(0, ahead, one, state)


def decay_logs(number, offset):
    heads_at = (offset + jnp.arange(number, dtype=jnp.int32)).astype(jnp.float32)
    return jnp.log1p(-jnp.exp2(-5.0 - heads_at))


def doc_positions(lengths, offset, number):
    doc_ends = jnp.cumsum(lengths)
    indices = offset + jnp.arange(number, dtype=jnp.int32)
    passed = jnp.where(doc_ends[None, :] <= indices[:, None], lengths[None, :], 0)
    doc_starts = jnp.sum(passed, axis=1)
    return (indices - doc_starts).astype(jnp.float32)


def rotation_tables(positions, key_size):
    middle = key_size // 2
    frequency = jnp.exp(-math.log(10000.0) * jnp.arange(middle, dtype=jnp.float32) / (middle - 1))
    phases = positions[..., None] * frequency
    return (jnp.cos(phases), jnp.sin(phases))


def rotate(values, cosine_table, sine_table):
    middle = values.shape[-1] // 2
    former, latter = (values[..., :middle], values[..., middle:])
    return jnp.concatenate(
        [former * cosine_table - latter * sine_table, latter * cosine_table + former * sine_table],
        axis=-1,
    )


def rotate_back(values, cosine_table, sine_table):
    middle = values.shape[-1] // 2
    former, latter = (values[..., :middle], values[..., middle:])
    return jnp.concatenate(
        [former * cosine_table + latter * sine_table, latter * cosine_table - former * sine_table],
        axis=-1,
    )


def contract_rows(left_side, right_side):
    return lax.dot_general(
        left_side, right_side, (((0,), (0,)), ((), ())), preferred_element_type=jnp.float32
    )


def contract_cols(left_side, right_side):
    return lax.dot_general(
        left_side, right_side, (((1,), (1,)), ((), ())), preferred_element_type=jnp.float32
    )


def chain(earlier, latter):
    return (earlier[0] * latter[0], latter[0][:, :, None, None] * earlier[1] + latter[1])


def normalize_back(grad_unit, unit_norm, inverse):
    mean_grad = jnp.mean(grad_unit, axis=-1, keepdims=True)
    mean_cross = jnp.mean(grad_unit * unit_norm, axis=-1, keepdims=True)
    return inverse * (grad_unit - mean_grad - unit_norm * mean_cross)


def retention_tables(segments, before, log_rates, block_size):
    indices = jnp.arange(block_size, dtype=jnp.int32)
    distance = indices[:, None] - indices[None, :]
    causal = distance >= 0
    decays = jnp.exp(
        jnp.where(causal, distance, 0).astype(jnp.float32)[None] * log_rates[:, None, None]
    )
    linked = (segments[:, :, None] == segments[:, None, :]) & causal[None]
    decay_matrix = jnp.where(linked[:, None], decays[None], 0.0)
    last_segment = segments[:, block_size - 1]
    entry_rate = jnp.exp(
        (indices + 1).astype(jnp.float32)[None, :, None] * log_rates[None, None, :]
    )
    entry_weight = entry_rate * (segments == before[:, None]).astype(jnp.float32)[:, :, None]
    exit_rate = jnp.exp(
        (block_size - 1 - indices).astype(jnp.float32)[None, :, None] * log_rates[None, None, :]
    )
    exit_weight = exit_rate * (segments == last_segment[:, None]).astype(jnp.float32)[:, :, None]
    carried = (
        jnp.exp(block_size * log_rates)[None, :]
        * (last_segment == before).astype(jnp.float32)[:, None]
    )
    return (decay_matrix, entry_weight[..., None], exit_weight[..., None], carried)


def retention_mixing(queries, keys_in, decay_matrix):
    scores = jnp.einsum("bnhk,bmhk->bhnm", queries, keys_in, preferred_element_type=jnp.float32)
    return (scores * decay_matrix).astype(jnp.bfloat16)


def body(
    tokens,
    prescale,
    query_weight,
    key_weight,
    value_weight,
    gate_weight,
    groupscale,
    groupshift,
    output_weight,
    postscale,
    postshift,
    expand_weight,
    hiddenbias,
    reduce_weight,
    outputbias,
    cotangent,
    doc_lengths,
    segments,
):
    streams, block_size, model_width = tokens.shape
    row_count = streams * block_size
    head_count = HEADS // lax.axis_size("head")
    gathered = (
        lax.all_gather(query_weight, "seq", axis=0, tiled=True),
        lax.all_gather(key_weight, "seq", axis=0, tiled=True),
        lax.all_gather(value_weight, "seq", axis=0, tiled=True),
        lax.all_gather(gate_weight, "seq", axis=0, tiled=True),
        lax.all_gather(output_weight, "seq", axis=1, tiled=True),
        lax.all_gather(expand_weight, "seq", axis=0, tiled=True),
        lax.all_gather(reduce_weight, "seq", axis=1, tiled=True),
    )
    query_full, key_full, value_full, gate_full, output_full, expand_full, reduce_full = gathered
    inputs = tokens.reshape(row_count, model_width).astype(jnp.float32)
    inverse = lax.rsqrt(jnp.mean(inputs * inputs, axis=-1, keepdims=True) + 1e-06)
    scaled = inputs * inverse
    normed = (scaled * prescale).astype(jnp.bfloat16)
    query_pre = jnp.dot(normed, query_full, preferred_element_type=jnp.float32)
    key_pre = jnp.dot(normed, key_full, preferred_element_type=jnp.float32)
    value_all = jnp.dot(normed, value_full, preferred_element_type=jnp.float32).astype(jnp.bfloat16)
    gate_pre = jnp.dot(normed, gate_full, preferred_element_type=jnp.float32)
    offset = lax.axis_index("seq") * block_size
    positions = jnp.stack([doc_positions(doc_lengths[0], offset, block_size)])
    cosine_table, sine_table = rotation_tables(positions, KEY)
    cosine_table = cosine_table[:, :, None, :]
    sine_table = sine_table[:, :, None, :]
    queries = rotate(
        query_pre.reshape(streams, block_size, head_count, KEY), cosine_table, sine_table
    ).astype(jnp.bfloat16)
    keys_in = (
        rotate(key_pre.reshape(streams, block_size, head_count, KEY), cosine_table, sine_table)
        * KEY ** (-0.5)
    ).astype(jnp.bfloat16)
    values = value_all.reshape(streams, block_size, head_count, VAL)
    log_rates = decay_logs(head_count, lax.axis_index("head") * head_count)
    before = from_behind(segments[:, block_size - 1 :], "seq", 1)[:, 0]
    first_block = lax.axis_index("seq") == 0
    before = jnp.where(first_block, jnp.full_like(before, -1), before)
    decay_matrix, entry_weight, exit_weight, carried = retention_tables(
        segments, before, log_rates, block_size
    )
    query_incoming = (queries.astype(jnp.float32) * entry_weight).astype(jnp.bfloat16)
    key_projected = (keys_in.astype(jnp.float32) * exit_weight).astype(jnp.bfloat16)
    state_increment = jnp.einsum(
        "bmhk,bmhv->bhkv", key_projected, values, preferred_element_type=jnp.float32
    )
    prefix_keep, memory_in = entering(
        (carried, state_increment),
        "seq",
        chain,
        (jnp.ones_like(carried), jnp.zeros_like(state_increment)),
    )
    memory_low = memory_in.astype(jnp.bfloat16)
    mixing = retention_mixing(queries, keys_in, decay_matrix)
    retained = jnp.einsum("bhnm,bmhv->bnhv", mixing, values, preferred_element_type=jnp.float32)
    retained = retained + jnp.einsum(
        "bnhk,bhkv->bnhv", query_incoming, memory_low, preferred_element_type=jnp.float32
    )
    retained = retained.reshape(row_count, head_count, VAL)
    centred = retained - jnp.mean(retained, axis=-1, keepdims=True)
    group_inverse = lax.rsqrt(jnp.mean(centred * centred, axis=-1, keepdims=True) + 1.0)
    unit_heads = centred * group_inverse
    unit_norm = unit_heads.reshape(row_count, head_count * VAL)
    grouped = unit_norm * groupscale + groupshift
    sigmoid = jax.nn.sigmoid(gate_pre)
    swish_out = gate_pre * sigmoid
    gated_out = (swish_out * grouped).astype(jnp.bfloat16)
    branch = lax.psum(jnp.dot(gated_out, output_full, preferred_element_type=jnp.float32), "head")
    residual = inputs + branch
    shifted = residual - jnp.mean(residual, axis=-1, keepdims=True)
    layer_inverse = lax.rsqrt(jnp.mean(shifted * shifted, axis=-1, keepdims=True) + 1e-05)
    standard = shifted * layer_inverse
    layered = (standard * postscale + postshift).astype(jnp.bfloat16)
    hidden = jnp.dot(layered, expand_full, preferred_element_type=jnp.float32) + hiddenbias
    active = jax.nn.gelu(hidden, approximate=False).astype(jnp.bfloat16)
    expanded = lax.psum(
        jnp.dot(active, reduce_full, preferred_element_type=jnp.float32).astype(jnp.bfloat16),
        "head",
    ).astype(jnp.float32)
    layer_output = (
        (residual + expanded + outputbias)
        .astype(jnp.bfloat16)
        .reshape(streams, block_size, model_width)
    )
    regathered = (
        lax.all_gather(query_weight, "seq", axis=0, tiled=True),
        lax.all_gather(key_weight, "seq", axis=0, tiled=True),
        lax.all_gather(value_weight, "seq", axis=0, tiled=True),
        lax.all_gather(gate_weight, "seq", axis=0, tiled=True),
        lax.all_gather(output_weight, "seq", axis=1, tiled=True),
        lax.all_gather(expand_weight, "seq", axis=0, tiled=True),
        lax.all_gather(reduce_weight, "seq", axis=1, tiled=True),
    )
    query_full, key_full, value_full, gate_full, output_full, expand_full, reduce_full = regathered
    incoming = cotangent.reshape(row_count, model_width)
    incoming_wide = incoming.astype(jnp.float32)
    outputbias_grad = jnp.sum(incoming_wide, axis=0)
    reduce_grad = contract_rows(active, incoming)
    grad_active = contract_cols(incoming, reduce_full)
    gelu_slope = (
        0.5 * (1.0 + lax.erf(hidden * 0.5**0.5))
        + hidden * jnp.exp(-0.5 * hidden * hidden) * (0.5 / math.pi) ** 0.5
    )
    grad_hidden = (grad_active * gelu_slope).astype(jnp.bfloat16)
    hiddenbias_grad = jnp.sum(grad_hidden.astype(jnp.float32), axis=0)
    expand_grad = contract_rows(layered, grad_hidden)
    grad_layered = lax.psum(contract_cols(grad_hidden, expand_full), "head")
    postscale_grad = jnp.sum(grad_layered * standard, axis=0)
    postshift_grad = jnp.sum(grad_layered, axis=0)
    grad_residual = incoming_wide + normalize_back(
        grad_layered * postscale, standard, layer_inverse
    )
    grad_branch = grad_residual.astype(jnp.bfloat16)
    output_grad = contract_rows(gated_out, grad_branch)
    grad_gated = contract_cols(grad_branch, output_full)
    grad_gate = (grad_gated * grouped * sigmoid * (1.0 + gate_pre * (1.0 - sigmoid))).astype(
        jnp.bfloat16
    )
    grad_grouped = grad_gated * swish_out
    groupscale_grad = jnp.sum(grad_grouped * unit_norm, axis=0)
    groupshift_grad = jnp.sum(grad_grouped, axis=0)
    grad_unit = (grad_grouped * groupscale).reshape(row_count, head_count, VAL)
    grad_retained = normalize_back(grad_unit, unit_heads, group_inverse).astype(jnp.bfloat16)
    grad_retained = grad_retained.reshape(streams, block_size, head_count, VAL)
    reach_terms = jnp.einsum(
        "bnhk,bnhv->bhkv", query_incoming, grad_retained, preferred_element_type=jnp.float32
    )
    suffix_keep, memory_grad = entering_2(
        (carried, reach_terms), "seq", chain, (jnp.ones_like(carried), jnp.zeros_like(reach_terms))
    )
    grad_memory = memory_grad.astype(jnp.bfloat16)
    mixing_again = retention_mixing(queries, keys_in, decay_matrix)
    grad_mixing = jnp.einsum(
        "bnhv,bmhv->bhnm", grad_retained, values, preferred_element_type=jnp.float32
    )
    grad_scores = (grad_mixing * decay_matrix).astype(jnp.bfloat16)
    grad_queries = jnp.einsum(
        "bhnm,bmhk->bnhk", grad_scores, keys_in, preferred_element_type=jnp.float32
    )
    grad_queries = grad_queries + entry_weight * jnp.einsum(
        "bnhv,bhkv->bnhk", grad_retained, memory_low, preferred_element_type=jnp.float32
    )
    grad_keys = jnp.einsum(
        "bhnm,bnhk->bmhk", grad_scores, queries, preferred_element_type=jnp.float32
    )
    grad_keys = grad_keys + exit_weight * jnp.einsum(
        "bmhv,bhkv->bmhk", values, grad_memory, preferred_element_type=jnp.float32
    )
    grad_values = jnp.einsum(
        "bhnm,bnhv->bmhv", mixing_again, grad_retained, preferred_element_type=jnp.float32
    )
    grad_values = grad_values + jnp.einsum(
        "bmhk,bhkv->bmhv", key_projected, grad_memory, preferred_element_type=jnp.float32
    )
    grad_query = (
        rotate_back(grad_queries, cosine_table, sine_table)
        .reshape(row_count, head_count * KEY)
        .astype(jnp.bfloat16)
    )
    grad_key = (
        (rotate_back(grad_keys, cosine_table, sine_table) * KEY ** (-0.5))
        .reshape(row_count, head_count * KEY)
        .astype(jnp.bfloat16)
    )
    grad_value = grad_values.reshape(row_count, head_count * VAL).astype(jnp.bfloat16)
    query_grad = contract_rows(normed, grad_query)
    key_grad = contract_rows(normed, grad_key)
    value_grad = contract_rows(normed, grad_value)
    gate_grad = contract_rows(normed, grad_gate)
    back_terms = contract_cols(grad_query, query_full) + contract_cols(grad_key, key_full)
    back_terms = (
        back_terms + contract_cols(grad_value, value_full) + contract_cols(grad_gate, gate_full)
    )
    grad_normed = lax.psum(back_terms.astype(jnp.bfloat16), "head").astype(jnp.float32)
    prescale_grad = jnp.sum(grad_normed * scaled, axis=0)
    grad_scaled = grad_normed * prescale
    input_grad = grad_residual + inverse * (
        grad_scaled - scaled * jnp.mean(grad_scaled * scaled, axis=-1, keepdims=True)
    )
    row_parts = (
        lax.psum_scatter(
            query_grad.astype(jnp.bfloat16), "seq", scatter_dimension=0, tiled=True
        ).astype(jnp.float32),
        lax.psum_scatter(
            key_grad.astype(jnp.bfloat16), "seq", scatter_dimension=0, tiled=True
        ).astype(jnp.float32),
        lax.psum_scatter(
            value_grad.astype(jnp.bfloat16), "seq", scatter_dimension=0, tiled=True
        ).astype(jnp.float32),
        lax.psum_scatter(
            gate_grad.astype(jnp.bfloat16), "seq", scatter_dimension=0, tiled=True
        ).astype(jnp.float32),
        lax.psum_scatter(
            expand_grad.astype(jnp.bfloat16), "seq", scatter_dimension=0, tiled=True
        ).astype(jnp.float32),
    )
    col_parts = (
        lax.psum_scatter(
            output_grad.astype(jnp.bfloat16), "seq", scatter_dimension=1, tiled=True
        ).astype(jnp.float32),
        lax.psum_scatter(
            reduce_grad.astype(jnp.bfloat16), "seq", scatter_dimension=1, tiled=True
        ).astype(jnp.float32),
    )
    summed = (
        lax.psum(row_parts[0].astype(jnp.bfloat16), "batch").astype(jnp.float32),
        lax.psum(row_parts[1].astype(jnp.bfloat16), "batch").astype(jnp.float32),
        lax.psum(row_parts[2].astype(jnp.bfloat16), "batch").astype(jnp.float32),
        lax.psum(row_parts[3].astype(jnp.bfloat16), "batch").astype(jnp.float32),
        lax.psum(row_parts[4].astype(jnp.bfloat16), "batch").astype(jnp.float32),
        lax.psum(col_parts[0].astype(jnp.bfloat16), "batch").astype(jnp.float32),
        lax.psum(col_parts[1].astype(jnp.bfloat16), "batch").astype(jnp.float32),
    )
    small_sums = lax.psum(
        (
            prescale_grad,
            groupscale_grad,
            groupshift_grad,
            postscale_grad,
            postshift_grad,
            hiddenbias_grad,
            outputbias_grad,
        ),
        ("seq", "batch"),
    )
    return (
        layer_output,
        input_grad.reshape(streams, block_size, model_width),
        small_sums[0],
        summed[0],
        summed[1],
        summed[2],
        summed[3],
        small_sums[1],
        small_sums[2],
        summed[5],
        small_sums[3],
        small_sums[4],
        summed[4],
        small_sums[5],
        summed[6],
        small_sums[6],
    )


def solution(mesh):
    in_specs = (
        P("batch", "seq", None),
        P(),
        P("seq", "head"),
        P("seq", "head"),
        P("seq", "head"),
        P("seq", "head"),
        P("head"),
        P("head"),
        P("head", "seq"),
        P(),
        P(),
        P("seq", "head"),
        P("head"),
        P("head", "seq"),
        P(),
        P("batch", "seq", None),
        P("batch", None),
        P("batch", "seq"),
    )
    out_specs = (
        P("batch", "seq", None),
        P("batch", "seq", None),
        P(),
        P("seq", "head"),
        P("seq", "head"),
        P("seq", "head"),
        P("seq", "head"),
        P("head"),
        P("head"),
        P("head", "seq"),
        P(),
        P(),
        P("seq", "head"),
        P("head"),
        P("head", "seq"),
        P(),
    )
    return jax.shard_map(body, mesh=mesh, in_specs=in_specs, out_specs=out_specs, check_vma=False)
```

profile of v0, /device:TPU:0, one launch (start us, length us, event | category | flops | bytes accessed | tf_op | source)
XLA Modules:
  0.0 2511.2 jit_solution(712260957237997530)
XLA Ops:
  10.1 5.4 collective-permute-start
  18.8 74.3 %all-gather.16.cloned.1.call-done = bf16[2048,1024]{1,0:T(8,128)(2,1)} async-done(((bf16[512,1024]{1,0:T(8,128)(2,1)}), bf16[2048,1024]{1,0:T(8,128)(2,1)}) %all-gather.16.cloned.1.call-update) | async-done | bytes 4194320 | tf_op jit(solution)/shard_map/all_gather | solution.py:169
  93.1 6.4 copy.107
  99.5 74.5 %all-gather.18.cloned.1.call-done = bf16[2048,1024]{1,0:T(8,128)(2,1)} async-done(((bf16[512,1024]{1,0:T(8,128)(2,1)}), bf16[2048,1024]{1,0:T(8,128)(2,1)}) %all-gather.18.cloned.1.call-update) | async-done | bytes 4194320 | tf_op jit(solution)/shard_map/all_gather | solution.py:170
  174.0 6.4 copy.108
  180.4 5.3 fusion.61
  190.3 133.5 %all-gather.14.cloned.1.call-done = bf16[2048,2048]{1,0:T(8,128)(2,1)} async-done(((bf16[512,2048]{1,0:T(8,128)(2,1)}), bf16[2048,2048]{1,0:T(8,128)(2,1)}) %all-gather.14.cloned.1.call-update) | async-done | bytes 8388624 | tf_op jit(solution)/shard_map/all_gather | solution.py:171
  323.8 8.2 convolution_convert_fusion.8
  338.2 8.0 all_gather.52
  352.5 130.9 %all-gather.26.cloned.1.call-done = f32[16,256,512]{2,1,0:T(8,128)} async-done(((f32[4,256,512]{2,1,0:T(8,128)}), f32[16,256,512]{2,1,0:T(8,128)}) %all-gather.26.cloned.1.call-update) | async-done | bytes 8388624 | tf_op jit(solution)/shard_map/all_gather | solution.py:21
  491.5 5.7 copy.141
  497.2 5.3 copy.139
  505.1 5.4 copy.140
  510.4 122.3 %all-gather.12.cloned.1.call-done = bf16[2048,2048]{1,0:T(8,128)(2,1)} async-done(((bf16[512,2048]{1,0:T(8,128)(2,1)}), bf16[2048,2048]{1,0:T(8,128)(2,1)}) %all-gather.12.cloned.1.call-update) | async-done | bytes 8388624 | tf_op jit(solution)/shard_map/all_gather | solution.py:172
  632.8 17.5 multiply_convert_fusion.2
  650.3 131.8 %all-gather.20.cloned.1.call-done = bf16[2048,2048]{1,0:T(8,128)(2,1)} async-done(((bf16[2048,512]{1,0:T(8,128)(2,1)}), bf16[2048,2048]{1,0:T(8,128)(2,1)}) %all-gather.20.cloned.1.call-update) | async-done | bytes 8388624 | tf_op jit(solution)/shard_map/all_gather | solution.py:173
  782.1 10.5 fusion.104
  794.2 25.2 %all-reduce.8.cloned.1.call-done = f32[512,2048]{1,0:T(8,128)} async-done(((f32[512,2048]{1,0:T(8,128)}), f32[512,2048]{1,0:T(8,128)}) %all-reduce.8.cloned.1.call-update) | async-done | bytes 4194320 | tf_op jit(solution)/shard_map/psum | solution.py:232
  825.3 146.6 %all-gather.22.cloned.1.call-done = bf16[2048,2048]{1,0:T(8,128)(2,1)} async-done(((bf16[512,2048]{1,0:T(8,128)(2,1)}), bf16[2048,2048]{1,0:T(8,128)(2,1)}) %all-gather.22.cloned.1.call-update) | async-done | bytes 8388624 | tf_op jit(solution)/shard_map/all_gather | solution.py:174
  971.9 27.6 %fusion.19 = (bf16[512,2048]{1,0:T(8,128)(2,1)}, f32[512,2048]{1,0:T(8,128)}) fusion(f32[2048]{0:T(1024)S(1)} %copy-done.66, bf16[2048,2048]{1,0:T(8,128)(2,1)} %all-gather.22.cloned.1.call-done, f32[512,2048]{1,0:T(8,128)} %copy-done, f32[2048]{0:T(1024)S(1)} %copy-done.68, f32[2048]{0:T(1024)S(1)} %copy-done.52, f32[512]{0:T(512)S(1)} %add_rsqrt_fusion.1, ...), kind=kOutput, calls=%fused_computation.35 | convolution fusion | flops 4369416192 | bytes 18903040 | tf_op jit(solution)/shard_map/dot_general | solution.py:238
  999.5 122.0 %all-gather.24.cloned.1.call-done = bf16[2048,2048]{1,0:T(8,128)(2,1)} async-done(((bf16[2048,512]{1,0:T(8,128)(2,1)}), bf16[2048,2048]{1,0:T(8,128)(2,1)}) %all-gather.24.cloned.1.call-update) | async-done | bytes 8388624 | tf_op jit(solution)/shard_map/all_gather | solution.py:175
  1121.4 10.2 convert_reduce_fusion.1
  1133.0 6.1 fusion.105
  1139.2 26.7 %all-reduce.10.cloned.1.call-done = f32[512,2048]{1,0:T(8,128)} async-done(((f32[512,2048]{1,0:T(8,128)}), f32[512,2048]{1,0:T(8,128)}) %all-reduce.10.cloned.1.call-update) | async-done | bytes 4194320 | tf_op jit(solution)/shard_map/psum | solution.py:271
  1165.9 5.6 multiply_reduce_fusion
  1176.1 12.7 fusion.99
  1191.3 5.3 copy.142
  1196.6 6.0 reshape.835
  1240.0 9.4 convolution_convert_fusion.1
  1251.1 8.4 convolution_convert_fusion
  1260.1 11.5 all_gather.58
  1274.9 30.4 %all-gather.28.cloned.1.call-done = bf16[16,256,512]{2,1,0:T(8,128)(2,1)} async-done(((bf16[4,256,512]{2,1,0:T(8,128)(2,1)}), bf16[16,256,512]{2,1,0:T(8,128)(2,1)}) %all-gather.28.cloned.1.call-update) | async-done | bytes 4194320 | tf_op jit(solution)/shard_map/all_gather | solution.py:37
  1305.5 6.0 while.27
  1321.9 10.2 convolution_convert_fusion.3
  1332.4 10.7 convolution_convert_fusion.2
  1348.8 7.3 convolution_convert_fusion.4
  1357.7 9.2 convolution_convert_fusion.7
  1376.1 6.1 fusion.110
  1382.2 10.9 add_convert_fusion
  1393.4 137.3 %reduce-scatter.18.cloned.1.call-done = bf16[512,2048]{1,0:T(8,128)(2,1)} async-done(((bf16[2048,2048]{1,0:T(8,128)(2,1)}), bf16[512,2048]{1,0:T(8,128)(2,1)}) %reduce-scatter.18.cloned.1.call-update) | async-done | bytes 2097168 | tf_op jit(solution)/shard_map/reduce_scatter | solution.py:357
  1530.8 147.6 %reduce-scatter.20.cloned.1.call-done = bf16[2048,512]{1,0:T(8,128)(2,1)} async-done(((bf16[2048,2048]{1,0:T(8,128)(2,1)}), bf16[2048,512]{1,0:T(8,128)(2,1)}) %reduce-scatter.20.cloned.1.call-update) | async-done | bytes 2097168 | tf_op jit(solution)/shard_map/reduce_scatter | solution.py:365
  1678.3 79.8 %reduce-scatter.10.cloned.1.call-done = bf16[512,1024]{1,0:T(8,128)(2,1)} async-done(((bf16[2048,1024]{1,0:T(8,128)(2,1)}), bf16[512,1024]{1,0:T(8,128)(2,1)}) %reduce-scatter.10.cloned.1.call-update) | async-done | bytes 1048592 | tf_op jit(solution)/shard_map/reduce_scatter | solution.py:348
  1758.1 147.2 %reduce-scatter.14.cloned.1.call-done = bf16[512,2048]{1,0:T(8,128)(2,1)} async-done(((bf16[2048,2048]{1,0:T(8,128)(2,1)}), bf16[512,2048]{1,0:T(8,128)(2,1)}) %reduce-scatter.14.cloned.1.call-update) | async-done | bytes 2097168 | tf_op jit(solution)/shard_map/reduce_scatter | solution.py:354
  1905.3 147.4 %reduce-scatter.16.cloned.1.call-done = bf16[2048,512]{1,0:T(8,128)(2,1)} async-done(((bf16[2048,2048]{1,0:T(8,128)(2,1)}), bf16[2048,512]{1,0:T(8,128)(2,1)}) %reduce-scatter.16.cloned.1.call-update) | async-done | bytes 2097168 | tf_op jit(solution)/shard_map/reduce_scatter | solution.py:362
  2052.7 147.4 %reduce-scatter.12.cloned.1.call-done = bf16[512,2048]{1,0:T(8,128)(2,1)} async-done(((bf16[2048,2048]{1,0:T(8,128)(2,1)}), bf16[512,2048]{1,0:T(8,128)(2,1)}) %reduce-scatter.12.cloned.1.call-update) | async-done | bytes 2097168 | tf_op jit(solution)/shard_map/reduce_scatter | solution.py:351
  2200.3 32.3 %all-reduce.14.cloned.1.call-done = (bf16[512,2048]{1,0:T(8,128)(2,1)}, bf16[512,2048]{1,0:T(8,128)(2,1)}) async-done(((bf16[512,2048]{1,0:T(8,128)(2,1)}, bf16[512,2048]{1,0:T(8,128)(2,1)}), (bf16[512,2048]{1,0:T(8,128)(2,1)}, bf16[512,2048]{1,0:T(8,128)(2,1)})) %all-reduce.14.cloned.1.call-update) | async-done | bytes 4194320 | tf_op jit(solution)/shard_map/psum | solution.py:240
  2235.6 79.2 %all-reduce = (f32[2048]{0:T(1024)}, f32[2048]{0:T(1024)}, f32[2048]{0:T(1024)}, f32[2048]{0:T(1024)}, f32[2048]{0:T(1024)}, /*index=5*/f32[2048]{0:T(1024)}, f32[2048]{0:T(1024)}) all-reduce(f32[2048]{0:T(1024)S(1)} %get-tuple-element.189, f32[2048]{0:T(1024)S(1)} %copy-done.60, ...), channel_id=1, replica_groups=mesh['seq'=4,'batch'=4,'head'=2] {'seq','batch'}, use_global_device_ids=true, to_apply=%region_21.22 | all-reduce | flops 14336 | bytes 114688 | tf_op jit(solution)/shard_map/psum | solution.py:378
  2323.2 161.8 %all-reduce.12.cloned.1.call-done = (bf16[512,1024]{1,0:T(8,128)(2,1)}, bf16[512,1024]{1,0:T(8,128)(2,1)}, bf16[512,2048]{1,0:T(8,128)(2,1)}, bf16[512,2048]{1,0...) async-done(((bf16[512,1024]{1,0:T(8,128)(2,1)}, bf16[512,1024]{1,0:T(8,128)(2,1)}, bf16[512,2048]{1,0:T(8,128)(2,1)}, ...) | async-done | bytes 12582928 | tf_op jit(solution)/shard_map/psum | solution.py:370
  (277 shorter events, 154.2 us)
Async XLA Ops:
  7.2 85.9 %all-gather.16.cloned.1.call-start = ((), (), s32[]{:S(2)}) async-start(), calls=%async_computation.9 | async-start | bytes 5242880 | tf_op jit(solution)/shard_map/all_gather | solution.py:169
  7.9 166.1 %all-gather.18.cloned.1.call-start = ((), (), s32[]{:S(2)}) async-start(), calls=%async_computation.10 | async-start | bytes 5242880 | tf_op jit(solution)/shard_map/all_gather | solution.py:170
  8.7 315.1 %all-gather.14.cloned.1.call-start = ((), (), s32[]{:S(2)}) async-start(), calls=%async_computation.8 | async-start | bytes 10485760 | tf_op jit(solution)/shard_map/all_gather | solution.py:171
  9.4 474.0 %all-gather.26.cloned.1.call-start = ((), (), s32[]{:S(2)}) async-start(), calls=%async_computation.23 | async-start | bytes 10485760 | tf_op jit(solution)/shard_map/all_gather | solution.py:21
  10.1 7.3 collective-permute-start
  15.7 330.6 %copy-start.63 = (f32[4]{0:T(128)}, f32[4]{0:T(128)S(1)}, u32[]{:S(2)}) copy-start(f32[4]{0:T(128)S(1)} %negate_log-plus-one_fusion) | copy-start | bytes 52
  17.3 171.0 %copy-start.25 = (f32[512,128]{0,1:T(8,128)}, f32[512,128]{0,1:T(8,128)S(1)}, u32[]{:S(2)}) copy-start(f32[512,128]{0,1:T(8,128)S(1)} %get-tuple-element.250) | copy-start | bytes 786436
  17.3 171.0 %copy-start.27 = (f32[512,128]{0,1:T(8,128)}, f32[512,128]{0,1:T(8,128)S(1)}, u32[]{:S(2)}) copy-start(f32[512,128]{0,1:T(8,128)S(1)} %get-tuple-element.251) | copy-start | bytes 786436
  18.8 313.3 %copy-start.48 = (f32[512,4]{0,1:T(4,128)}, f32[512,4]{0,1:T(4,128)S(1)}, u32[]{:S(2)}) copy-start(f32[512,4]{0,1:T(4,128)S(1)} %get-tuple-element.254) | copy-start | bytes 24580
  190.3 156.0 %copy-start.14 = (bf16[512,4,256]{0,2,1:T(8,128)(2,1)}, bf16[512,4,256]{0,2,1:T(8,128)(2,1)S(1)}, u32[]{:S(2)}) copy-start(bf16[512,4,256]{0,2,1:T(8,128)(2,1)S(1)} %fusion.48) | copy-start | bytes 3145732
  335.4 10.9 copy-start.21
  335.4 10.9 copy-start.23
  335.4 297.3 %all-gather.12.cloned.1.call-start = ((), (), s32[]{:S(2)}) async-start(), calls=%async_computation.7 | async-start | bytes 10485760 | tf_op jit(solution)/shard_map/all_gather | solution.py:172
  336.0 446.1 %all-gather.20.cloned.1.call-start = ((), (), s32[]{:S(2)}) async-start(), calls=%async_computation.11 | async-start | bytes 10485760 | tf_op jit(solution)/shard_map/all_gather | solution.py:173
  336.6 482.8 %all-reduce.8.cloned.1.call-start = ((), (), s32[]{:S(2)}) async-start(), calls=%async_computation.12 | async-start | bytes 8388608 | tf_op jit(solution)/shard_map/psum | solution.py:232
  336.8 10.9 copy-start.43
  337.0 9.3 copy-start.46
  505.1 127.7 %copy-start.56 = (f32[2048]{0:T(1024)S(1)}, f32[2048]{0:T(1024)}, u32[]{:S(2)}) copy-start(f32[2048]{0:T(1024)} %param.28) | copy-start | bytes 24580
  505.1 127.7 %copy-start.67 = (f32[2048]{0:T(1024)S(1)}, f32[2048]{0:T(1024)}, u32[]{:S(2)}) copy-start(f32[2048]{0:T(1024)} %param.29) | copy-start | bytes 24580
  792.6 179.2 %all-gather.22.cloned.1.call-start = ((), (), s32[]{:S(2)}) async-start(), calls=%async_computation.13 | async-start | bytes 10485760 | tf_op jit(solution)/shard_map/all_gather | solution.py:174
  793.4 328.0 %all-gather.24.cloned.1.call-start = ((), (), s32[]{:S(2)}) async-start(), calls=%async_computation.14 | async-start | bytes 10485760 | tf_op jit(solution)/shard_map/all_gather | solution.py:175
  794.1 371.7 %all-reduce.10.cloned.1.call-start = ((), (), s32[]{:S(2)}) async-start(), calls=%async_computation.15 | async-start | bytes 8388608 | tf_op jit(solution)/shard_map/psum | solution.py:271
  822.7 149.1 %copy-start.52 = (f32[2048]{0:T(1024)S(1)}, f32[2048]{0:T(1024)}, u32[]{:S(2)}) copy-start(f32[2048]{0:T(1024)} %param.31) | copy-start | bytes 24580
  822.8 149.1 %copy-start.66 = (f32[2048]{0:T(1024)S(1)}, f32[2048]{0:T(1024)}, u32[]{:S(2)}) copy-start(f32[2048]{0:T(1024)} %param.34) | copy-start | bytes 24580
  822.8 149.1 %copy-start.68 = (f32[2048]{0:T(1024)S(1)}, f32[2048]{0:T(1024)}, u32[]{:S(2)}) copy-start(f32[2048]{0:T(1024)} %param.32) | copy-start | bytes 24580
  1121.4 11.6 copy-start.65
  1139.1 166.1 %all-gather.28.cloned.1.call-start = ((), (), s32[]{:S(2)}) async-start(), calls=%async_computation.24 | async-start | bytes 5242880 | tf_op jit(solution)/shard_map/all_gather | solution.py:37
  1176.1 12.7 copy-start.12
  1223.1 170.3 %reduce-scatter.8.cloned.1.call-start = ((), (), s32[]{:S(2)}) async-start(), calls=%async_computation.16 | async-start | bytes 5242880 | tf_op jit(solution)/shard_map/reduce_scatter | solution.py:345
  1238.5 292.3 %reduce-scatter.18.cloned.1.call-start = ((), (), s32[]{:S(2)}) async-start(), calls=%async_computation.21 | async-start | bytes 10485760 | tf_op jit(solution)/shard_map/reduce_scatter | solution.py:357
  1249.5 428.8 %reduce-scatter.20.cloned.1.call-start = ((), (), s32[]{:S(2)}) async-start(), calls=%async_computation.22 | async-start | bytes 10485760 | tf_op jit(solution)/shard_map/reduce_scatter | solution.py:365
  1259.5 12.1 copy-start.20
  1259.5 498.6 %reduce-scatter.10.cloned.1.call-start = ((), (), s32[]{:S(2)}) async-start(), calls=%async_computation.17 | async-start | bytes 5242880 | tf_op jit(solution)/shard_map/reduce_scatter | solution.py:348
  1321.9 583.4 %reduce-scatter.14.cloned.1.call-start = ((), (), s32[]{:S(2)}) async-start(), calls=%async_computation.19 | async-start | bytes 10485760 | tf_op jit(solution)/shard_map/reduce_scatter | solution.py:354
  1332.1 720.6 %reduce-scatter.16.cloned.1.call-start = ((), (), s32[]{:S(2)}) async-start(), calls=%async_computation.20 | async-start | bytes 10485760 | tf_op jit(solution)/shard_map/reduce_scatter | solution.py:362
  1343.1 857.0 %reduce-scatter.12.cloned.1.call-start = ((), (), s32[]{:S(2)}) async-start(), calls=%async_computation.18 | async-start | bytes 10485760 | tf_op jit(solution)/shard_map/reduce_scatter | solution.py:351
  1356.2 10.8 copy-start.45
  1356.2 876.4 %all-reduce.14.cloned.1.call-start = ((), (), s32[]{:S(2)}) async-start(), calls=%async_computation.26 | async-start | bytes 8388608 | tf_op jit(solution)/shard_map/psum | solution.py:240
  1371.5 10.7 slice-start.2
  1393.1 1092.0 %all-reduce.12.cloned.1.call-start = ((), (), s32[]{:S(2)}) async-start(), calls=%async_computation.25 | async-start | bytes 25165824 | tf_op jit(solution)/shard_map/psum | solution.py:370
  2200.2 32.4 %copy-start.7 = (bf16[1,512,2048]{2,1,0:T(8,128)(2,1)S(1)}, bf16[1,512,2048]{2,1,0:T(8,128)(2,1)}, u32[]{:S(2)}) copy-start(bf16[1,512,2048]{2,1,0:T(8,128)(2,1)} %param.22) | copy-start | bytes 6291460
  2200.2 35.3 %copy-start.51 = (f32[2048]{0:T(1024)S(1)}, f32[2048]{0:T(1024)}, u32[]{:S(2)}) copy-start(f32[2048]{0:T(1024)} %get-tuple-element.246) | copy-start | bytes 24580
  2200.2 35.3 %copy-start.53 = (f32[2048]{0:T(1024)S(1)}, f32[2048]{0:T(1024)}, u32[]{:S(2)}) copy-start(f32[2048]{0:T(1024)} %get-tuple-element.186) | copy-start | bytes 24580
  2200.2 35.3 %copy-start.54 = (f32[2048]{0:T(1024)S(1)}, f32[2048]{0:T(1024)}, u32[]{:S(2)}) copy-start(f32[2048]{0:T(1024)} %get-tuple-element.191) | copy-start | bytes 24580
  2200.2 35.3 %copy-start.58 = (f32[2048]{0:T(1024)S(1)}, f32[2048]{0:T(1024)}, u32[]{:S(2)}) copy-start(f32[2048]{0:T(1024)} %get-tuple-element.261) | copy-start | bytes 24580
  2200.3 35.3 %copy-start.59 = (f32[2048]{0:T(1024)S(1)}, f32[2048]{0:T(1024)}, u32[]{:S(2)}) copy-start(f32[2048]{0:T(1024)} %get-tuple-element.192) | copy-start | bytes 24580
  2200.3 35.3 %copy-start.60 = (f32[2048]{0:T(1024)S(1)}, f32[2048]{0:T(1024)}, u32[]{:S(2)}) copy-start(f32[2048]{0:T(1024)} %get-tuple-element.193) | copy-start | bytes 24580
  2200.3 114.4 %copy-start.57 = (f32[2048]{0:T(1024)S(1)}, f32[2048]{0:T(1024)}, u32[]{:S(2)}) copy-start(f32[2048]{0:T(1024)} %param.36) | copy-start | bytes 24580
  (50 other events, 176.6 us)
Sparse Core Ops, SparseCore 0:
  9.6 83.4 all-gather.15
  94.7 79.2 all-gather.17
  175.6 148.1 all-gather.13
  335.6 147.8 all-gather.25
  484.9 147.8 all-gather.11
  634.2 147.8 all-gather.19
  792.7 26.5 all-reduce.7
  821.0 150.7 all-gather.21
  973.5 147.8 all-gather.23
  1139.2 26.5 all-reduce.9
  1223.2 81.9 all-gather.27
  1308.0 75.2 reduce-scatter.7
  1385.8 144.9 reduce-scatter.17
  1533.1 145.1 reduce-scatter.19
  1680.6 77.4 reduce-scatter.9
  1760.3 144.9 reduce-scatter.13
  1907.5 145.1 reduce-scatter.15
  2055.0 145.1 reduce-scatter.11
  2203.3 29.2 all-reduce.13
  2237.8 247.1 all-reduce.11
where the time goes:
time: 2520 us; the launch traced here: 2510 us
  waiting for transfers between devices  2020 us (80%)
  matrix products  220 us (9%)
  blocking collectives  98.7 us (4%)
  local copies, waits for them, and re-layouts  72.2 us (3%)
  other arithmetic  71.5 us (3%)
    psum x1, waiting for transfers between devices, body(): lax.psum(row_parts[0].astype(jnp.bfloat16), 'batch').astype(jnp.float32)  162 us
    reduce_scatter x1, waiting for transfers between devices, body(): lax.psum_scatter(reduce_grad.astype(jnp.bfloat16), 'seq', scatter_dimensi...  148 us
    reduce_scatter x1, waiting for transfers between devices, body(): lax.psum_scatter(value_grad.astype(jnp.bfloat16), 'seq', scatter_dimensio...  147 us
    reduce_scatter x1, waiting for transfers between devices, body(): lax.psum_scatter(output_grad.astype(jnp.bfloat16), 'seq', scatter_dimensi...  147 us
    reduce_scatter x1, waiting for transfers between devices, body(): lax.psum_scatter(gate_grad.astype(jnp.bfloat16), 'seq', scatter_dimension...  147 us
    all_gather x1, waiting for transfers between devices, body(): lax.all_gather(expand_weight, 'seq', axis=0, tiled=True)  147 us
    reduce_scatter x1, waiting for transfers between devices, body(): lax.psum_scatter(expand_grad.astype(jnp.bfloat16), 'seq', scatter_dimensi...  137 us
    all_gather x1, waiting for transfers between devices, body(): lax.all_gather(value_weight, 'seq', axis=0, tiled=True)  133 us
  transfers between devices with their start and end apart: 21, of which 19 were waited for; matrix products, arithmetic and copies ran while one was open for 9% of the time, Pallas kernels for 0%

commit v1 on v0

v1 whole, which is shorter than its diff:
```python
import math

import jax
import jax.numpy as jnp
from jax import lax
from jax.sharding import PartitionSpec as P

KEY = 256
VAL = 512
F32 = jnp.float32
BF16 = jnp.bfloat16


def swap_core(value):
    return lax.ppermute(value, "head", [(0, 1), (1, 0)])


def swap_batch(value, mask):
    return lax.ppermute(value, "batch", [(place, place ^ mask) for place in range(4)])


def spread(piece):
    middle = piece.shape[0] // 2
    first = swap_batch(piece, 1)
    second = swap_batch(piece, 2)
    upper = swap_batch(first[:middle], 2)
    lower = swap_batch(second[middle:], 1)
    return first, second, jnp.concatenate([upper, lower], axis=0)


def fold(parts):
    middle = parts[3].shape[0] // 2
    far = parts[3].astype(BF16)
    upper = swap_batch(far[:middle], 1)
    lower = swap_batch(far[middle:], 2)
    to_first = jnp.concatenate(
        [parts[1][:middle], parts[1][middle:] + lower.astype(F32)], axis=0
    ).astype(BF16)
    to_second = jnp.concatenate(
        [parts[2][:middle] + upper.astype(F32), parts[2][middle:]], axis=0
    ).astype(BF16)
    first = swap_batch(to_first, 1)
    second = swap_batch(to_second, 2)
    return parts[0] + first.astype(F32) + second.astype(F32)


def total(value):
    for axis in ("batch", "seq"):
        count = lax.axis_size(axis)
        step = 1
        while step < count:
            moved = lax.ppermute(value, axis, [(place, place ^ step) for place in range(count)])
            value = value + moved
            step *= 2
    return value


def hop(value, source, target):
    return lax.ppermute(value, "seq", [(source, target)])


def carry(keep, added, forward):
    count = lax.axis_size("seq")
    entered = []
    for chunk in range(0, 4, 2):
        factor = keep[chunk : chunk + 2, None, None]
        own = added[chunk : chunk + 2]
        state = jnp.zeros(own.shape, BF16)
        for step in range(count - 1):
            sent = (factor * state.astype(F32) + own).astype(BF16)
            source, target = (step, step + 1) if forward else (count - 1 - step, count - 2 - step)
            state = state + hop(sent, source, target)
        entered.append(state)
    return jnp.concatenate(entered, axis=0)


def dot(left, right):
    return jnp.dot(left, right, preferred_element_type=F32)


def contract_rows(left, right):
    return lax.dot_general(left, right, (((0,), (0,)), ((), ())), preferred_element_type=F32)


def contract_cols(left, right):
    return lax.dot_general(left, right, (((1,), (1,)), ((), ())), preferred_element_type=F32)


def normalize_back(grad_unit, unit_norm, inverse):
    mean_grad = jnp.mean(grad_unit, axis=-1, keepdims=True)
    mean_cross = jnp.mean(grad_unit * unit_norm, axis=-1, keepdims=True)
    return inverse * (grad_unit - mean_grad - unit_norm * mean_cross)


def rotate(values, cosine, sine, sign):
    middle = values.shape[-1] // 2
    former, latter = (values[..., :middle], values[..., middle:])
    return jnp.concatenate(
        [former * cosine - sign * latter * sine, latter * cosine + sign * former * sine], axis=-1
    )


def batched(subscripts, left, right):
    return jnp.einsum(subscripts, left, right, preferred_element_type=F32)


def place_columns(pieces, place, width):
    rows = pieces[0].shape[0]
    result = jnp.zeros((rows, 4 * width), F32)
    for slot, piece in enumerate(pieces):
        result = lax.dynamic_update_slice(result, piece.astype(F32), (0, (place ^ slot) * width))
    return result


def place_rows(pieces, place, height):
    result = jnp.zeros((4 * height, pieces[0].shape[1]), F32)
    for slot, piece in enumerate(pieces):
        result = lax.dynamic_update_slice(result, piece.astype(F32), ((place ^ slot) * height, 0))
    return result


def body(
    tokens,
    prescale,
    query_weight,
    key_weight,
    value_weight,
    gate_weight,
    groupscale,
    groupshift,
    output_weight,
    postscale,
    postshift,
    expand_weight,
    hiddenbias,
    reduce_weight,
    outputbias,
    cotangent,
    doc_lengths,
    segments,
):
    _, rows, width = tokens.shape
    half = rows // 2
    part = hiddenbias.shape[0] // 4
    core = lax.axis_index("head")
    place = lax.axis_index("batch")
    block = lax.axis_index("seq")

    def own_rows(value):
        return lax.dynamic_slice_in_dim(value, core * half, half, 0)

    def far_rows(value):
        return lax.dynamic_slice_in_dim(value, (1 - core) * half, half, 0)

    def cols_of(weight, size):
        return lax.dynamic_slice_in_dim(weight, place * size, size, 1)

    def rows_of(weight, size):
        return lax.dynamic_slice_in_dim(weight, place * size, size, 0)

    def gather_rows(weight):
        return lax.all_gather(weight, "seq", axis=0, tiled=True)

    def gather_cols(weight):
        return lax.all_gather(weight, "seq", axis=1, tiled=True)

    def scatter(grad, dimension):
        return lax.psum_scatter(grad.astype(BF16), "seq", scatter_dimension=dimension, tiled=True)

    key_value = gather_rows(
        jnp.concatenate([cols_of(key_weight, KEY), cols_of(value_weight, VAL)], axis=1)
    )
    query_gate = gather_rows(
        jnp.concatenate([cols_of(query_weight, KEY), cols_of(gate_weight, VAL)], axis=1)
    )
    output_own = gather_cols(rows_of(output_weight, VAL))
    expand_own = gather_rows(cols_of(expand_weight, part))
    reduce_own = gather_cols(rows_of(reduce_weight, part))

    tokens_own, tokens_far = own_rows(tokens[0]), far_rows(tokens[0])
    before = jnp.where(block == 0, -1, lax.ppermute(
        segments[0, rows - 1 :],
        "seq",
        [(source, source + 1) for source in range(lax.axis_size("seq") - 1)],
    ))
    marks = jnp.concatenate([segments[0], doc_lengths[0], before])[None]
    marks = jnp.concatenate([marks, swap_batch(marks, 1)], axis=0)
    marks = jnp.concatenate([marks, swap_batch(marks, 2)], axis=0)
    arrived = spread(tokens_own)
    pieces = [tokens_own, tokens_far]
    for piece in arrived:
        pieces += [piece, swap_core(piece)]
    dy = cotangent[0]
    dy_own = own_rows(dy)
    dy_rows = jnp.concatenate((dy_own,) + spread(dy_own), axis=0)

    inputs = jnp.concatenate(pieces, axis=0).astype(F32)
    inverse = lax.rsqrt(jnp.mean(inputs * inputs, axis=-1, keepdims=True) + 1e-06)
    normed = (inputs * inverse * prescale).astype(BF16)

    spans = marks[:, rows:-1]
    before = marks[:, -1]
    natural = marks[:, :rows]
    last = natural[:, rows - 1]
    segment = jnp.where(
        core == 0, natural, jnp.concatenate([natural[:, half:], natural[:, :half]], axis=1)
    )
    steps = jnp.arange(half, dtype=jnp.int32)
    index = jnp.concatenate([core * half + steps, (1 - core) * half + steps])
    stream_index = block * rows + index
    ends = jnp.cumsum(spans, axis=1)
    starts = jnp.sum(
        jnp.where(ends[:, None, :] <= stream_index[None, :, None], spans[:, None, :], 0), axis=2
    )
    positions = (stream_index[None, :] - starts).astype(F32)
    middle = KEY // 2
    frequency = jnp.exp(-math.log(10000.0) * jnp.arange(middle, dtype=F32) / (middle - 1))
    phases = positions[..., None] * frequency
    cosine, sine = jnp.cos(phases), jnp.sin(phases)
    head = (core * 4 + place).astype(F32)
    log_rate = jnp.log1p(-jnp.exp2(-5.0 - head))
    distance = index[:, None] - index[None, :]
    causal = distance >= 0
    decays = jnp.exp(jnp.where(causal, distance, 0).astype(F32) * log_rate)
    linked = (segment[:, :, None] == segment[:, None, :]) & causal[None]
    decay_matrix = jnp.where(linked, decays[None], 0.0)
    entry = jnp.exp((index + 1).astype(F32) * log_rate)[None] * (
        segment == before[:, None]
    ).astype(F32)
    exit_weight = jnp.exp((rows - 1 - index).astype(F32) * log_rate)[None] * (
        segment == last[:, None]
    ).astype(F32)
    entry, exit_weight = entry[..., None], exit_weight[..., None]
    keep = jnp.exp(rows * log_rate) * (last == before).astype(F32)

    key_value_pre = dot(normed, key_value)
    keys_in = (
        rotate(key_value_pre[:, :KEY].reshape(4, rows, KEY), cosine, sine, 1.0) * KEY ** (-0.5)
    ).astype(BF16)
    values = key_value_pre[:, KEY:].astype(BF16).reshape(4, rows, VAL)
    key_out = (keys_in.astype(F32) * exit_weight).astype(BF16)
    memory = carry(keep, batched("bmk,bmv->bkv", key_out, values), True)
    query_gate_pre = dot(normed, query_gate)
    queries = rotate(
        query_gate_pre[:, :KEY].reshape(4, rows, KEY), cosine, sine, 1.0
    ).astype(BF16)
    gate_pre = query_gate_pre[:, KEY:]
    query_in = (queries.astype(F32) * entry).astype(BF16)
    mixing = (batched("bnk,bmk->bnm", queries, keys_in) * decay_matrix).astype(BF16)
    retained = batched("bnm,bmv->bnv", mixing, values) + batched(
        "bnk,bkv->bnv", query_in, memory
    )
    retained = retained.reshape(4 * rows, VAL)
    centred = retained - jnp.mean(retained, axis=-1, keepdims=True)
    group_inverse = lax.rsqrt(jnp.mean(centred * centred, axis=-1, keepdims=True) + 1.0)
    unit_norm = centred * group_inverse
    scale_own = lax.dynamic_slice_in_dim(groupscale, place * VAL, VAL, 0)
    shift_own = lax.dynamic_slice_in_dim(groupshift, place * VAL, VAL, 0)
    grouped = unit_norm * scale_own + shift_own
    sigmoid = jax.nn.sigmoid(gate_pre)
    swish = gate_pre * sigmoid
    gated = (swish * grouped).astype(BF16).reshape(4, 2, half, VAL)
    gated_far = swap_core(gated[:, 1])
    gated_both = jnp.concatenate([gated[:, 0], gated_far], axis=-1).reshape(4 * half, 2 * VAL)

    output_both = jnp.concatenate([output_own, swap_core(output_own)], axis=0)
    expand_both = jnp.concatenate([expand_own, swap_core(expand_own)], axis=1)
    reduce_both = jnp.concatenate([reduce_own, swap_core(reduce_own)], axis=0)
    bias_own = lax.dynamic_slice_in_dim(hiddenbias, place * part, part, 0)
    bias_both = jnp.concatenate([bias_own, swap_core(bias_own)], axis=0)

    def slots(value):
        return value.reshape(4, half, value.shape[-1])

    branch = fold(slots(dot(gated_both, output_both)))
    residual = tokens_own.astype(F32) + branch
    shifted = residual - jnp.mean(residual, axis=-1, keepdims=True)
    layer_inverse = lax.rsqrt(jnp.mean(shifted * shifted, axis=-1, keepdims=True) + 1e-05)
    standard = shifted * layer_inverse
    layered_own = (standard * postscale + postshift).astype(BF16)
    layered = jnp.concatenate((layered_own,) + spread(layered_own), axis=0)

    hidden = dot(layered, expand_both) + bias_both
    cumulative = 0.5 * (1.0 + lax.erf(hidden * 0.5**0.5))
    active = (hidden * cumulative).astype(BF16)
    expanded = fold(slots(dot(active, reduce_both)))
    output_rows = (residual + expanded + outputbias).astype(BF16)
    output_far = swap_core(output_rows)
    layer_output = jnp.where(
        core == 0,
        jnp.concatenate([output_rows, output_far], axis=0),
        jnp.concatenate([output_far, output_rows], axis=0),
    )

    def core_sum(grad, dimension):
        size = grad.shape[dimension] // 2
        own = lax.slice_in_dim(grad, 0, size, axis=dimension)
        far = lax.slice_in_dim(grad, size, 2 * size, axis=dimension)
        return own + swap_core(far.astype(BF16)).astype(F32)

    dy_wide = dy_own.astype(F32)
    outputbias_grad = jnp.sum(dy_wide, axis=0)
    reduce_grad = scatter(core_sum(contract_rows(active, dy_rows), 0), 1)
    grad_active = contract_cols(dy_rows, reduce_both)
    slope = cumulative + hidden * jnp.exp(-0.5 * hidden * hidden) * (0.5 / math.pi) ** 0.5
    grad_hidden = (grad_active * slope).astype(BF16)
    hiddenbias_grad = jnp.sum(grad_hidden.astype(F32), axis=0)
    grad_layered = fold(slots(contract_cols(grad_hidden, expand_both)))
    expand_grad = scatter(core_sum(contract_rows(layered, grad_hidden), 1), 0)
    postscale_grad = jnp.sum(grad_layered * standard, axis=0)
    postshift_grad = jnp.sum(grad_layered, axis=0)
    grad_residual = dy_wide + normalize_back(grad_layered * postscale, standard, layer_inverse)
    grad_branch_own = grad_residual.astype(BF16)
    grad_branch = jnp.concatenate((grad_branch_own,) + spread(grad_branch_own), axis=0)

    grad_gated_both = contract_cols(grad_branch, output_both).astype(BF16).reshape(4, half, 2 * VAL)
    grad_gated_far = swap_core(grad_gated_both[..., VAL:])
    grad_gated = (
        jnp.stack([grad_gated_both[..., :VAL], grad_gated_far], axis=1)
        .reshape(4 * rows, VAL)
        .astype(F32)
    )
    output_grad = scatter(core_sum(contract_rows(gated_both, grad_branch), 0), 1)
    grad_gate = (grad_gated * grouped * sigmoid * (1.0 + gate_pre * (1.0 - sigmoid))).astype(BF16)
    grad_grouped = grad_gated * swish
    groupscale_grad = jnp.sum(grad_grouped * unit_norm, axis=0)
    groupshift_grad = jnp.sum(grad_grouped, axis=0)
    grad_retained = normalize_back(grad_grouped * scale_own, unit_norm, group_inverse)
    grad_retained = grad_retained.astype(BF16).reshape(4, rows, VAL)
    grad_memory = carry(keep, batched("bnk,bnv->bkv", query_in, grad_retained), False)
    grad_scores = (batched("bnv,bmv->bnm", grad_retained, values) * decay_matrix).astype(BF16)
    grad_queries = batched("bnm,bmk->bnk", grad_scores, keys_in) + entry * batched(
        "bnv,bkv->bnk", grad_retained, memory
    )
    grad_query = rotate(grad_queries, cosine, sine, -1.0).astype(BF16).reshape(4 * rows, KEY)
    grad_query_gate = jnp.concatenate([grad_query, grad_gate], axis=1)
    query_gate_grad = scatter(contract_rows(normed, grad_query_gate), 0)
    grad_keys = batched("bnm,bnk->bmk", grad_scores, queries) + exit_weight * batched(
        "bmv,bkv->bmk", values, grad_memory
    )
    grad_values = batched("bnm,bnv->bmv", mixing, grad_retained) + batched(
        "bmk,bkv->bmv", key_out, grad_memory
    )
    grad_key = (rotate(grad_keys, cosine, sine, -1.0) * KEY ** (-0.5)).astype(BF16)
    grad_key_value = jnp.concatenate([grad_key, grad_values.astype(BF16)], axis=-1).reshape(
        4 * rows, KEY + VAL
    )
    key_value_grad = scatter(contract_rows(normed, grad_key_value), 0)
    grad_normed = contract_cols(grad_key_value, key_value) + contract_cols(
        grad_query_gate, query_gate
    )
    grad_normed = grad_normed.reshape(4, 2, half, width)
    grad_normed = fold(
        grad_normed[:, 0] + swap_core(grad_normed[:, 1].astype(BF16)).astype(F32)
    )
    inverse_own = inverse[:half]
    scaled = tokens_own.astype(F32) * inverse_own
    prescale_grad = jnp.sum(grad_normed * scaled, axis=0)
    grad_scaled = grad_normed * prescale
    grad_rows = grad_residual + inverse_own * (
        grad_scaled - scaled * jnp.mean(grad_scaled * scaled, axis=-1, keepdims=True)
    )
    grad_far = swap_core(grad_rows)
    tokens_grad = jnp.where(
        core == 0,
        jnp.concatenate([grad_rows, grad_far], axis=0),
        jnp.concatenate([grad_far, grad_rows], axis=0),
    )

    over_cores = jnp.concatenate(
        [hiddenbias_grad[part:], postscale_grad, postshift_grad, outputbias_grad]
    )
    over_cores = swap_core(over_cores) + jnp.concatenate(
        [hiddenbias_grad[:part], postscale_grad, postshift_grad, outputbias_grad]
    )
    columns = [
        lax.dynamic_update_slice(jnp.zeros((4 * part,), F32), piece, (place * part,))
        for piece in (over_cores[:part], groupscale_grad, groupshift_grad)
    ]
    sums = total(jnp.concatenate([over_cores[part:]] + columns))
    cuts = [width, 2 * width, 3 * width, 3 * width + 4 * part, 3 * width + 8 * part]
    postscale_sum, postshift_sum, outputbias_sum, hiddenbias_sum, scale_sum, shift_sum = jnp.split(
        sums, cuts
    )
    prescale_sum = total(prescale_grad + swap_core(prescale_grad))

    def all_pieces(grad):
        return (grad,) + spread(grad)

    reduce_pieces = all_pieces(reduce_grad)
    expand_pieces = all_pieces(expand_grad)
    output_pieces = all_pieces(output_grad)
    query_gate_pieces = all_pieces(query_gate_grad)
    key_value_pieces = all_pieces(key_value_grad)
    return (
        layer_output[None],
        tokens_grad[None],
        prescale_sum,
        place_columns([piece[:, :KEY] for piece in query_gate_pieces], place, KEY),
        place_columns([piece[:, :KEY] for piece in key_value_pieces], place, KEY),
        place_columns([piece[:, KEY:] for piece in key_value_pieces], place, VAL),
        place_columns([piece[:, KEY:] for piece in query_gate_pieces], place, VAL),
        scale_sum,
        shift_sum,
        place_rows(output_pieces, place, VAL),
        postscale_sum,
        postshift_sum,
        place_columns(expand_pieces, place, part),
        hiddenbias_sum,
        place_rows(reduce_pieces, place, part),
        outputbias_sum,
    )


def solution(mesh):
    in_specs = (
        P("batch", "seq", None),
        P(),
        P("seq", "head"),
        P("seq", "head"),
        P("seq", "head"),
        P("seq", "head"),
        P("head"),
        P("head"),
        P("head", "seq"),
        P(),
        P(),
        P("seq", "head"),
        P("head"),
        P("head", "seq"),
        P(),
        P("batch", "seq", None),
        P("batch", None),
        P("batch", "seq"),
    )
    out_specs = (
        P("batch", "seq", None),
        P("batch", "seq", None),
        P(),
        P("seq", "head"),
        P("seq", "head"),
        P("seq", "head"),
        P("seq", "head"),
        P("head"),
        P("head"),
        P("head", "seq"),
        P(),
        P(),
        P("seq", "head"),
        P("head"),
        P("head", "seq"),
        P(),
    )
    return jax.shard_map(body, mesh=mesh, in_specs=in_specs, out_specs=out_specs, check_vma=False)
```

time: 2520 us -> 961 us (0.38)
  waiting for transfers between devices: 2020 us -> 488 us
  blocking collectives: 98.7 us -> 0 us
  starting transfers between devices: 7.4 us -> 93.2 us
  matrix products: 220 us -> 153 us
  other arithmetic: 71.5 us -> 119 us
    all_gather x9 -> x5, waiting for transfers between devices: 966 us -> 63.4 us  [the longest x3 55.3 us: gather_rows(): return lax.all_gather(weight, 'seq', axis=0, tiled=True)]
    reduce_scatter x7 -> x5, waiting for transfers between devices: 807 us -> 0.01 us  [scatter(): lax.psum_scatter(grad.astype(BF16), 'seq', scatter_dimension=dimension, t...]
    ppermute x1 -> x92, waiting for transfers between devices: 0.01 us -> 424 us  [the longest x54 250 us: swap_batch(): lax.ppermute(value, 'batch', [(place, place ^ mask) for place in range(4)])]
    psum x4 -> x0, waiting for transfers between devices: 246 us -> none  [the longest x1 162 us: body(): lax.psum(row_parts[0].astype(jnp.bfloat16), 'batch').astype(jnp.float32)]
    ppermute x1 -> x92, starting transfers between devices: 5.43 us -> 92.1 us  [the longest x54 64.3 us: swap_batch(): lax.ppermute(value, 'batch', [(place, place ^ mask) for place in range(4)])]
    psum x1 -> x0, blocking collectives: 79.2 us -> none  [body(): lax.psum((prescale_grad, groupscale_grad, groupshift_grad, postscale_grad...]
    dot_general x33 -> x27, matrix products: 220 us -> 153 us  [the longest x5 47.6 us: contract_cols(): lax.dot_general(left, right, (((1,), (1,)), ((), ())), preferred_element_...]
  transfers between devices with their start and end apart: 21 -> 102, of which waited for: 19 -> 44; matrix products, arithmetic and copies ran while one was open for 9% -> 34% of each run, Pallas kernels for 0% -> 0%
where the time goes in v1:
time: 961 us; the launch traced here: 951 us
  waiting for transfers between devices  488 us (51%)
  matrix products  153 us (16%)
  other arithmetic  119 us (12%)
  starting transfers between devices  93.2 us (10%)
  local copies, waits for them, and re-layouts  80.1 us (8%)
  between operations  17.7 us (2%)
    ppermute x54, waiting for transfers between devices, swap_batch(): lax.ppermute(value, 'batch', [(place, place ^ mask) for place in range(4)])  250 us
    ppermute x12, waiting for transfers between devices, hop(): return lax.ppermute(value, 'seq', [(source, target)])  151 us
    ppermute x54, starting transfers between devices, swap_batch(): lax.ppermute(value, 'batch', [(place, place ^ mask) for place in range(4)])  64.3 us
    all_gather x3, waiting for transfers between devices, gather_rows(): return lax.all_gather(weight, 'seq', axis=0, tiled=True)  55.3 us
    dot_general x5, matrix products, contract_cols(): lax.dot_general(left, right, (((1,), (1,)), ((), ())), preferred_element_...  47.6 us
    dot_general x5, matrix products, contract_rows(): lax.dot_general(left, right, (((0,), (0,)), ((), ())), preferred_element_...  44 us
    dot_general x5, matrix products, dot(): return jnp.dot(left, right, preferred_element_type=F32)  38.2 us
    unnamed x209, local copies, waits for them, and re-layouts  28.4 us
  transfers between devices with their start and end apart: 102, of which 44 were waited for; matrix products, arithmetic and copies ran while one was open for 34% of the time, Pallas kernels for 0%

profile of v1, /device:TPU:0, one launch (start us, length us, event | category | flops | bytes accessed | tf_op | source)
XLA Modules:
  0.0 950.8 jit_solution(8929182246106529150)
XLA Ops:
  31.2 11.3 %collective-permute-done.8 = s32[1,521]{1,0:T(1,128)S(1)} collective-permute-done((s32[1,521]{1,0:T(1,128)S(1)}, s32[1,521]{1,0:T(1,128)S(1)}, u32[]{:S(2)}, u32[]{:S(2)}) %collective-permute-start.8) | collective-permute-done | bytes 2116 | tf_op jit(solution)/shard_map/ppermute | solution.py:19
  51.5 9.8 %collective-permute-done.4 = bf16[128,2048]{1,0:T(8,128)(2,1)S(1)} collective-permute-done((bf16[128,2048]{1,0:T(8,128)(2,1)S(1)}, bf16[128,2048]{1,0:T(8,128)(2,1)S(1)}, u32[]{:S(2)}, u32[]{:S(2)}) %collective-permute-start.4) | collective-permute-done | bytes 524320 | tf_op jit(solution)/shard_map/ppermute | solution.py:19
  69.2 5.1 fusion
  77.1 11.8 %fusion.98 = f32[2048,768]{1,0:T(8,128)} fusion(bf16[2048,768]{1,0:T(8,128)(2,1)} %all-gather.8.cloned.1.call-done, bf16[2048,2048]{1,0:T(8,128)(2,1)} %constant_dynamic-update-slice_fusion, f32[2048]{0:T(1024)S(1)} %copy-done.71, f32[2048]{0:T(1024)S(1)} %add_rsqrt_fusion), kind=kOutput, calls=%fused_computation.311 | convolution fusion | flops 6459228160 | bytes 17842176 | tf_op jit(solution)/shard_map/dot_general | solution.py:78
  88.9 52.5 %all-gather.6.cloned.1.call-done = bf16[2048,768]{1,0:T(8,128)(2,1)} async-done(((bf16[512,768]{1,0:T(8,128)(2,1)}), bf16[2048,768]{1,0:T(8,128)(2,1)}) %all-gather.6.cloned.1.call-update) | async-done | bytes 3145744 | tf_op jit(solution)/shard_map/all_gather | solution.py:162
  141.4 10.3 %fusion.100 = f32[2048,768]{1,0:T(8,128)S(1)} fusion(bf16[2048,768]{1,0:T(8,128)(2,1)} %all-gather.6.cloned.1.call-done, bf16[2048,2048]{1,0:T(8,128)(2,1)} %constant_dynamic-update-slice_fusion, f32[2048]{0:T(1024)S(1)} %copy-done.71, f32[2048]{0:T(1024)S(1)} %add_rsqrt_fusion), kind=kOutput, calls=%fused_computation.312 | convolution fusion | flops 6459228160 | bytes 17842176 | tf_op jit(solution)/shard_map/dot_general | solution.py:78
  155.0 5.6 fusion.58
  163.4 23.2 %collective-permute-done.10 = bf16[2,256,512]{2,1,0:T(8,128)(2,1)S(1)} collective-permute-done((bf16[2,256,512]{2,1,0:T(8,128)(2,1)S(1)}, bf16[2,256,512]{2,1,0:T(8,128)(2,1)S(1)}, u32[]{:S(2)}, u32[]{:S(2)}) %collective-permute-start.10) | collective-permute-done | bytes 524320 | tf_op jit(solution)/shard_map/ppermute | solution.py:59
  189.5 5.8 collective-permute-start.13
  197.4 9.6 %collective-permute-done.13 = bf16[2,256,512]{2,1,0:T(8,128)(2,1)} collective-permute-done((bf16[2,256,512]{2,1,0:T(8,128)(2,1)}, bf16[2,256,512]{2,1,0:T(8,128)(2,1)}, u32[]{:S(2)}, u32[]{:S(2)}) %collective-permute-start.13) | collective-permute-done | bytes 524320 | tf_op jit(solution)/shard_map/ppermute | solution.py:59
  237.3 6.5 fusion.114
  251.1 7.8 collective-permute-done.18
  266.0 17.0 %collective-permute-done.34 = bf16[256,2048]{1,0:T(8,128)(2,1)S(1)} collective-permute-done((bf16[256,2048]{1,0:T(8,128)(2,1)S(1)}, bf16[256,2048]{1,0:T(8,128)(2,1)S(1)}, u32[]{:S(2)}, u32[]{:S(2)}) %collective-permute-start.34) | collective-permute-done | bytes 1048608 | tf_op jit(solution)/shard_map/ppermute | solution.py:19
  288.0 26.2 %collective-permute-done.36 = bf16[128,2048]{1,0:T(8,128)(2,1)S(1)} collective-permute-done((bf16[128,2048]{1,0:T(8,128)(2,1)S(1)}, bf16[128,2048]{1,0:T(8,128)(2,1)S(1)}, u32[]{:S(2)}, u32[]{:S(2)}) %collective-permute-start.36) | collective-permute-done | bytes 524320 | tf_op jit(solution)/shard_map/ppermute | solution.py:19
  315.1 8.1 all-gather.14.cloned.1.call-done
  334.5 18.3 %collective-permute-done.22 = bf16[256,2048]{1,0:T(8,128)(2,1)S(1)} collective-permute-done((bf16[256,2048]{1,0:T(8,128)(2,1)S(1)}, bf16[256,2048]{1,0:T(8,128)(2,1)S(1)}, u32[]{:S(2)}, u32[]{:S(2)}) %collective-permute-start.22) | collective-permute-done | bytes 1048608 | tf_op jit(solution)/shard_map/ppermute | solution.py:19
  356.7 10.3 %collective-permute-done.24 = bf16[128,2048]{1,0:T(8,128)(2,1)S(1)} collective-permute-done((bf16[128,2048]{1,0:T(8,128)(2,1)S(1)}, bf16[128,2048]{1,0:T(8,128)(2,1)S(1)}, u32[]{:S(2)}, u32[]{:S(2)}) %collective-permute-start.24) | collective-permute-done | bytes 524320 | tf_op jit(solution)/shard_map/ppermute | solution.py:19
  369.2 4.9 multiply_convert_fusion.1
  382.2 9.2 convert_reduce_fusion
  391.4 7.0 fusion.115
  404.9 8.7 collective-permute-done.38
  417.7 6.5 fusion.122
  424.7 11.8 %collective-permute-done.30 = bf16[256,2048]{1,0:T(8,128)(2,1)S(1)} collective-permute-done((bf16[256,2048]{1,0:T(8,128)(2,1)S(1)}, bf16[256,2048]{1,0:T(8,128)(2,1)S(1)}, u32[]{:S(2)}, u32[]{:S(2)}) %collective-permute-start.30) | collective-permute-done | bytes 1048608 | tf_op jit(solution)/shard_map/ppermute | solution.py:19
  436.6 19.1 %collective-permute-done.39 = bf16[256,2048]{1,0:T(8,128)(2,1)S(1)} collective-permute-done((bf16[256,2048]{1,0:T(8,128)(2,1)S(1)}, bf16[256,2048]{1,0:T(8,128)(2,1)S(1)}, u32[]{:S(2)}, u32[]{:S(2)}) %collective-permute-start.39) | collective-permute-done | bytes 1048608 | tf_op jit(solution)/shard_map/ppermute | solution.py:19
  467.0 7.3 fusion.121
  474.7 9.9 %collective-permute-done.42 = bf16[256,2048]{1,0:T(8,128)(2,1)} collective-permute-done((bf16[256,2048]{1,0:T(8,128)(2,1)}, bf16[256,2048]{1,0:T(8,128)(2,1)}, u32[]{:S(2)}, u32[]{:S(2)}) %collective-permute-start.42) | collective-permute-done | bytes 1048608 | tf_op jit(solution)/shard_map/ppermute | solution.py:19
  495.8 7.0 collective-permute-done.45
  502.9 4.8 convolution_convert_fusion.2
  511.4 7.2 fusion.55
  521.3 7.2 multiply_reduce_fusion
  555.7 88.1 %collective-permute-done.49 = bf16[2,256,512]{2,1,0:T(8,128)(2,1)S(1)} collective-permute-done((bf16[2,256,512]{2,1,0:T(8,128)(2,1)}, bf16[2,256,512]{2,1,0:T(8,128)(2,1)S(1)}, u32[]{:S(2)}, u32[]{:S(2)}) %collective-permute-start.49) | collective-permute-done | bytes 524320 | tf_op jit(solution)/shard_map/ppermute | solution.py:59
  644.0 30.1 %collective-permute-done.52 = bf16[2,256,512]{2,1,0:T(8,128)(2,1)S(1)} collective-permute-done((bf16[2,256,512]{2,1,0:T(8,128)(2,1)S(1)}, bf16[2,256,512]{2,1,0:T(8,128)(2,1)S(1)}, u32[]{:S(2)}, u32[]{:S(2)}) %collective-permute-start.52) | collective-permute-done | bytes 524320 | tf_op jit(solution)/shard_map/ppermute | solution.py:59
  676.0 5.8 fusion.66
  688.9 4.8 copy.82
  693.7 11.0 %convolution_convert_fusion.1 = bf16[2048,768]{1,0:T(8,128)(2,1)} fusion(bf16[2048,512]{1,0:T(8,128)(2,1)S(1)} %copy-done.44, bf16[2048,128]{1,0:T(8,128)(2,1)S(1)} %bitcast.157, bf16[2048,128]{1,0:T(8,128)(2,1)S(1)} %bitcast.155, bf16[2048,2048]{1,0:T(8,128)(2,1)} %constant_dynamic-update-slice_fusion, f32[2048]{0:T(1024)S(1)} %copy-done.72, ...), kind=kOutput, calls=%fused_computation.54 | convolution fusion | flops 6470238208 | bytes 14696448 | tf_op jit(solution)/shard_map/dot_general | solution.py:82
  704.8 13.0 %fusion.119 = f32[2048,2048]{1,0:T(8,128)} fusion(bf16[2048,768]{1,0:T(8,128)(2,1)} %bitcast.150, bf16[2048,768]{1,0:T(8,128)(2,1)} %all-gather.8.cloned.1.call-done), kind=kOutput, calls=%fused_computation.328 | convolution fusion | flops 6442450944 | bytes 23068672 | tf_op jit(solution)/shard_map/dot_general | solution.py:86
  717.7 13.7 %convolution_add_fusion = f32[2048,2048]{1,0:T(8,128)} fusion(f32[2048,2048]{1,0:T(8,128)} %fusion.119, bf16[2048,768]{1,0:T(8,128)(2,1)S(1)} %copy-done.87, bf16[2048,512]{1,0:T(8,128)(2,1)S(1)} %copy-done.44, bf16[2048,128]{1,0:T(8,128)(2,1)S(1)} %bitcast.158, bf16[2048,128]{1,0:T(8,128)(2,1)S(1)} %bitcast.156), kind=kOutput, calls=%fused_computation.8 | convolution fusion | flops 6456082432 | bytes 39845888 | tf_op jit(solution)/shard_map/dot_general | solution.py:86
  731.4 6.1 fusion.15
  746.9 7.4 collective-permute-done.75
  770.9 12.0 %convolution_convert_fusion = bf16[2048,768]{1,0:T(8,128)(2,1)} fusion(bf16[2048,768]{1,0:T(8,128)(2,1)} %bitcast.151, bf16[2048,2048]{1,0:T(8,128)(2,1)} %constant_dynamic-update-slice_fusion, f32[2048]{0:T(1024)S(1)} %copy-done.72, f32[2048]{0:T(1024)S(1)} %copy-done.76), kind=kOutput, calls=%fused_computation.53 | convolution fusion | flops 6460801024 | bytes 14696448 | tf_op jit(solution)/shard_map/dot_general | solution.py:82
  791.6 6.0 fusion.102
  802.5 10.2 %collective-permute-done.54 = bf16[128,2048]{1,0:T(8,128)(2,1)S(1)} collective-permute-done((bf16[128,2048]{1,0:T(8,128)(2,1)S(1)}, bf16[128,2048]{1,0:T(8,128)(2,1)S(1)}, u32[]{:S(2)}, u32[]{:S(2)}) %collective-permute-start.54) | collective-permute-done | bytes 524320 | tf_op jit(solution)/shard_map/ppermute | solution.py:19
  824.2 21.9 %collective-permute-done.86 = bf16[256,512]{1,0:T(8,128)(2,1)} collective-permute-done((bf16[256,512]{1,0:T(8,128)(2,1)S(1)}, bf16[256,512]{1,0:T(8,128)(2,1)}, u32[]{:S(2)}, u32[]{:S(2)}) %collective-permute-start.86) | collective-permute-done | bytes 262176 | tf_op jit(solution)/shard_map/ppermute | solution.py:19
  884.6 13.7 %collective-permute-done.64 = bf16[512,768]{1,0:T(8,128)(2,1)S(1)} collective-permute-done((bf16[512,768]{1,0:T(8,128)(2,1)}, bf16[512,768]{1,0:T(8,128)(2,1)S(1)}, u32[]{:S(2)}, u32[]{:S(2)}) %collective-permute-start.64) | collective-permute-done | bytes 786464 | tf_op jit(solution)/shard_map/ppermute | solution.py:19
  900.7 14.5 %collective-permute-done.68 = bf16[512,768]{1,0:T(8,128)(2,1)S(1)} collective-permute-done((bf16[512,768]{1,0:T(8,128)(2,1)}, bf16[512,768]{1,0:T(8,128)(2,1)S(1)}, u32[]{:S(2)}, u32[]{:S(2)}) %collective-permute-start.68) | collective-permute-done | bytes 786464 | tf_op jit(solution)/shard_map/ppermute | solution.py:19
  918.3 6.9 collective-permute-done.66
  925.2 7.1 collective-permute-done.70
  932.9 10.5 %maximum_select_fusion = f32[1,512,2048]{2,1,0:T(8,128)} fusion(f32[1,256,2048]{2,1,0:T(8,128)} %bitcast.38, f32[1,256,2048]{2,1,0:T(8,128)} %bitcast.37, pred[]{:T(512)S(6)} %eq.42), kind=kLoop, calls=%fused_computation.36 | loop fusion | flops 3145728 | bytes 8388609 | tf_op jit(solution)/shard_map/jit(_where)/select_n | solution.py:364
  (597 shorter events, 300.4 us)
Async XLA Ops:
  7.2 69.9 %all-gather.8.cloned.1.call-start = ((), (), s32[]{:S(2)}) async-start(), calls=%async_computation.6 | async-start | bytes 3932160 | tf_op jit(solution)/shard_map/all_gather | solution.py:162
  10.8 130.7 %all-gather.6.cloned.1.call-start = ((), (), s32[]{:S(2)}) async-start(), calls=%async_computation.5 | async-start | bytes 3932160 | tf_op jit(solution)/shard_map/all_gather | solution.py:162
  13.8 201.3 %all-gather.10.cloned.1.call-start = ((), (), s32[]{:S(2)}) async-start(), calls=%async_computation.7 | async-start | bytes 2621440 | tf_op jit(solution)/shard_map/all_gather | solution.py:165
  16.4 30.5 %collective-permute-start = (bf16[256,2048]{1,0:T(8,128)(2,1)S(1)}, bf16[256,2048]{1,0:T(8,128)(2,1)S(1)}, u32[]{:S(2)}, u32[]{:S(2)}) collective-permute-start(bf16[256,2048]{1,0:T(8,128)(2,1)S(1)} %get-tuple-element.52), channel_id=1, source_target_pairs={{0,2},{2,0},{4,6},{6,4},{1,3},{3,1},{5,7},{7,5},{8,10},{10,8},{12,... | collective-permute-start | bytes 3145736 | tf_op jit(solution)/shard_map/ppermute | solution.py:19
  19.3 29.5 %collective-permute-start.2 = (bf16[256,2048]{1,0:T(8,128)(2,1)S(1)}, bf16[256,2048]{1,0:T(8,128)(2,1)S(1)}, u32[]{:S(2)}, u32[]{:S(2)}) collective-permute-start(bf16[256,2048]{1,0:T(8,128)(2,1)S(1)} %get-tuple-element.52), channel_id=1, source_target_pairs={{0,4},{2,6},{4,0},{6,2},{1,5},{3,7},{5,1},{7,3},{8,12},{10,14},{12... | collective-permute-start | bytes 3145736 | tf_op jit(solution)/shard_map/ppermute | solution.py:19
  27.4 287.7 %all-gather.12.cloned.1.call-start = ((), (), s32[]{:S(2)}) async-start(), calls=%async_computation.8 | async-start | bytes 2621440 | tf_op jit(solution)/shard_map/all_gather | solution.py:162
  197.1 126.1 %all-gather.14.cloned.1.call-start = ((), (), s32[]{:S(2)}) async-start(), calls=%async_computation.9 | async-start | bytes 2621440 | tf_op jit(solution)/shard_map/all_gather | solution.py:165
  233.2 528.4 %reduce-scatter.14.cloned.1.call-start = ((), (), s32[]{:S(2)}) async-start(), calls=%async_computation.14 | async-start | bytes 2621440 | tf_op jit(solution)/shard_map/reduce_scatter | solution.py:168
  247.4 35.5 %collective-permute-start.34 = (bf16[256,2048]{1,0:T(8,128)(2,1)S(1)}, bf16[256,2048]{1,0:T(8,128)(2,1)S(1)}, u32[]{:S(2)}, u32[]{:S(2)}) collective-permute-start(bf16[256,2048]{1,0:T(8,128)(2,1)S(1)} %get-tuple-element.29), channel_id=1, source_target_pairs={{0,2},{2,0},{4,6},{6,4},{1,3},{3,1},{5,7},{7,5},{8,10},{10,8},{12,... | collective-permute-start | bytes 3145736 | tf_op jit(solution)/shard_map/ppermute | solution.py:19
  248.9 34.7 %collective-permute-start.35 = (bf16[256,2048]{1,0:T(8,128)(2,1)S(1)}, bf16[256,2048]{1,0:T(8,128)(2,1)S(1)}, u32[]{:S(2)}, u32[]{:S(2)}) collective-permute-start(bf16[256,2048]{1,0:T(8,128)(2,1)S(1)} %get-tuple-element.29), channel_id=1, source_target_pairs={{0,4},{2,6},{4,0},{6,2},{1,5},{3,7},{5,1},{7,3},{8,12},{10,14},{12... | collective-permute-start | bytes 3145736 | tf_op jit(solution)/shard_map/ppermute | solution.py:19
  251.1 32.5 %collective-permute-start.27 = (f32[512]{0:T(512)S(1)}, f32[512]{0:T(512)S(1)}, u32[]{:S(2)}, u32[]{:S(2)}) collective-permute-start(f32[512]{0:T(512)S(1)} %dynamic_slice.57), channel_id=1, source_target_pairs={{0,1},{1,0},{2,3},{3,2},{4,5},{5,4},{6,7},{7,6},{8,9},{9,8},{10,11... | collective-permute-start | bytes 6152 | tf_op jit(solution)/shard_map/ppermute | solution.py:15
  261.9 61.3 %collective-permute-start.19 = (bf16[256,2048]{1,0:T(8,128)(2,1)}, bf16[256,2048]{1,0:T(8,128)(2,1)}, u32[]{:S(2)}, u32[]{:S(2)}) collective-permute-start(bf16[256,2048]{1,0:T(8,128)(2,1)} %pad_maximum_fusion.11), channel_id=1, source_target_pairs={{0,2},{2,0},{4,6},{6,4},{1,3},{3,1},{5,7},{7,5},{8,10},{10,8},{12,... | collective-permute-start | bytes 3145736 | tf_op jit(solution)/shard_map/ppermute | solution.py:19
  264.4 58.9 %collective-permute-start.21 = (bf16[256,2048]{1,0:T(8,128)(2,1)}, bf16[256,2048]{1,0:T(8,128)(2,1)}, u32[]{:S(2)}, u32[]{:S(2)}) collective-permute-start(bf16[256,2048]{1,0:T(8,128)(2,1)} %pad_maximum_fusion.12), channel_id=1, source_target_pairs={{0,4},{2,6},{4,0},{6,2},{1,5},{3,7},{5,1},{7,3},{8,12},{10,14},{12... | collective-permute-start | bytes 3145736 | tf_op jit(solution)/shard_map/ppermute | solution.py:19
  283.0 31.2 %collective-permute-start.36 = (bf16[128,2048]{1,0:T(8,128)(2,1)S(1)}, bf16[128,2048]{1,0:T(8,128)(2,1)S(1)}, u32[]{:S(2)}, u32[]{:S(2)}) collective-permute-start(bf16[128,2048]{1,0:T(8,128)(2,1)S(1)} %slice.561), channel_id=1, source_target_pairs={{0,4},{2,6},{4,0},{6,2},{1,5},{3,7},{5,1},{7,3},{8,12},{10,14},{12... | collective-permute-start | bytes 1572872 | tf_op jit(solution)/shard_map/ppermute | solution.py:19
  284.4 44.2 %collective-permute-start.37 = (bf16[128,2048]{1,0:T(8,128)(2,1)}, bf16[128,2048]{1,0:T(8,128)(2,1)}, u32[]{:S(2)}, u32[]{:S(2)}) collective-permute-start(bf16[128,2048]{1,0:T(8,128)(2,1)} %slice.562), channel_id=1, source_target_pairs={{0,2},{2,0},{4,6},{6,4},{1,3},{3,1},{5,7},{7,5},{8,10},{10,8},{12,... | collective-permute-start | bytes 1572872 | tf_op jit(solution)/shard_map/ppermute | solution.py:19
  323.2 31.2 %collective-permute-start.28 = (bf16[512,2048]{1,0:T(8,128)(2,1)}, bf16[512,2048]{1,0:T(8,128)(2,1)S(1)}, u32[]{:S(2)}, u32[]{:S(2)}) collective-permute-start(bf16[512,2048]{1,0:T(8,128)(2,1)} %all-gather.14.cloned.1.call-done), channel_id=1, source_target_pairs={{0,1},{1,0},{2,3},{3,2},{4,5},{5,4},{6,7},{7,6},{8,9},{9,8},{10,11... | collective-permute-start | bytes 6291464 | tf_op jit(solution)/shard_map/ppermute | solution.py:15
  327.2 25.6 %collective-permute-start.22 = (bf16[256,2048]{1,0:T(8,128)(2,1)S(1)}, bf16[256,2048]{1,0:T(8,128)(2,1)S(1)}, u32[]{:S(2)}, u32[]{:S(2)}) collective-permute-start(bf16[256,2048]{1,0:T(8,128)(2,1)S(1)} %get-tuple-element.42), channel_id=1, source_target_pairs={{0,2},{2,0},{4,6},{6,4},{1,3},{3,1},{5,7},{7,5},{8,10},{10,8},{12,... | collective-permute-start | bytes 3145736 | tf_op jit(solution)/shard_map/ppermute | solution.py:19
  330.5 25.8 %collective-permute-start.23 = (bf16[256,2048]{1,0:T(8,128)(2,1)S(1)}, bf16[256,2048]{1,0:T(8,128)(2,1)S(1)}, u32[]{:S(2)}, u32[]{:S(2)}) collective-permute-start(bf16[256,2048]{1,0:T(8,128)(2,1)S(1)} %get-tuple-element.42), channel_id=1, source_target_pairs={{0,4},{2,6},{4,0},{6,2},{1,5},{3,7},{5,1},{7,3},{8,12},{10,14},{12... | collective-permute-start | bytes 3145736 | tf_op jit(solution)/shard_map/ppermute | solution.py:19
  402.9 33.7 %collective-permute-start.30 = (bf16[256,2048]{1,0:T(8,128)(2,1)S(1)}, bf16[256,2048]{1,0:T(8,128)(2,1)S(1)}, u32[]{:S(2)}, u32[]{:S(2)}) collective-permute-start(bf16[256,2048]{1,0:T(8,128)(2,1)S(1)} %pad_maximum_fusion.13), channel_id=1, source_target_pairs={{0,2},{2,0},{4,6},{6,4},{1,3},{3,1},{5,7},{7,5},{8,10},{10,8},{12,... | collective-permute-start | bytes 3145736 | tf_op jit(solution)/shard_map/ppermute | solution.py:19
  403.8 32.8 %collective-permute-start.32 = (bf16[256,2048]{1,0:T(8,128)(2,1)S(1)}, bf16[256,2048]{1,0:T(8,128)(2,1)S(1)}, u32[]{:S(2)}, u32[]{:S(2)}) collective-permute-start(bf16[256,2048]{1,0:T(8,128)(2,1)S(1)} %pad_maximum_fusion.14), channel_id=1, source_target_pairs={{0,4},{2,6},{4,0},{6,2},{1,5},{3,7},{5,1},{7,3},{8,12},{10,14},{12... | collective-permute-start | bytes 3145736 | tf_op jit(solution)/shard_map/ppermute | solution.py:19
  414.6 41.1 %collective-permute-start.39 = (bf16[256,2048]{1,0:T(8,128)(2,1)S(1)}, bf16[256,2048]{1,0:T(8,128)(2,1)S(1)}, u32[]{:S(2)}, u32[]{:S(2)}) collective-permute-start(bf16[256,2048]{1,0:T(8,128)(2,1)S(1)} %pad_maximum_fusion.15), channel_id=1, source_target_pairs={{0,2},{2,0},{4,6},{6,4},{1,3},{3,1},{5,7},{7,5},{8,10},{10,8},{12,... | collective-permute-start | bytes 3145736 | tf_op jit(solution)/shard_map/ppermute | solution.py:19
  416.1 39.5 %collective-permute-start.41 = (bf16[256,2048]{1,0:T(8,128)(2,1)S(1)}, bf16[256,2048]{1,0:T(8,128)(2,1)S(1)}, u32[]{:S(2)}, u32[]{:S(2)}) collective-permute-start(bf16[256,2048]{1,0:T(8,128)(2,1)S(1)} %pad_maximum_fusion.16), channel_id=1, source_target_pairs={{0,4},{2,6},{4,0},{6,2},{1,5},{3,7},{5,1},{7,3},{8,12},{10,14},{12... | collective-permute-start | bytes 3145736 | tf_op jit(solution)/shard_map/ppermute | solution.py:19
  424.6 40.1 %collective-permute-start.87 = (bf16[512,2048]{1,0:T(8,128)(2,1)S(1)}, bf16[512,2048]{1,0:T(8,128)(2,1)S(1)}, u32[]{:S(2)}, u32[]{:S(2)}) collective-permute-start(bf16[512,2048]{1,0:T(8,128)(2,1)S(1)} %slice.755), channel_id=1, source_target_pairs={{0,1},{1,0},{2,3},{3,2},{4,5},{5,4},{6,7},{7,6},{8,9},{9,8},{10,11... | collective-permute-start | bytes 6291464 | tf_op jit(solution)/shard_map/ppermute | solution.py:15
  466.9 299.8 %reduce-scatter.12.cloned.1.call-start = ((), (), s32[]{:S(2)}) async-start(), calls=%async_computation.13 | async-start | bytes 2621440 | tf_op jit(solution)/shard_map/reduce_scatter | solution.py:168
  474.6 34.6 %collective-permute-start.82 = (bf16[2048,512]{1,0:T(8,128)(2,1)S(1)}, bf16[2048,512]{1,0:T(8,128)(2,1)S(1)}, u32[]{:S(2)}, u32[]{:S(2)}) collective-permute-start(bf16[2048,512]{1,0:T(8,128)(2,1)S(1)} %slice.756), channel_id=1, source_target_pairs={{0,1},{1,0},{2,3},{3,2},{4,5},{5,4},{6,7},{7,6},{8,9},{9,8},{10,11... | collective-permute-start | bytes 6291464 | tf_op jit(solution)/shard_map/ppermute | solution.py:15
  487.3 250.2 %collective-permute-start.72 = (f32[6656]{0:T(1024)S(1)}, f32[6656]{0:T(1024)S(1)}, u32[]{:S(2)}, u32[]{:S(2)}) collective-permute-start(f32[6656]{0:T(1024)S(1)} %pad_maximum_fusion.28), channel_id=1, source_target_pairs={{0,1},{1,0},{2,3},{3,2},{4,5},{5,4},{6,7},{7,6},{8,9},{9,8},{10,11... | collective-permute-start | bytes 79880 | tf_op jit(solution)/shard_map/ppermute | solution.py:15
  487.3 267.1 %collective-permute-start.33 = (bf16[256,2048]{1,0:T(8,128)(2,1)}, bf16[256,2048]{1,0:T(8,128)(2,1)}, u32[]{:S(2)}, u32[]{:S(2)}) collective-permute-start(bf16[256,2048]{1,0:T(8,128)(2,1)} %get-tuple-element.91), channel_id=1, source_target_pairs={{0,1},{1,0},{2,3},{3,2},{4,5},{5,4},{6,7},{7,6},{8,9},{9,8},{10,11... | collective-permute-start | bytes 3145736 | tf_op jit(solution)/shard_map/ppermute | solution.py:15
  511.3 309.8 %reduce-scatter.10.cloned.1.call-start = ((), (), s32[]{:S(2)}) async-start(), calls=%async_computation.12 | async-start | bytes 2621440 | tf_op jit(solution)/shard_map/reduce_scatter | solution.py:168
  544.9 332.8 %reduce-scatter.6.cloned.1.call-start = ((), (), s32[]{:S(2)}) async-start(), calls=%async_computation.10 | async-start | bytes 3932160 | tf_op jit(solution)/shard_map/reduce_scatter | solution.py:168
  545.0 98.9 %collective-permute-start.49 = (bf16[2,256,512]{2,1,0:T(8,128)(2,1)}, bf16[2,256,512]{2,1,0:T(8,128)(2,1)S(1)}, u32[]{:S(2)}, u32[]{:S(2)}) collective-permute-start(bf16[2,256,512]{2,1,0:T(8,128)(2,1)} %get-tuple-element.32), channel_id=1, source_target_pairs={{8,0},{9,1},{10,2},{11,3},{12,4},{13,5},{14,6},{15,7}} | collective-permute-start | bytes 1572872 | tf_op jit(solution)/shard_map/ppermute | solution.py:59
  548.4 125.8 %collective-permute-start.52 = (bf16[2,256,512]{2,1,0:T(8,128)(2,1)S(1)}, bf16[2,256,512]{2,1,0:T(8,128)(2,1)S(1)}, u32[]{:S(2)}, u32[]{:S(2)}) collective-permute-start(bf16[2,256,512]{2,1,0:T(8,128)(2,1)S(1)} %get-tuple-element.34), channel_id=1, source_target_pairs={{8,0},{9,1},{10,2},{11,3},{12,4},{13,5},{14,6},{15,7}} | collective-permute-start | bytes 1572872 | tf_op jit(solution)/shard_map/ppermute | solution.py:59
  704.7 175.2 %reduce-scatter.8.cloned.1.call-start = ((), (), s32[]{:S(2)}) async-start(), calls=%async_computation.11 | async-start | bytes 3932160 | tf_op jit(solution)/shard_map/reduce_scatter | solution.py:168
  737.5 54.1 %collective-permute-start.53 = (bf16[4,256,2048]{2,1,0:T(8,128)(2,1)}, bf16[4,256,2048]{2,1,0:T(8,128)(2,1)}, u32[]{:S(2)}, u32[]{:S(2)}) collective-permute-start(bf16[4,256,2048]{2,1,0:T(8,128)(2,1)} %fusion.15), channel_id=1, source_target_pairs={{0,1},{1,0},{2,3},{3,2},{4,5},{5,4},{6,7},{7,6},{8,9},{9,8},{10,11... | collective-permute-start | bytes 12582920 | tf_op jit(solution)/shard_map/ppermute | solution.py:15
  761.6 24.9 %collective-permute-start.88 = (bf16[512,512]{1,0:T(8,128)(2,1)}, bf16[512,512]{1,0:T(8,128)(2,1)S(1)}, u32[]{:S(2)}, u32[]{:S(2)}) collective-permute-start(bf16[512,512]{1,0:T(8,128)(2,1)} %reduce-scatter.14.cloned.1.call-done), channel_id=1, source_target_pairs={{0,2},{2,0},{4,6},{6,4},{1,3},{3,1},{5,7},{7,5},{8,10},{10,8},{12,... | collective-permute-start | bytes 1572872 | tf_op jit(solution)/shard_map/ppermute | solution.py:19
  763.1 25.6 %collective-permute-start.89 = (bf16[512,512]{1,0:T(8,128)(2,1)}, bf16[512,512]{1,0:T(8,128)(2,1)S(1)}, u32[]{:S(2)}, u32[]{:S(2)}) collective-permute-start(bf16[512,512]{1,0:T(8,128)(2,1)} %reduce-scatter.14.cloned.1.call-done), channel_id=1, source_target_pairs={{0,4},{2,6},{4,0},{6,2},{1,5},{3,7},{5,1},{7,3},{8,12},{10,14},{12... | collective-permute-start | bytes 1572872 | tf_op jit(solution)/shard_map/ppermute | solution.py:19
  786.6 31.9 %collective-permute-start.90 = (bf16[256,512]{1,0:T(8,128)(2,1)S(1)}, bf16[256,512]{1,0:T(8,128)(2,1)S(1)}, u32[]{:S(2)}, u32[]{:S(2)}) collective-permute-start(bf16[256,512]{1,0:T(8,128)(2,1)S(1)} %slice.622), channel_id=1, source_target_pairs={{0,4},{2,6},{4,0},{6,2},{1,5},{3,7},{5,1},{7,3},{8,12},{10,14},{12... | collective-permute-start | bytes 786440 | tf_op jit(solution)/shard_map/ppermute | solution.py:19
  788.7 32.4 %collective-permute-start.91 = (bf16[256,512]{1,0:T(8,128)(2,1)S(1)}, bf16[256,512]{1,0:T(8,128)(2,1)}, u32[]{:S(2)}, u32[]{:S(2)}) collective-permute-start(bf16[256,512]{1,0:T(8,128)(2,1)S(1)} %slice.623), channel_id=1, source_target_pairs={{0,2},{2,0},{4,6},{6,4},{1,3},{3,1},{5,7},{7,5},{8,10},{10,8},{12,... | collective-permute-start | bytes 786440 | tf_op jit(solution)/shard_map/ppermute | solution.py:19
  790.9 30.8 %collective-permute-start.85 = (bf16[256,512]{1,0:T(8,128)(2,1)}, bf16[256,512]{1,0:T(8,128)(2,1)}, u32[]{:S(2)}, u32[]{:S(2)}) collective-permute-start(bf16[256,512]{1,0:T(8,128)(2,1)} %slice.618), channel_id=1, source_target_pairs={{0,4},{2,6},{4,0},{6,2},{1,5},{3,7},{5,1},{7,3},{8,12},{10,14},{12... | collective-permute-start | bytes 786440 | tf_op jit(solution)/shard_map/ppermute | solution.py:19
  814.1 43.5 %collective-permute-start.55 = (bf16[256,2048]{1,0:T(8,128)(2,1)}, bf16[256,2048]{1,0:T(8,128)(2,1)S(1)}, u32[]{:S(2)}, u32[]{:S(2)}) collective-permute-start(bf16[256,2048]{1,0:T(8,128)(2,1)} %pad_maximum_fusion.18), channel_id=1, source_target_pairs={{0,2},{2,0},{4,6},{6,4},{1,3},{3,1},{5,7},{7,5},{8,10},{10,8},{12,... | collective-permute-start | bytes 3145736 | tf_op jit(solution)/shard_map/ppermute | solution.py:19
  815.7 41.9 %collective-permute-start.57 = (bf16[256,2048]{1,0:T(8,128)(2,1)}, bf16[256,2048]{1,0:T(8,128)(2,1)S(1)}, u32[]{:S(2)}, u32[]{:S(2)}) collective-permute-start(bf16[256,2048]{1,0:T(8,128)(2,1)} %pad_maximum_fusion.19), channel_id=1, source_target_pairs={{0,4},{2,6},{4,0},{6,2},{1,5},{3,7},{5,1},{7,3},{8,12},{10,14},{12... | collective-permute-start | bytes 3145736 | tf_op jit(solution)/shard_map/ppermute | solution.py:19
  818.5 27.6 %collective-permute-start.86 = (bf16[256,512]{1,0:T(8,128)(2,1)S(1)}, bf16[256,512]{1,0:T(8,128)(2,1)}, u32[]{:S(2)}, u32[]{:S(2)}) collective-permute-start(bf16[256,512]{1,0:T(8,128)(2,1)S(1)} %slice.619), channel_id=1, source_target_pairs={{0,2},{2,0},{4,6},{6,4},{1,3},{3,1},{5,7},{7,5},{8,10},{10,8},{12,... | collective-permute-start | bytes 786440 | tf_op jit(solution)/shard_map/ppermute | solution.py:19
  821.1 34.6 %collective-permute-start.78 = (bf16[512,512]{1,0:T(8,128)(2,1)}, bf16[512,512]{1,0:T(8,128)(2,1)S(1)}, u32[]{:S(2)}, u32[]{:S(2)}) collective-permute-start(bf16[512,512]{1,0:T(8,128)(2,1)} %reduce-scatter.10.cloned.1.call-done), channel_id=1, source_target_pairs={{0,2},{2,0},{4,6},{6,4},{1,3},{3,1},{5,7},{7,5},{8,10},{10,8},{12,... | collective-permute-start | bytes 1572872 | tf_op jit(solution)/shard_map/ppermute | solution.py:19
  821.7 35.5 %collective-permute-start.79 = (bf16[512,512]{1,0:T(8,128)(2,1)}, bf16[512,512]{1,0:T(8,128)(2,1)S(1)}, u32[]{:S(2)}, u32[]{:S(2)}) collective-permute-start(bf16[512,512]{1,0:T(8,128)(2,1)} %reduce-scatter.10.cloned.1.call-done), channel_id=1, source_target_pairs={{0,4},{2,6},{4,0},{6,2},{1,5},{3,7},{5,1},{7,3},{8,12},{10,14},{12... | collective-permute-start | bytes 1572872 | tf_op jit(solution)/shard_map/ppermute | solution.py:19
  876.6 56.3 %collective-permute-start.58 = (f32[256,2048]{1,0:T(8,128)}, f32[256,2048]{1,0:T(8,128)}, u32[]{:S(2)}, u32[]{:S(2)}) collective-permute-start(f32[256,2048]{1,0:T(8,128)} %fusion.27), channel_id=1, source_target_pairs={{0,1},{1,0},{2,3},{3,2},{4,5},{5,4},{6,7},{7,6},{8,9},{9,8},{10,11... | collective-permute-start | bytes 6291464 | tf_op jit(solution)/shard_map/ppermute | solution.py:15
  879.9 35.3 %collective-permute-start.68 = (bf16[512,768]{1,0:T(8,128)(2,1)}, bf16[512,768]{1,0:T(8,128)(2,1)S(1)}, u32[]{:S(2)}, u32[]{:S(2)}) collective-permute-start(bf16[512,768]{1,0:T(8,128)(2,1)} %reduce-scatter.8.cloned.1.call-done), channel_id=1, source_target_pairs={{0,2},{2,0},{4,6},{6,4},{1,3},{3,1},{5,7},{7,5},{8,10},{10,8},{12,... | collective-permute-start | bytes 2359304 | tf_op jit(solution)/shard_map/ppermute | solution.py:19
  880.3 36.4 %collective-permute-start.69 = (bf16[512,768]{1,0:T(8,128)(2,1)}, bf16[512,768]{1,0:T(8,128)(2,1)S(1)}, u32[]{:S(2)}, u32[]{:S(2)}) collective-permute-start(bf16[512,768]{1,0:T(8,128)(2,1)} %reduce-scatter.8.cloned.1.call-done), channel_id=1, source_target_pairs={{0,4},{2,6},{4,0},{6,2},{1,5},{3,7},{5,1},{7,3},{8,12},{10,14},{12... | collective-permute-start | bytes 2359304 | tf_op jit(solution)/shard_map/ppermute | solution.py:19
  898.4 26.8 %collective-permute-start.66 = (bf16[256,768]{1,0:T(8,128)(2,1)S(1)}, bf16[256,768]{1,0:T(8,128)(2,1)S(1)}, u32[]{:S(2)}, u32[]{:S(2)}) collective-permute-start(bf16[256,768]{1,0:T(8,128)(2,1)S(1)} %slice.593), channel_id=1, source_target_pairs={{0,4},{2,6},{4,0},{6,2},{1,5},{3,7},{5,1},{7,3},{8,12},{10,14},{12... | collective-permute-start | bytes 1179656 | tf_op jit(solution)/shard_map/ppermute | solution.py:19
  899.9 32.4 %collective-permute-start.67 = (bf16[256,768]{1,0:T(8,128)(2,1)S(1)}, bf16[256,768]{1,0:T(8,128)(2,1)S(1)}, u32[]{:S(2)}, u32[]{:S(2)}) collective-permute-start(bf16[256,768]{1,0:T(8,128)(2,1)S(1)} %slice.594), channel_id=1, source_target_pairs={{0,2},{2,0},{4,6},{6,4},{1,3},{3,1},{5,7},{7,5},{8,10},{10,8},{12,... | collective-permute-start | bytes 1179656 | tf_op jit(solution)/shard_map/ppermute | solution.py:19
  (147 other events, 2436.0 us)
Sparse Core Ops, SparseCore 0:
  10.9 66.1 all-gather.7
  79.3 62.1 all-gather.5
  143.6 53.2 all-gather.9
  198.9 45.1 all-gather.11
  245.5 77.6 all-gather.13
  467.0 77.5 reduce-scatter.13
  547.6 54.4 reduce-scatter.11
  604.9 70.8 reduce-scatter.9
  704.8 59.5 reduce-scatter.5
  783.0 58.9 reduce-scatter.7

commit v2 on v1

v2 whole, which is shorter than its diff:
```python
import math

import jax
import jax.numpy as jnp
from jax import lax
from jax.experimental import pallas as pl
from jax.experimental.pallas import tpu as pltpu
from jax.sharding import PartitionSpec as P

KEY = 256
VAL = 512
F32 = jnp.float32
BF16 = jnp.bfloat16


def swap_core(value):
    return lax.ppermute(value, "head", [(0, 1), (1, 0)])


def swap_batch(value, mask):
    return lax.ppermute(value, "batch", [(place, place ^ mask) for place in range(4)])


def after(value, *earlier):
    return lax.optimization_barrier((value,) + earlier)[0]


def spread(piece):
    middle = piece.shape[0] // 2
    first = swap_batch(piece, 1)
    second = swap_batch(piece, 2)
    upper = swap_batch(first[:middle], 2)
    lower = swap_batch(second[middle:], 1)
    return first, second, jnp.concatenate([upper, lower], axis=0)


def fold(parts):
    middle = parts[3].shape[0] // 2
    far = parts[3]
    upper = swap_batch(far[:middle], 1)
    lower = swap_batch(far[middle:], 2)
    to_first = jnp.concatenate(
        [parts[1][:middle], parts[1][middle:] + lower.astype(F32)], axis=0
    ).astype(BF16)
    to_second = jnp.concatenate(
        [parts[2][:middle] + upper.astype(F32), parts[2][middle:]], axis=0
    ).astype(BF16)
    first = swap_batch(to_first, 1)
    second = swap_batch(to_second, 2)
    return parts[0] + first.astype(F32) + second.astype(F32)


def total(value):
    for axis in ("batch", "seq"):
        count = lax.axis_size(axis)
        step = 1
        while step < count:
            moved = lax.ppermute(value, axis, [(place, place ^ step) for place in range(count)])
            value = value + moved
            step *= 2
    return value


def turn(value, steps):
    count = lax.axis_size("seq")
    return lax.ppermute(
        value, "seq", [(source, (source + steps) % count) for source in range(count)]
    )


def hop(value, source, target):
    return lax.ppermute(value, "seq", [(source, target)])


def carry(keep, added, forward):
    count = lax.axis_size("seq")
    entered = []
    for chunk in range(0, 4, 2):
        factor = keep[chunk : chunk + 2, None, None]
        own = added[chunk : chunk + 2]
        state = jnp.zeros(own.shape, BF16)
        for step in range(count - 1):
            sent = (factor * state.astype(F32) + own).astype(BF16)
            source, target = (step, step + 1) if forward else (count - 1 - step, count - 2 - step)
            state = state + hop(sent, source, target)
        entered.append(state)
    return jnp.concatenate(entered, axis=0)


def dot(left, right):
    return jnp.dot(left, right, preferred_element_type=F32)


def contract_rows(left, right):
    return lax.dot_general(left, right, (((0,), (0,)), ((), ())), preferred_element_type=F32)


def contract_cols(left, right):
    return lax.dot_general(left, right, (((1,), (1,)), ((), ())), preferred_element_type=F32)


def normalize_back(grad_unit, unit_norm, inverse):
    mean_grad = jnp.mean(grad_unit, axis=-1, keepdims=True)
    mean_cross = jnp.mean(grad_unit * unit_norm, axis=-1, keepdims=True)
    return inverse * (grad_unit - mean_grad - unit_norm * mean_cross)


def rotated(values, cosine, sine):
    middle = values.shape[-1] // 2
    former, latter = (values[:, :middle], values[:, middle:])
    return jnp.concatenate(
        [former * cosine - latter * sine, latter * cosine + former * sine], axis=-1
    )


def flat(ref):
    value = ref[...]
    return value.reshape(-1, value.shape[-1])


def put(ref, value):
    ref[...] = value.reshape(ref.shape).astype(ref.dtype)


def weigh(value, weight):
    return (value.astype(F32) * weight).astype(BF16)


def decay_of(columns, lines, rate):
    distance = columns[:, 3:4] - lines[1:2]
    linked = (columns[:, 2:3] == lines[0:1]) & (distance >= 0)
    return jnp.where(linked, jnp.exp(jnp.maximum(distance, 0.0) * rate), 0.0)


def key_value_kernel(normed, weight, cosine, sine, columns, keys, values, added):
    product = dot(flat(normed), weight[...])
    key = (rotated(product[:, :KEY], flat(cosine), flat(sine)) * KEY ** (-0.5)).astype(BF16)
    value = product[:, KEY:].astype(BF16)
    put(keys, key)
    put(values, value)
    put(added, contract_rows(weigh(key, flat(columns)[:, 1:2]), value))


def retain_kernel(
    normed, weight, cosine, sine, columns, lines, rate, keys, values, memory, scale, shift,
    queries, gate, unit, inverse, gated,
):
    product = dot(flat(normed), weight[...])
    query = rotated(product[:, :KEY], flat(cosine), flat(sine)).astype(BF16)
    table = flat(columns)
    decay = decay_of(table, flat(lines), rate[...])
    mixing = (contract_cols(query, flat(keys)) * decay).astype(BF16)
    retained = dot(mixing, flat(values)) + dot(weigh(query, table[:, 0:1]), flat(memory))
    centred = retained - jnp.mean(retained, axis=-1, keepdims=True)
    factor = lax.rsqrt(jnp.mean(centred * centred, axis=-1, keepdims=True) + 1.0)
    unit_norm = centred * factor
    gate_pre = product[:, KEY:]
    put(queries, query)
    put(gate, gate_pre)
    put(unit, unit_norm)
    put(inverse, factor)
    grouped = unit_norm * scale[...] + shift[...]
    put(gated, gate_pre * jax.nn.sigmoid(gate_pre) * grouped)


def gate_back_kernel(
    grad_own, grad_far, gate, unit, inverse, scale, shift, columns, queries,
    grad_gate, grad_retained, reach, sums,
):
    grad_gated = jnp.concatenate([flat(grad_own), flat(grad_far)], axis=0).astype(F32)
    gate_pre, unit_norm = flat(gate), flat(unit)
    grouped = unit_norm * scale[...] + shift[...]
    sigmoid = jax.nn.sigmoid(gate_pre)
    put(grad_gate, grad_gated * grouped * sigmoid * (1.0 + gate_pre * (1.0 - sigmoid)))
    grad_grouped = grad_gated * (gate_pre * sigmoid)
    part = jnp.concatenate(
        [
            jnp.sum(grad_grouped * unit_norm, axis=0, keepdims=True),
            jnp.sum(grad_grouped, axis=0, keepdims=True),
        ],
        axis=0,
    )

    @pl.when(pl.program_id(0) == 0)
    def first():
        sums[...] = part

    @pl.when(pl.program_id(0) > 0)
    def later():
        sums[...] += part

    grad = normalize_back(grad_grouped * scale[...], unit_norm, flat(inverse)).astype(BF16)
    put(grad_retained, grad)
    put(reach, contract_rows(weigh(flat(queries), flat(columns)[:, 0:1]), grad))


def local_back_kernel(
    grad_retained, grad_gate, queries, keys, values, memory, columns, lines, rate, cosine, sine,
    grad_query_gate, grad_keys, grad_values,
):
    grad, query, key, value = flat(grad_retained), flat(queries), flat(keys), flat(values)
    table = flat(columns)
    decay = decay_of(table, flat(lines), rate[...])
    mixing = (contract_cols(query, key) * decay).astype(BF16)
    grad_scores = (contract_cols(grad, value) * decay).astype(BF16)
    grad_query = dot(grad_scores, key) + table[:, 0:1] * contract_cols(grad, flat(memory))
    grad_query = rotated(grad_query, flat(cosine), -flat(sine)).astype(BF16)
    put(grad_query_gate, jnp.concatenate([grad_query, flat(grad_gate)], axis=-1))
    put(grad_keys, contract_rows(grad_scores, query))
    put(grad_values, contract_rows(mixing, grad))


def state_back_kernel(
    grad_keys, grad_values, keys, values, grad_memory, columns, cosine, sine, grad_key_value
):
    weight = flat(columns)[:, 1:2]
    state = flat(grad_memory)
    grad_key = flat(grad_keys) + weight * contract_cols(flat(values), state)
    grad_key = rotated(grad_key, flat(cosine), -flat(sine)) * KEY ** (-0.5)
    grad_value = flat(grad_values) + dot(weigh(flat(keys), weight), state)
    put(
        grad_key_value,
        jnp.concatenate([grad_key.astype(BF16), grad_value.astype(BF16)], axis=-1),
    )


def stream_kernel(
    normed, weight, cosine, sine, columns, lines, rate, scale, shift,
    queries, keys, values, memory, gate, unit, inverse, gated, state,
):
    @pl.when(pl.program_id(0) == 0)
    def first():
        state[...] = jnp.zeros_like(state)

    product = dot(flat(normed), weight[...])
    table = flat(columns)
    query = rotated(product[:, :KEY], flat(cosine), flat(sine)).astype(BF16)
    key = rotated(product[:, KEY : 2 * KEY], flat(cosine), flat(sine)) * KEY ** (-0.5)
    key = key.astype(BF16)
    value = product[:, 2 * KEY : 2 * KEY + VAL].astype(BF16)
    gate_pre = product[:, 2 * KEY + VAL :]
    low = state[...].astype(BF16)
    decay = decay_of(table, flat(lines), rate[...])
    mixing = (contract_cols(query, key) * decay).astype(BF16)
    retained = dot(mixing, value) + dot(weigh(query, table[:, 0:1]), low)
    state[...] = table[0:1, 4:5] * state[...] + contract_rows(weigh(key, table[:, 1:2]), value)
    centred = retained - jnp.mean(retained, axis=-1, keepdims=True)
    factor = lax.rsqrt(jnp.mean(centred * centred, axis=-1, keepdims=True) + 1.0)
    unit_norm = centred * factor
    put(queries, query)
    put(keys, key)
    put(values, value)
    put(memory, low)
    put(gate, gate_pre)
    put(unit, unit_norm)
    put(inverse, factor)
    grouped = unit_norm * scale[...] + shift[...]
    put(gated, gate_pre * jax.nn.sigmoid(gate_pre) * grouped)


def stream_back_kernel(
    grad_own, grad_far, gate, unit, inverse, scale, shift, columns, lines, rate, cosine, sine,
    queries, keys, values, memory, grads, sums, state,
):
    grad_gated = jnp.concatenate([flat(grad_own), flat(grad_far)], axis=0).astype(F32)
    gate_pre, unit_norm, table = flat(gate), flat(unit), flat(columns)
    query, key, value = flat(queries), flat(keys), flat(values)
    entry, weight = table[:, 0:1], table[:, 1:2]
    grouped = unit_norm * scale[...] + shift[...]
    sigmoid = jax.nn.sigmoid(gate_pre)
    grad_gate = grad_gated * grouped * sigmoid * (1.0 + gate_pre * (1.0 - sigmoid))
    grad_grouped = grad_gated * (gate_pre * sigmoid)

    @pl.when(pl.program_id(0) == 0)
    def first():
        state[...] = jnp.zeros_like(state)
        sums[...] = jnp.zeros_like(sums)

    sums[0:1] += jnp.sum(grad_grouped * unit_norm, axis=0, keepdims=True)
    sums[1:2] += jnp.sum(grad_grouped, axis=0, keepdims=True)
    grad = normalize_back(grad_grouped * scale[...], unit_norm, flat(inverse)).astype(BF16)
    decay = decay_of(table, flat(lines), rate[...])
    mixing = (contract_cols(query, key) * decay).astype(BF16)
    grad_scores = (contract_cols(grad, value) * decay).astype(BF16)
    low = state[...].astype(BF16)
    grad_query = dot(grad_scores, key) + entry * contract_cols(grad, flat(memory))
    grad_key = contract_rows(grad_scores, query) + weight * contract_cols(value, low)
    grad_value = contract_rows(mixing, grad) + dot(weigh(key, weight), low)
    state[...] = table[0:1, 4:5] * state[...] + contract_rows(weigh(query, entry), grad)
    cosines, sines = flat(cosine), -flat(sine)
    put(
        grads,
        jnp.concatenate(
            [
                rotated(grad_query, cosines, sines).astype(BF16),
                (rotated(grad_key, cosines, sines) * KEY ** (-0.5)).astype(BF16),
                grad_value.astype(BF16),
                grad_gate.astype(BF16),
            ],
            axis=-1,
        ),
    )


def rows_spec(value, whole=False):
    if whole:
        return pl.BlockSpec(value.shape, lambda slot: (0,) * len(value.shape))
    if len(value.shape) == 4:
        two, _, half, width = value.shape
        return pl.BlockSpec((two, 1, half, width), lambda slot: (0, slot, 0, 0))
    return pl.BlockSpec((1,) + value.shape[1:], lambda slot: (slot, 0, 0))


def block_spec(value, whole=False, last=False):
    if whole:
        return pl.BlockSpec(value.shape, lambda step: (0,) * len(value.shape))
    rank = len(value.shape)
    shape = value.shape[: rank - 3] + (1,) + value.shape[rank - 2 :]
    return pl.BlockSpec(
        shape, lambda step: (0,) * (rank - 3) + (3 - step if last else step,) + (0, 0)
    )


def by_block(kernel, inputs, shared, out_shapes, last, summed=0):
    outs = [jax.ShapeDtypeStruct(shape, dtype) for shape, dtype in out_shapes]
    return pl.pallas_call(
        kernel,
        grid=(4,),
        in_specs=[block_spec(v, at in shared, last) for at, v in enumerate(inputs)],
        out_specs=[block_spec(v, at >= len(outs) - summed, last) for at, v in enumerate(outs)],
        out_shape=outs,
        scratch_shapes=[pltpu.VMEM((KEY, VAL), F32)],
        compiler_params=pltpu.CompilerParams(
            dimension_semantics=("arbitrary",), vmem_limit_bytes=56 * 2**20
        ),
    )(*inputs)


def by_slot(kernel, slotted, shared, order, out_shapes, summed=0):
    inputs = tuple(slotted) + tuple(shared)
    specs = [rows_spec(v) for v in slotted] + [rows_spec(v, True) for v in shared]
    outs = [jax.ShapeDtypeStruct(shape, dtype) for shape, dtype in out_shapes]
    out_specs = [rows_spec(v, at >= len(outs) - summed) for at, v in enumerate(outs)]
    return pl.pallas_call(
        kernel,
        grid=(4,),
        in_specs=[specs[at] for at in order],
        out_specs=out_specs,
        out_shape=outs,
        compiler_params=pltpu.CompilerParams(
            dimension_semantics=("arbitrary",), vmem_limit_bytes=56 * 2**20
        ),
    )(*[inputs[at] for at in order])


def slot_products(product, left, right):
    size = left.shape[0] // 4
    far = product(left[3 * size :], right).astype(BF16)
    left, right, far = lax.optimization_barrier((left, right, far))
    near = product(left[size : 3 * size], right)
    own = product(left[:size], right)
    return [own, near[:size], near[size:], far]


def place_columns(pieces, place, width):
    rows = pieces[0].shape[0]
    result = jnp.zeros((rows, 4 * width), F32)
    for slot, piece in enumerate(pieces):
        result = lax.dynamic_update_slice(result, piece.astype(F32), (0, (place ^ slot) * width))
    return result


def place_rows(pieces, place, height):
    result = jnp.zeros((4 * height, pieces[0].shape[1]), F32)
    for slot, piece in enumerate(pieces):
        result = lax.dynamic_update_slice(result, piece.astype(F32), ((place ^ slot) * height, 0))
    return result


def body(
    tokens,
    prescale,
    query_weight,
    key_weight,
    value_weight,
    gate_weight,
    groupscale,
    groupshift,
    output_weight,
    postscale,
    postshift,
    expand_weight,
    hiddenbias,
    reduce_weight,
    outputbias,
    cotangent,
    doc_lengths,
    segments,
):
    _, rows, width = tokens.shape
    half = rows // 2
    part = hiddenbias.shape[0] // 4
    core = lax.axis_index("head")
    place = lax.axis_index("batch")
    block = lax.axis_index("seq")
    within = lax.axis_size("seq") == 4
    size = half // 4

    def shares_of(*values):
        def share(of):
            cut = [lax.dynamic_slice_in_dim(v, (2 * of + core) * size, size, 0) for v in values]
            return jnp.concatenate(cut + [marks], axis=0)

        held = [share(place)]
        held += [swap_batch(share(place ^ slot), slot) for slot in (1, 2, 3)]
        return jnp.stack(held)

    def plane_of(held):
        result = jnp.zeros(held.shape, held.dtype)
        for steps in range(4):
            moved = lax.dynamic_index_in_dim(held, place ^ ((block + steps) % 4), 0, True)
            if steps:
                moved = turn(moved, steps)
            result = lax.dynamic_update_slice_in_dim(result, moved, (block - steps) % 4, 0)
        return result

    def give_back(value, dtype):
        if not within:
            return both_rows(value, swap_core(value)).astype(dtype)
        value = value.reshape(4, size, width)
        held = jnp.zeros((4, size, width), value.dtype)
        for steps in range(4):
            moved = lax.dynamic_index_in_dim(value, (block - steps) % 4, 0, True)
            if steps:
                moved = turn(moved, -steps)
            held = lax.dynamic_update_slice_in_dim(held, moved, (block + steps) % 4, 0)
        own = []
        for slot in range(4):
            moved = lax.dynamic_index_in_dim(held, place ^ slot, 0, False)
            own.append(swap_batch(moved, slot) if slot else moved)
        own = jnp.stack(own)
        far = swap_core(own)
        result = jnp.zeros((8, size, width), dtype)
        for slot in range(4):
            for side, shared in ((core, own), (1 - core, far)):
                result = lax.dynamic_update_slice_in_dim(
                    result, shared[slot : slot + 1].astype(dtype), 2 * (place ^ slot) + side, 0
                )
        return result.reshape(rows, width)

    def both_rows(own, far):
        result = jnp.zeros((rows, width), own.dtype)
        result = lax.dynamic_update_slice_in_dim(result, own, core * half, 0)
        return lax.dynamic_update_slice_in_dim(result, far, (1 - core) * half, 0)

    def cols_of(weight, size):
        return lax.dynamic_slice_in_dim(weight, place * size, size, 1)

    def rows_of(weight, size):
        return lax.dynamic_slice_in_dim(weight, place * size, size, 0)

    def gather_rows(weight):
        return lax.all_gather(weight, "seq", axis=0, tiled=True)

    def gather_cols(weight):
        return lax.all_gather(weight, "seq", axis=1, tiled=True)

    def scatter(grad, dimension):
        return lax.psum_scatter(grad.astype(BF16), "seq", scatter_dimension=dimension, tiled=True)

    project = jnp.concatenate(
        [
            cols_of(query_weight, KEY),
            cols_of(key_weight, KEY),
            cols_of(value_weight, VAL),
            cols_of(gate_weight, VAL),
        ],
        axis=1,
    )
    tokens = after(tokens, project)
    project = gather_rows(project)

    steps = jnp.arange(half, dtype=jnp.int32)
    if within:
        lengths = doc_lengths[0]
        marks = jnp.concatenate([segments[0], lengths // 64, lengths % 64]).astype(BF16)
        marks = jnp.pad(marks[None], ((0, 7), (0, width - marks.shape[0])))
        held = shares_of(cotangent[0], tokens[0])
        held_dy, held = held[:, :size], held[:, size:]
        held = plane_of(held)
        tokens_own = held[:, :size].reshape(half, width)
        marks = held[:, size].astype(jnp.int32)
        natural = marks[:, :rows]
        count = doc_lengths.shape[1]
        spans = marks[:, rows : rows + count] * 64 + marks[:, rows + count : rows + 2 * count]
        before = jnp.concatenate([jnp.full((1,), -1, jnp.int32), natural[:-1, rows - 1]])
        side, slot = jnp.arange(2)[:, None], jnp.arange(4)[None]
        share = 2 * (place ^ slot) + (core ^ side)
        index = share[:, :, None, None] * size + steps[:size]
        segment = jnp.take(natural.reshape(4, 8, size), share.reshape(8), axis=1)
        segment = segment.transpose(1, 0, 2).reshape(2, 4, 4, size)
        index = jnp.broadcast_to(index, segment.shape)
        at_block = jnp.arange(4)[None, None, :, None]
        stream_index = at_block * rows + index
        form = (1, 1, 4, 1)
    else:
        before = lax.ppermute(
            segments[0, rows - 1 :],
            "seq",
            [(source, source + 1) for source in range(lax.axis_size("seq") - 1)],
        )
        before = jnp.where(block == 0, -1, before)
        marks = jnp.concatenate([segments[0], doc_lengths[0], before])[None]
        marks = jnp.concatenate([marks, swap_batch(marks, 1)], axis=0)
        marks = jnp.concatenate([marks, swap_batch(marks, 2)], axis=0)
        natural, spans, before = marks[:, :rows], marks[:, rows:-1], marks[:, -1]
        tokens_own = lax.dynamic_slice_in_dim(tokens[0], core * half, half, 0)
        dy_own = lax.dynamic_slice_in_dim(cotangent[0], core * half, half, 0)
        index = jnp.stack([core * half + steps, (1 - core) * half + steps])[:, None]
        upper, lower = natural[None, :, :half], natural[None, :, half:]
        segment = jnp.where(
            core == 0,
            jnp.concatenate([upper, lower], axis=0),
            jnp.concatenate([lower, upper], axis=0),
        )
        index = jnp.broadcast_to(index, segment.shape)
        stream_index = block * rows + index
        form = (1, 4, 1)
    wide = tokens_own.astype(F32)
    inverse = lax.rsqrt(jnp.mean(wide * wide, axis=-1, keepdims=True) + 1e-06)
    scaled = wide * inverse
    normed_own = lax.optimization_barrier((scaled * prescale).astype(BF16))
    arrived = spread(normed_own)
    if within:
        dy_own = plane_of(after(held_dy, arrived[0])).reshape(half, width)
    normed = (normed_own,) + arrived
    normed = jnp.concatenate(normed + tuple(swap_core(piece) for piece in normed), axis=0)
    normed = lax.optimization_barrier(normed)
    dy_rows = jnp.concatenate((dy_own,) + spread(after(dy_own, arrived)), axis=0)
    output_own = gather_cols(after(rows_of(output_weight, VAL), arrived))
    expand_own = gather_rows(after(cols_of(expand_weight, part), dy_own))
    reduce_own = gather_cols(after(rows_of(reduce_weight, part), dy_rows))

    last = natural[:, rows - 1]
    ends = jnp.cumsum(spans, axis=1).reshape(form + (-1,))
    spans = spans.reshape(form + (-1,))
    starts = jnp.sum(jnp.where(ends <= stream_index[..., None], spans, 0), axis=-1)
    positions = (stream_index - starts).astype(F32)
    middle = KEY // 2
    frequency = jnp.exp(-math.log(10000.0) * jnp.arange(middle, dtype=F32) / (middle - 1))
    phases = positions[..., None] * frequency
    cosine, sine = jnp.cos(phases), jnp.sin(phases)
    head = (core * 4 + place).astype(F32)
    log_rate = jnp.log1p(-jnp.exp2(-5.0 - head))
    entry = jnp.exp((index + 1).astype(F32) * log_rate) * (
        segment == before.reshape(form)
    ).astype(F32)
    exit_weight = jnp.exp((rows - 1 - index).astype(F32) * log_rate) * (
        segment == last.reshape(form)
    ).astype(F32)
    keep = jnp.exp(rows * log_rate) * (last == before).astype(F32)
    segment, index = segment.astype(F32), index.astype(F32)
    wide_keep = jnp.broadcast_to(keep.reshape(form), segment.shape)
    columns = jnp.stack([entry, exit_weight, segment, index, wide_keep], axis=-1)
    lines = jnp.stack([segment, index], axis=0)
    if within:
        lines = lines.transpose(3, 0, 1, 2, 4)
    else:
        lines = lines.transpose(2, 0, 1, 3)
    lines = lines.reshape(4, 2, rows)
    rate = jnp.full((1, 1), log_rate)
    cosine, sine, columns, lines = lax.optimization_barrier((cosine, sine, columns, lines))

    def rows_of_width(size, dtype=BF16):
        return (segment.shape + (size,), dtype)

    def entries(size, dtype=BF16):
        return ((4, KEY, size), dtype)

    scale_own = lax.dynamic_slice_in_dim(groupscale, place * VAL, VAL, 0)[None]
    shift_own = lax.dynamic_slice_in_dim(groupshift, place * VAL, VAL, 0)[None]
    normed_slots = normed.reshape(segment.shape + (width,))
    if within:
        queries, keys, values, memory, gate, unit, group_inverse, gated = by_block(
            stream_kernel,
            (normed_slots, project, cosine, sine, columns, lines, rate, scale_own, shift_own),
            (1, 6, 7, 8),
            (
                rows_of_width(KEY),
                rows_of_width(KEY),
                rows_of_width(VAL),
                entries(VAL),
                rows_of_width(VAL, F32),
                rows_of_width(VAL, F32),
                rows_of_width(1, F32),
                rows_of_width(VAL),
            ),
            False,
        )
    else:
        key_value = project[:, KEY : 2 * KEY + VAL]
        query_gate = jnp.concatenate([project[:, :KEY], project[:, 2 * KEY + VAL :]], axis=1)
        keys, values, added = by_slot(
            key_value_kernel,
            (normed_slots, cosine, sine, columns),
            (key_value,),
            (0, 4, 1, 2, 3),
            (rows_of_width(KEY), rows_of_width(VAL), entries(VAL, F32)),
        )
        memory = carry(keep, added, True)
        queries, gate, unit, group_inverse, gated = by_slot(
            retain_kernel,
            (normed_slots, cosine, sine, columns, lines, keys, values, memory),
            (query_gate, rate, scale_own, shift_own),
            (0, 8, 1, 2, 3, 4, 9, 5, 6, 7, 10, 11),
            (
                rows_of_width(KEY),
                rows_of_width(VAL, F32),
                rows_of_width(VAL, F32),
                rows_of_width(1, F32),
                rows_of_width(VAL),
            ),
        )
    gated_own = gated[0].reshape(4 * half, VAL)
    gated_far = swap_core(gated[1].reshape(4 * half, VAL))
    gated_both = jnp.concatenate([gated_own, gated_far], axis=-1)

    output_own = after(output_own, gated_both)
    output_both = jnp.concatenate([output_own, swap_core(output_own)], axis=0)
    bias_own = lax.dynamic_slice_in_dim(hiddenbias, place * part, part, 0)
    bias_both = jnp.concatenate([bias_own, swap_core(bias_own)], axis=0)

    branch = fold(slot_products(dot, gated_both, output_both))
    residual = wide + branch
    shifted = residual - jnp.mean(residual, axis=-1, keepdims=True)
    layer_inverse = lax.rsqrt(jnp.mean(shifted * shifted, axis=-1, keepdims=True) + 1e-05)
    standard = shifted * layer_inverse
    layered_own = (standard * postscale + postshift).astype(BF16)
    layered = jnp.concatenate((layered_own,) + spread(layered_own), axis=0)
    expand_own = after(expand_own, layered_own)
    expand_both = jnp.concatenate([expand_own, swap_core(expand_own)], axis=1)
    reduce_own = after(reduce_own, expand_own)
    reduce_both = jnp.concatenate([reduce_own, swap_core(reduce_own)], axis=0)

    hidden = dot(layered, expand_both) + bias_both
    cumulative = 0.5 * (1.0 + lax.erf(hidden * 0.5**0.5))
    active = (hidden * cumulative).astype(BF16)
    def core_sum(grad, dimension):
        size = grad.shape[dimension] // 2
        own = lax.slice_in_dim(grad, 0, size, axis=dimension)
        far = lax.slice_in_dim(grad, size, 2 * size, axis=dimension)
        return own + swap_core(far.astype(BF16)).astype(F32)

    dy_wide = dy_own.astype(F32)
    outputbias_grad = jnp.sum(dy_wide, axis=0)
    reduce_grad = scatter(core_sum(contract_rows(active, dy_rows), 0), 1)
    grad_active = contract_cols(dy_rows, reduce_both)
    slope = cumulative + hidden * jnp.exp(-0.5 * hidden * hidden) * (0.5 / math.pi) ** 0.5
    grad_hidden = (grad_active * slope).astype(BF16)
    hiddenbias_grad = jnp.sum(grad_hidden.astype(F32), axis=0)
    grad_layered = fold(slot_products(contract_cols, grad_hidden, expand_both))
    expand_grad = scatter(core_sum(contract_rows(layered, grad_hidden), 1), 0)
    postscale_grad = jnp.sum(grad_layered * standard, axis=0)
    postshift_grad = jnp.sum(grad_layered, axis=0)
    grad_residual = dy_wide + normalize_back(grad_layered * postscale, standard, layer_inverse)
    grad_branch_own = grad_residual.astype(BF16)
    grad_branch = jnp.concatenate((grad_branch_own,) + spread(grad_branch_own), axis=0)

    expanded = fold(slot_products(dot, after(active, grad_branch), reduce_both))
    output_rows = (residual + expanded + outputbias).astype(BF16)
    layer_output = give_back(output_rows, BF16)

    grad_gated_both = contract_cols(grad_branch, output_both).astype(BF16)
    grad_gated_own = grad_gated_both[:, :VAL].reshape(segment.shape[1:] + (VAL,))
    grad_gated_far = swap_core(grad_gated_both[:, VAL:]).reshape(segment.shape[1:] + (VAL,))
    output_grad = core_sum(contract_rows(gated_both, grad_branch), 0)
    if within:
        grads, group_sums = by_block(
            stream_back_kernel,
            (grad_gated_own, grad_gated_far, gate, unit, group_inverse, scale_own, shift_own)
            + (columns, lines, rate, cosine, sine, queries, keys, values, memory),
            (5, 6, 9),
            (rows_of_width(2 * KEY + 2 * VAL), ((2, VAL), F32)),
            True,
            summed=1,
        )
    else:
        grad_gate, grad_retained, reach, group_sums = by_slot(
            gate_back_kernel,
            (grad_gated_own, grad_gated_far, gate, unit, group_inverse, columns, queries),
            (scale_own, shift_own),
            (0, 1, 2, 3, 4, 7, 8, 5, 6),
            (rows_of_width(VAL), rows_of_width(VAL), entries(VAL, F32), ((2, VAL), F32)),
            summed=1,
        )
        grad_memory = carry(keep, reach, False)
        grad_query_gate, grad_keys, grad_values = by_slot(
            local_back_kernel,
            (grad_retained, grad_gate, queries, keys, values, memory, columns, lines)
            + (cosine, sine),
            (rate,),
            (0, 1, 2, 3, 4, 5, 6, 7, 10, 8, 9),
            (rows_of_width(KEY + VAL), rows_of_width(KEY, F32), rows_of_width(VAL, F32)),
        )
        (grad_key_value,) = by_slot(
            state_back_kernel,
            (grad_keys, grad_values, keys, values, grad_memory, columns, cosine, sine),
            (),
            range(8),
            (rows_of_width(KEY + VAL),),
        )
        grads = jnp.concatenate(
            [grad_query_gate[..., :KEY], grad_key_value, grad_query_gate[..., KEY:]], axis=-1
        )
    groupscale_grad, groupshift_grad = group_sums[0], group_sums[1]
    grads = grads.reshape(4 * rows, 2 * KEY + 2 * VAL)
    gate_grad = contract_rows(normed, grads[:, 2 * KEY + VAL :]).astype(BF16)
    first_grad = contract_rows(normed, grads[:, : 2 * KEY + VAL]).astype(BF16)
    grads = after(grads, gate_grad, first_grad)
    far_terms = contract_cols(grads[4 * half :], project).astype(BF16)
    far_terms = swap_core(far_terms).astype(F32)
    far_corner = contract_cols(grads[3 * half : 4 * half], project) + far_terms[3 * half :]
    own_terms = contract_cols(grads[: 3 * half], project) + far_terms[: 3 * half]
    own_terms = [own_terms[slot * half : (slot + 1) * half] for slot in range(3)]
    grad_normed = fold(own_terms + [far_corner.astype(BF16)])
    output_grad = scatter(output_grad, 1)
    gate_grad = scatter(gate_grad, 0)
    first_grad = scatter(first_grad, 0)
    prescale_grad = jnp.sum(grad_normed * scaled, axis=0)
    grad_scaled = grad_normed * prescale
    grad_rows = grad_residual + inverse * (
        grad_scaled - scaled * jnp.mean(grad_scaled * scaled, axis=-1, keepdims=True)
    )
    tokens_grad = give_back(grad_rows.astype(BF16) if within else grad_rows, F32)

    by_width = [prescale_grad, postscale_grad, postshift_grad, outputbias_grad]
    over_cores = swap_core(jnp.concatenate([hiddenbias_grad[part:]] + by_width))
    over_cores = over_cores + jnp.concatenate([hiddenbias_grad[:part]] + by_width)
    spaced = [
        lax.dynamic_update_slice(jnp.zeros((4 * part,), F32), piece, (place * part,))
        for piece in (over_cores[:part], groupscale_grad, groupshift_grad)
    ]
    sums = total(jnp.concatenate([over_cores[part:]] + spaced))
    cuts = [width * at for at in range(1, 5)] + [4 * width + 4 * part, 4 * width + 8 * part]
    prescale_sum, postscale_sum, postshift_sum, outputbias_sum, hiddenbias_sum, scale_sum, shift_sum = (
        jnp.split(sums, cuts)
    )

    def all_pieces(grad):
        return (grad,) + spread(grad)

    reduce_pieces = all_pieces(reduce_grad)
    expand_pieces = all_pieces(expand_grad)
    output_pieces = all_pieces(output_grad)
    gate_pieces = all_pieces(gate_grad)
    first_pieces = all_pieces(first_grad)
    return (
        layer_output[None],
        tokens_grad[None],
        prescale_sum,
        place_columns([piece[:, :KEY] for piece in first_pieces], place, KEY),
        place_columns([piece[:, KEY : 2 * KEY] for piece in first_pieces], place, KEY),
        place_columns([piece[:, 2 * KEY :] for piece in first_pieces], place, VAL),
        place_columns(gate_pieces, place, VAL),
        scale_sum,
        shift_sum,
        place_rows(output_pieces, place, VAL),
        postscale_sum,
        postshift_sum,
        place_columns(expand_pieces, place, part),
        hiddenbias_sum,
        place_rows(reduce_pieces, place, part),
        outputbias_sum,
    )


def solution(mesh):
    in_specs = (
        P("batch", "seq", None),
        P(),
        P("seq", "head"),
        P("seq", "head"),
        P("seq", "head"),
        P("seq", "head"),
        P("head"),
        P("head"),
        P("head", "seq"),
        P(),
        P(),
        P("seq", "head"),
        P("head"),
        P("head", "seq"),
        P(),
        P("batch", "seq", None),
        P("batch", None),
        P("batch", "seq"),
    )
    out_specs = (
        P("batch", "seq", None),
        P("batch", "seq", None),
        P(),
        P("seq", "head"),
        P("seq", "head"),
        P("seq", "head"),
        P("seq", "head"),
        P("head"),
        P("head"),
        P("head", "seq"),
        P(),
        P(),
        P("seq", "head"),
        P("head"),
        P("head", "seq"),
        P(),
    )
    return jax.shard_map(body, mesh=mesh, in_specs=in_specs, out_specs=out_specs, check_vma=False)
```

time: 961 us -> 824 us (0.86)
  waiting for transfers between devices: 488 us -> 348 us
  other arithmetic: 119 us -> 73.8 us
  Pallas kernels: 0 us -> 43 us
  matrix products: 153 us -> 111 us
  starting transfers between devices: 93.2 us -> 119 us
  local copies, waits for them, and re-layouts: 80.1 us -> 104 us
    ppermute x13 -> x12, waiting for transfers between devices: 151 us -> 93.2 us  [turn(): lax.ppermute(value, 'seq', [(source, (source + steps) % count) for source...]
    all_gather x3 -> x2, waiting for transfers between devices: 55.3 us -> 6.4 us  [gather_rows(): return lax.all_gather(weight, 'seq', axis=0, tiled=True)]
    pallas_call x0 -> x2, Pallas kernels: none -> 43 us  [by_block(): pl.pallas_call(kernel, grid=(4,), in_specs=[block_spec(v, at in shared, l...]
    ppermute x54 -> x61, waiting for transfers between devices: 250 us -> 223 us  [swap_batch(): lax.ppermute(value, 'batch', [(place, place ^ mask) for place in range(4)])]
    dot_general x12 -> x0, matrix products: 22.9 us -> none  [batched(): return jnp.einsum(subscripts, left, right, preferred_element_type=F32)]
    reduce_sum x6 -> x2, other arithmetic: 20.1 us -> 0.42 us  [the longest x1 0.29 us: body(): inverse = lax.rsqrt(jnp.mean(wide * wide, axis=-1, keepdims=True) + 1e-06)]
    dot_general x5 -> x7, matrix products: 38.2 us -> 21.4 us  [dot(): return jnp.dot(left, right, preferred_element_type=F32)]
    unnamed x209 -> x142, local copies, waits for them, and re-layouts: 28.4 us -> 44.8 us
  transfers between devices with their start and end apart: 102 -> 103, of which waited for: 44 -> 50; matrix products, arithmetic and copies ran while one was open for 34% -> 32% of each run, Pallas kernels for 0% -> 5%
where the time goes in v2:
time: 824 us; the launch traced here: 814 us
  waiting for transfers between devices  348 us (42%)
  starting transfers between devices  119 us (14%)
  matrix products  111 us (13%)
  local copies, waits for them, and re-layouts  104 us (13%)
  other arithmetic  73.8 us (9%)
  Pallas kernels  43 us (5%)
  between operations  15.9 us (2%)
    ppermute x61, waiting for transfers between devices, swap_batch(): lax.ppermute(value, 'batch', [(place, place ^ mask) for place in range(4)])  223 us
    ppermute x12, waiting for transfers between devices, turn(): lax.ppermute(value, 'seq', [(source, (source + steps) % count) for source...  93.2 us
    ppermute x61, starting transfers between devices, swap_batch(): lax.ppermute(value, 'batch', [(place, place ^ mask) for place in range(4)])  67.8 us
    dot_general x8, matrix products, contract_cols(): lax.dot_general(left, right, (((1,), (1,)), ((), ())), preferred_element_...  45.5 us
    unnamed x142, local copies, waits for them, and re-layouts  44.8 us
    dot_general x5, matrix products, contract_rows(): lax.dot_general(left, right, (((0,), (0,)), ((), ())), preferred_element_...  44 us
    pallas_call x2, Pallas kernels, by_block(): pl.pallas_call(kernel, grid=(4,), in_specs=[block_spec(v, at in shared, l...  43 us
    ppermute x12, starting transfers between devices, turn(): lax.ppermute(value, 'seq', [(source, (source + steps) % count) for source...  34.5 us
  transfers between devices with their start and end apart: 103, of which 50 were waited for; matrix products, arithmetic and copies ran while one was open for 32% of the time, Pallas kernels for 5%

profile of v2, /device:TPU:0, one launch (start us, length us, event | category | flops | bytes accessed | tf_op | source)
XLA Modules:
  0.0 814.1 jit_solution(8584454104313095850)
XLA Ops:
  15.0 3.9 collective-permute-start.2
  23.7 9.0 %collective-permute-done.2 = bf16[136,2048]{1,0:T(8,128)(2,1)S(1)} collective-permute-done((bf16[136,2048]{1,0:T(8,128)(2,1)}, bf16[136,2048]{1,0:T(8,128)(2,1)S(1)}, u32[]{:S(2)}, u32[]{:S(2)}) %collective-permute-start.2) | collective-permute-done | bytes 557088 | tf_op jit(solution)/shard_map/ppermute | solution.py:21
  32.6 11.2 %collective-permute-done.1 = bf16[136,2048]{1,0:T(8,128)(2,1)} collective-permute-done((bf16[136,2048]{1,0:T(8,128)(2,1)}, bf16[136,2048]{1,0:T(8,128)(2,1)}, u32[]{:S(2)}, u32[]{:S(2)}) %collective-permute-start.1) | collective-permute-done | bytes 557088 | tf_op jit(solution)/shard_map/ppermute | solution.py:21
  51.6 12.4 %collective-permute-done.3 = bf16[1,72,2048]{2,1,0:T(8,128)(2,1)S(1)} collective-permute-done((bf16[1,72,2048]{2,1,0:T(8,128)(2,1)S(1)}, bf16[1,72,2048]{2,1,0:T(8,128)(2,1)S(1)}, u32[]{:S(2)}, u32[]{:S(2)}) %collective-permute-start.3) | collective-permute-done | bytes 294944 | tf_op jit(solution)/shard_map/ppermute | solution.py:66
  64.0 21.0 %collective-permute-done.4 = bf16[1,72,2048]{2,1,0:T(8,128)(2,1)S(1)} collective-permute-done((bf16[1,72,2048]{2,1,0:T(8,128)(2,1)S(1)}, bf16[1,72,2048]{2,1,0:T(8,128)(2,1)S(1)}, u32[]{:S(2)}, u32[]{:S(2)}) %collective-permute-start.4) | collective-permute-done | bytes 294944 | tf_op jit(solution)/shard_map/ppermute | solution.py:66
  94.1 18.3 %collective-permute-done.6 = bf16[256,2048]{1,0:T(8,128)(2,1)} collective-permute-done((bf16[256,2048]{1,0:T(8,128)(2,1)}, bf16[256,2048]{1,0:T(8,128)(2,1)}, u32[]{:S(2)}, u32[]{:S(2)}) %collective-permute-start.6) | collective-permute-done | bytes 1048608 | tf_op jit(solution)/shard_map/ppermute | solution.py:21
  121.2 4.3 collective-permute-done.8
  131.6 5.5 multiply_sine_fusion
  147.9 6.4 all-gather.5.cloned.1.call-done.weight
  154.3 24.4 %shard_map.297 = (bf16[2,4,4,64,256]{4,3,2,1,0:T(8,128)(2,1)}, bf16[2,4,4,64,256]{4,3,2,1,0:T(8,128)(2,1)}, bf16[2,4,4,64,512]{4,3,2,1,0:T(8,128)(2,1)}, bf16[4,...) custom-call(bf16[2,4,4,64,2048]{4,3,2,1,0:T(8,128)(2,1)} %bitcast.13, ...), custom_call_target="tpu_custom_call" | custom-call | tf_op jit(solution)/shard_map/pallas_call | solution.py:326
  182.8 12.7 %collective-permute-start.24 = (bf16[1,64,2048]{2,1,0:T(8,128)(2,1)S(1)}, bf16[1,64,2048]{2,1,0:T(8,128)(2,1)S(1)}, u32[]{:S(2)}, u32[]{:S(2)}) collective-permute-start(bf16[1,64,2048]{2,1,0:T(8,128)(2,1)S(1)} %get-tuple-element.162), channel_id=1, source_target_pairs={{0,8},{8,16},{16,24},{24,0},{1,9},{9,17},{17,25},{25,1},{2,10},{10... | collective-permute-start | bytes 786440 | tf_op jit(solution)/shard_map/ppermute | solution.py:66
  195.5 7.3 collective-permute-start.25
  202.9 6.7 collective-permute-done.24
  212.1 8.2 %collective-permute-done.25 = bf16[1,64,2048]{2,1,0:T(8,128)(2,1)S(1)} collective-permute-done((bf16[1,64,2048]{2,1,0:T(8,128)(2,1)}, bf16[1,64,2048]{2,1,0:T(8,128)(2,1)S(1)}, u32[]{:S(2)}, u32[]{:S(2)}) %collective-permute-start.25) | collective-permute-done | bytes 262176 | tf_op jit(solution)/shard_map/ppermute | solution.py:66
  226.0 10.4 %all-gather.11.cloned.1.call-start = ((), (), s32[]{:S(2)}) async-start(), calls=%async_computation.8 | async-start | bytes 2621440 | tf_op jit(solution)/shard_map/all_gather | solution.py:466
  237.4 8.2 %collective-permute-done.29 = bf16[256,2048]{1,0:T(8,128)(2,1)} collective-permute-done((bf16[256,2048]{1,0:T(8,128)(2,1)S(1)}, bf16[256,2048]{1,0:T(8,128)(2,1)}, u32[]{:S(2)}, u32[]{:S(2)}) %collective-permute-start.29) | collective-permute-done | bytes 1048608 | tf_op jit(solution)/shard_map/ppermute | solution.py:21
  262.7 8.2 %collective-permute-done.16 = bf16[128,2048]{1,0:T(8,128)(2,1)S(1)} collective-permute-done((bf16[128,2048]{1,0:T(8,128)(2,1)S(1)}, bf16[128,2048]{1,0:T(8,128)(2,1)S(1)}, u32[]{:S(2)}, u32[]{:S(2)}) %collective-permute-start.16) | collective-permute-done | bytes 524320 | tf_op jit(solution)/shard_map/ppermute | solution.py:21
  278.6 19.2 %collective-permute-done.19 = bf16[256,2048]{1,0:T(8,128)(2,1)} collective-permute-done((bf16[256,2048]{1,0:T(8,128)(2,1)}, bf16[256,2048]{1,0:T(8,128)(2,1)}, u32[]{:S(2)}, u32[]{:S(2)}) %collective-permute-start.19) | collective-permute-done | bytes 1048608 | tf_op jit(solution)/shard_map/ppermute | solution.py:21
  299.8 4.7 fusion.91
  311.5 15.9 %all-gather.11.cloned.1.call-done = bf16[512,2048]{1,0:T(8,128)(2,1)} async-done(((bf16[512,512]{1,0:T(8,128)(2,1)}), bf16[512,2048]{1,0:T(8,128)(2,1)}) %all-gather.11.cloned.1.call-update) | async-done | bytes 2097168 | tf_op jit(solution)/shard_map/all_gather | solution.py:466
  338.4 6.0 collective-permute-done.22
  349.8 6.1 multiply_convert_fusion
  356.1 9.5 %convert_reduce_fusion = (f32[1024]{0:T(1024)S(1)}, bf16[1024,1024]{1,0:T(8,128)(2,1)S(1)}) fusion(f32[1024,1024]{1,0:T(8,128)S(1)} %get-tuple-element.212, f32[1024]{0:T(1024)S(1)} %pad_maximum_fusion.19, bf16[1024,2048]{1,0:T(8,128)(2,1)} %constant_dynamic-update-slice_fusion.25, bf16[1024,2048]{1,0:T(8,128)(2,1)S(1)} %constant_dynamic-update-slice_fusion.30), kind=kOutput, calls=%fused_computation.20 | convolution fusion | flops 4308597760 | bytes 14688256 | tf_op jit(solution)/shard_map/dot_general | solution.py:99
  367.0 4.6 fusion.95
  376.8 7.7 collective-permute-done.34
  392.4 7.5 fusion.96
  400.4 9.4 %collective-permute-done.37 = bf16[256,2048]{1,0:T(8,128)(2,1)} collective-permute-done((bf16[256,2048]{1,0:T(8,128)(2,1)}, bf16[256,2048]{1,0:T(8,128)(2,1)}, u32[]{:S(2)}, u32[]{:S(2)}) %collective-permute-start.37) | collective-permute-done | bytes 1048608 | tf_op jit(solution)/shard_map/ppermute | solution.py:21
  411.4 3.9 multiply_reduce_fusion
  420.2 19.5 %collective-permute-done.38 = bf16[256,2048]{1,0:T(8,128)(2,1)S(1)} collective-permute-done((bf16[256,2048]{1,0:T(8,128)(2,1)}, bf16[256,2048]{1,0:T(8,128)(2,1)S(1)}, u32[]{:S(2)}, u32[]{:S(2)}) %collective-permute-start.38) | collective-permute-done | bytes 1048608 | tf_op jit(solution)/shard_map/ppermute | solution.py:21
  460.4 4.9 convolution_convert_fusion.5
  472.2 18.6 %shard_map.298 = (bf16[2,4,4,64,1536]{4,3,2,1,0:T(8,128)(2,1)}, f32[2,512]{1,0:T(2,128)}) custom-call(bf16[4,4,64,512]{3,2,1,0:T(8,128)(2,1)} %bitcast.115, bf16[4,4,64,512]{3,2,1,0:T(8,128)(2,1)} %bitcast.120, f32[2,4,4,64,512]{4,3,2,1,0:T(8,128)} %get-tuple-element.74.gate, f32[2,4,4,64,512]{4,3,2,1,0:T(8,128)} %get-tuple-element.75.unit, ...), custom_call_target="tpu_custom_call" | custom-call | tf_op jit(solution)/shard_map/pallas_call | solution.py:326
  490.8 10.0 %convolution_convert_fusion.1 = bf16[2048,512]{1,0:T(8,128)(2,1)} fusion(bf16[2048,2048]{1,0:T(8,128)(2,1)} %constant_dynamic-update-slice_fusion.2, bf16[2048,1536]{1,0:T(8,128)(2,1)} %bitcast.143), kind=kOutput, calls=%fused_computation.26 | convolution fusion | flops 4296015872 | bytes 12582912 | tf_op jit(solution)/shard_map/dot_general | solution.py:95
  507.4 7.5 fusion.75
  515.3 13.8 %collective-permute-done.45 = bf16[256,2048]{1,0:T(8,128)(2,1)} collective-permute-done((bf16[256,2048]{1,0:T(8,128)(2,1)}, bf16[256,2048]{1,0:T(8,128)(2,1)}, u32[]{:S(2)}, u32[]{:S(2)}) %collective-permute-start.45) | collective-permute-done | bytes 1048608 | tf_op jit(solution)/shard_map/ppermute | solution.py:21
  535.2 3.8 collective-permute-start.46
  541.5 8.5 %collective-permute-done.46 = bf16[1,64,2048]{2,1,0:T(8,128)(2,1)S(1)} collective-permute-done((bf16[1,64,2048]{2,1,0:T(8,128)(2,1)S(1)}, bf16[1,64,2048]{2,1,0:T(8,128)(2,1)S(1)}, u32[]{:S(2)}, u32[]{:S(2)}) %collective-permute-start.46) | collective-permute-done | bytes 262176 | tf_op jit(solution)/shard_map/ppermute | solution.py:66
  550.1 17.8 %collective-permute-done.47 = bf16[1,64,2048]{2,1,0:T(8,128)(2,1)S(1)} collective-permute-done((bf16[1,64,2048]{2,1,0:T(8,128)(2,1)S(1)}, bf16[1,64,2048]{2,1,0:T(8,128)(2,1)S(1)}, u32[]{:S(2)}, u32[]{:S(2)}) %collective-permute-start.47) | collective-permute-done | bytes 262176 | tf_op jit(solution)/shard_map/ppermute | solution.py:66
  575.3 14.4 %fusion.11 = bf16[2048,1024]{1,0:T(8,128)(2,1)} fusion(bf16[2048,2048]{1,0:T(8,128)(2,1)} %constant_dynamic-update-slice_fusion.2, bf16[2048,1536]{1,0:T(8,128)(2,1)} %bitcast.144), kind=kOutput, calls=%fused_computation.24 | convolution fusion | flops 8592031744 | bytes 16777216 | tf_op jit(solution)/shard_map/dot_general | solution.py:95
  590.8 11.1 %convolution_convert_fusion = bf16[1024,2048]{1,0:T(8,128)(2,1)} fusion(bf16[2048,1536]{1,0:T(8,128)(2,1)} %all-gather.5.cloned.1.call-done.weight, bf16[2048,1536]{1,0:T(8,128)(2,1)} %bitcast.145), kind=kOutput, calls=%fused_computation.23 | convolution fusion | flops 6444548096 | bytes 13631488 | tf_op jit(solution)/shard_map/dot_general | solution.py:99
  612.8 6.9 collective-permute-done.86
  621.8 9.1 %collective-permute-done.91 = bf16[512,512]{1,0:T(8,128)(2,1)S(1)} collective-permute-done((bf16[512,512]{1,0:T(8,128)(2,1)S(1)}, bf16[512,512]{1,0:T(8,128)(2,1)S(1)}, u32[]{:S(2)}, u32[]{:S(2)}) %collective-permute-start.91) | collective-permute-done | bytes 524320 | tf_op jit(solution)/shard_map/ppermute | solution.py:21
  638.8 3.9 convert_element_type.356
  647.7 9.3 %fusion.94 = (bf16[768,2048]{1,0:T(8,128)(2,1)}, f32[768,2048]{1,0:T(8,128)}) fusion(f32[1024,2048]{1,0:T(8,128)S(1)} %convert_element_type.356, bf16[2048,1536]{1,0:T(8,128)(2,1)S(1)} %bitcast.114, bf16[2048,1536]{1,0:T(8,128)(2,1)} %bitcast.147), kind=kOutput, calls=%fused_computation.345 | convolution fusion | flops 4834983936 | bytes 24379392 | tf_op jit(solution)/shard_map/dot_general | solution.py:99
  678.7 20.1 %collective-permute-done.78 = bf16[256,512]{1,0:T(8,128)(2,1)S(1)} collective-permute-done((bf16[256,512]{1,0:T(8,128)(2,1)S(1)}, bf16[256,512]{1,0:T(8,128)(2,1)S(1)}, u32[]{:S(2)}, u32[]{:S(2)}) %collective-permute-start.78) | collective-permute-done | bytes 262176 | tf_op jit(solution)/shard_map/ppermute | solution.py:21
  705.2 3.5 add_convert_fusion
  718.6 17.5 %collective-permute-done.60 = bf16[1,64,2048]{2,1,0:T(8,128)(2,1)S(1)} collective-permute-done((bf16[1,64,2048]{2,1,0:T(8,128)(2,1)S(1)}, bf16[1,64,2048]{2,1,0:T(8,128)(2,1)S(1)}, u32[]{:S(2)}, u32[]{:S(2)}) %collective-permute-start.60) | collective-permute-done | bytes 262176 | tf_op jit(solution)/shard_map/ppermute | solution.py:66
  774.9 17.3 %collective-permute-done.71 = bf16[512,1024]{1,0:T(8,128)(2,1)S(1)} collective-permute-done((bf16[512,1024]{1,0:T(8,128)(2,1)}, bf16[512,1024]{1,0:T(8,128)(2,1)S(1)}, u32[]{:S(2)}, u32[]{:S(2)}) %collective-permute-start.71) | collective-permute-done | bytes 1048608 | tf_op jit(solution)/shard_map/ppermute | solution.py:21
  796.6 7.2 collective-permute-done.73
  (554 shorter events, 301.0 us)
Async XLA Ops:
  7.2 147.0 %all-gather.5.cloned.1.call-start = ((), (), s32[]{:S(2)}) async-start(), calls=%async_computation.5 | async-start | bytes 7864320 | tf_op jit(solution)/shard_map/all_gather | solution.py:463
  11.0 201.1 %all-gather.7.cloned.1.call-start = ((), (), s32[]{:S(2)}) async-start(), calls=%async_computation.6 | async-start | bytes 2621440 | tf_op jit(solution)/shard_map/all_gather | solution.py:466
  18.9 24.9 %collective-permute-start.1 = (bf16[136,2048]{1,0:T(8,128)(2,1)}, bf16[136,2048]{1,0:T(8,128)(2,1)}, u32[]{:S(2)}, u32[]{:S(2)}) collective-permute-start(bf16[136,2048]{1,0:T(8,128)(2,1)} %get-tuple-element.181), channel_id=1, source_target_pairs={{0,4},{2,6},{4,0},{6,2},{1,5},{3,7},{5,1},{7,3},{8,12},{10,14},{12... | collective-permute-start | bytes 1671176 | tf_op jit(solution)/shard_map/ppermute | solution.py:21
  19.4 24.7 %collective-permute-start = (bf16[136,2048]{1,0:T(8,128)(2,1)}, bf16[136,2048]{1,0:T(8,128)(2,1)}, u32[]{:S(2)}, u32[]{:S(2)}) collective-permute-start(bf16[136,2048]{1,0:T(8,128)(2,1)} %get-tuple-element.180), channel_id=1, source_target_pairs={{0,2},{2,0},{4,6},{6,4},{1,3},{3,1},{5,7},{7,5},{8,10},{10,8},{12,... | collective-permute-start | bytes 1671176 | tf_op jit(solution)/shard_map/ppermute | solution.py:21
  47.6 37.4 %collective-permute-start.4 = (bf16[1,72,2048]{2,1,0:T(8,128)(2,1)S(1)}, bf16[1,72,2048]{2,1,0:T(8,128)(2,1)S(1)}, u32[]{:S(2)}, u32[]{:S(2)}) collective-permute-start(bf16[1,72,2048]{2,1,0:T(8,128)(2,1)S(1)} %get-tuple-element.129), channel_id=1, source_target_pairs={{0,16},{8,24},{16,0},{24,8},{1,17},{9,25},{17,1},{25,9},{2,18},{10... | collective-permute-start | bytes 884744 | tf_op jit(solution)/shard_map/ppermute | solution.py:66
  50.2 36.0 %collective-permute-start.5 = (bf16[1,72,2048]{2,1,0:T(8,128)(2,1)S(1)}, bf16[1,72,2048]{2,1,0:T(8,128)(2,1)S(1)}, u32[]{:S(2)}, u32[]{:S(2)}) collective-permute-start(bf16[1,72,2048]{2,1,0:T(8,128)(2,1)S(1)} %get-tuple-element.128), channel_id=1, source_target_pairs={{0,24},{8,0},{16,8},{24,16},{1,25},{9,1},{17,9},{25,17},{2,26},{10... | collective-permute-start | bytes 884744 | tf_op jit(solution)/shard_map/ppermute | solution.py:66
  88.0 24.5 %collective-permute-start.6 = (bf16[256,2048]{1,0:T(8,128)(2,1)}, bf16[256,2048]{1,0:T(8,128)(2,1)}, u32[]{:S(2)}, u32[]{:S(2)}) collective-permute-start(bf16[256,2048]{1,0:T(8,128)(2,1)} %multiply_convert_fusion.1), channel_id=1, source_target_pairs={{0,2},{2,0},{4,6},{6,4},{1,3},{3,1},{5,7},{7,5},{8,10},{10,8},{12,... | collective-permute-start | bytes 3145736 | tf_op jit(solution)/shard_map/ppermute | solution.py:21
  89.4 25.7 %collective-permute-start.7 = (bf16[256,2048]{1,0:T(8,128)(2,1)}, bf16[256,2048]{1,0:T(8,128)(2,1)}, u32[]{:S(2)}, u32[]{:S(2)}) collective-permute-start(bf16[256,2048]{1,0:T(8,128)(2,1)} %multiply_convert_fusion.1), channel_id=1, source_target_pairs={{0,4},{2,6},{4,0},{6,2},{1,5},{3,7},{5,1},{7,3},{8,12},{10,14},{12... | collective-permute-start | bytes 3145736 | tf_op jit(solution)/shard_map/ppermute | solution.py:21
  90.0 48.6 %collective-permute-start.10 = (bf16[256,2048]{1,0:T(8,128)(2,1)}, bf16[256,2048]{1,0:T(8,128)(2,1)}, u32[]{:S(2)}, u32[]{:S(2)}) collective-permute-start(bf16[256,2048]{1,0:T(8,128)(2,1)} %multiply_convert_fusion.1), channel_id=1, source_target_pairs={{0,1},{1,0},{2,3},{3,2},{4,5},{5,4},{6,7},{7,6},{8,9},{9,8},{10,11... | collective-permute-start | bytes 3145736 | tf_op jit(solution)/shard_map/ppermute | solution.py:17
  116.6 24.3 %collective-permute-start.11 = (bf16[256,2048]{1,0:T(8,128)(2,1)}, bf16[256,2048]{1,0:T(8,128)(2,1)}, u32[]{:S(2)}, u32[]{:S(2)}) collective-permute-start(bf16[256,2048]{1,0:T(8,128)(2,1)} %collective-permute-done.6), channel_id=1, source_target_pairs={{0,1},{1,0},{2,3},{3,2},{4,5},{5,4},{6,7},{7,6},{8,9},{9,8},{10,11... | collective-permute-start | bytes 3145736 | tf_op jit(solution)/shard_map/ppermute | solution.py:17
  130.0 177.3 %all-gather.9.cloned.1.call-start = ((), (), s32[]{:S(2)}) async-start(), calls=%async_computation.7 | async-start | bytes 2621440 | tf_op jit(solution)/shard_map/all_gather | solution.py:463
  180.4 29.2 %collective-permute-start.14 = (bf16[1024,512]{1,0:T(8,128)(2,1)S(1)}, bf16[1024,512]{1,0:T(8,128)(2,1)S(1)}, u32[]{:S(2)}, u32[]{:S(2)}) collective-permute-start(bf16[1024,512]{1,0:T(8,128)(2,1)S(1)} %bitcast.122), channel_id=1, source_target_pairs={{0,1},{1,0},{2,3},{3,2},{4,5},{5,4},{6,7},{7,6},{8,9},{9,8},{10,11... | collective-permute-start | bytes 3145736 | tf_op jit(solution)/shard_map/ppermute | solution.py:17
  182.8 26.7 %collective-permute-start.24 = (bf16[1,64,2048]{2,1,0:T(8,128)(2,1)S(1)}, bf16[1,64,2048]{2,1,0:T(8,128)(2,1)S(1)}, u32[]{:S(2)}, u32[]{:S(2)}) collective-permute-start(bf16[1,64,2048]{2,1,0:T(8,128)(2,1)S(1)} %get-tuple-element.162), channel_id=1, source_target_pairs={{0,8},{8,16},{16,24},{24,0},{1,9},{9,17},{17,25},{25,1},{2,10},{10... | collective-permute-start | bytes 786440 | tf_op jit(solution)/shard_map/ppermute | solution.py:66
  195.5 24.8 %collective-permute-start.25 = (bf16[1,64,2048]{2,1,0:T(8,128)(2,1)}, bf16[1,64,2048]{2,1,0:T(8,128)(2,1)S(1)}, u32[]{:S(2)}, u32[]{:S(2)}) collective-permute-start(bf16[1,64,2048]{2,1,0:T(8,128)(2,1)} %get-tuple-element.161), channel_id=1, source_target_pairs={{0,16},{8,24},{16,0},{24,8},{1,17},{9,25},{17,1},{25,9},{2,18},{10... | collective-permute-start | bytes 786440 | tf_op jit(solution)/shard_map/ppermute | solution.py:66
  212.1 42.4 %collective-permute-start.15 = (bf16[512,2048]{1,0:T(8,128)(2,1)}, bf16[512,2048]{1,0:T(8,128)(2,1)}, u32[]{:S(2)}, u32[]{:S(2)}) collective-permute-start(bf16[512,2048]{1,0:T(8,128)(2,1)} %all-gather.7.cloned.1.call-done), channel_id=1, source_target_pairs={{0,1},{1,0},{2,3},{3,2},{4,5},{5,4},{6,7},{7,6},{8,9},{9,8},{10,11... | collective-permute-start | bytes 6291464 | tf_op jit(solution)/shard_map/ppermute | solution.py:17
  220.4 25.2 %collective-permute-start.29 = (bf16[256,2048]{1,0:T(8,128)(2,1)S(1)}, bf16[256,2048]{1,0:T(8,128)(2,1)}, u32[]{:S(2)}, u32[]{:S(2)}) collective-permute-start(bf16[256,2048]{1,0:T(8,128)(2,1)S(1)} %bitcast.106), channel_id=1, source_target_pairs={{0,2},{2,0},{4,6},{6,4},{1,3},{3,1},{5,7},{7,5},{8,10},{10,8},{12,... | collective-permute-start | bytes 3145736 | tf_op jit(solution)/shard_map/ppermute | solution.py:21
  220.6 26.4 %collective-permute-start.30 = (bf16[256,2048]{1,0:T(8,128)(2,1)S(1)}, bf16[256,2048]{1,0:T(8,128)(2,1)}, u32[]{:S(2)}, u32[]{:S(2)}) collective-permute-start(bf16[256,2048]{1,0:T(8,128)(2,1)S(1)} %bitcast.107), channel_id=1, source_target_pairs={{0,4},{2,6},{4,0},{6,2},{1,5},{3,7},{5,1},{7,3},{8,12},{10,14},{12... | collective-permute-start | bytes 3145736 | tf_op jit(solution)/shard_map/ppermute | solution.py:21
  226.0 101.4 %all-gather.11.cloned.1.call-start = ((), (), s32[]{:S(2)}) async-start(), calls=%async_computation.8 | async-start | bytes 2621440 | tf_op jit(solution)/shard_map/all_gather | solution.py:466
  246.7 29.9 %collective-permute-start.31 = (bf16[128,2048]{1,0:T(8,128)(2,1)S(1)}, bf16[128,2048]{1,0:T(8,128)(2,1)S(1)}, u32[]{:S(2)}, u32[]{:S(2)}) collective-permute-start(bf16[128,2048]{1,0:T(8,128)(2,1)S(1)} %slice.477), channel_id=1, source_target_pairs={{0,4},{2,6},{4,0},{6,2},{1,5},{3,7},{5,1},{7,3},{8,12},{10,14},{12... | collective-permute-start | bytes 1572872 | tf_op jit(solution)/shard_map/ppermute | solution.py:21
  248.1 29.3 %collective-permute-start.32 = (bf16[128,2048]{1,0:T(8,128)(2,1)S(1)}, bf16[128,2048]{1,0:T(8,128)(2,1)S(1)}, u32[]{:S(2)}, u32[]{:S(2)}) collective-permute-start(bf16[128,2048]{1,0:T(8,128)(2,1)S(1)} %slice.478), channel_id=1, source_target_pairs={{0,2},{2,0},{4,6},{6,4},{1,3},{3,1},{5,7},{7,5},{8,10},{10,8},{12,... | collective-permute-start | bytes 1572872 | tf_op jit(solution)/shard_map/ppermute | solution.py:21
  273.4 24.3 %collective-permute-start.19 = (bf16[256,2048]{1,0:T(8,128)(2,1)}, bf16[256,2048]{1,0:T(8,128)(2,1)}, u32[]{:S(2)}, u32[]{:S(2)}) collective-permute-start(bf16[256,2048]{1,0:T(8,128)(2,1)} %pad_maximum_fusion.9), channel_id=1, source_target_pairs={{0,4},{2,6},{4,0},{6,2},{1,5},{3,7},{5,1},{7,3},{8,12},{10,14},{12... | collective-permute-start | bytes 3145736 | tf_op jit(solution)/shard_map/ppermute | solution.py:21
  276.2 23.6 %collective-permute-start.17 = (bf16[256,2048]{1,0:T(8,128)(2,1)}, bf16[256,2048]{1,0:T(8,128)(2,1)}, u32[]{:S(2)}, u32[]{:S(2)}) collective-permute-start(bf16[256,2048]{1,0:T(8,128)(2,1)} %pad_maximum_fusion.8), channel_id=1, source_target_pairs={{0,2},{2,0},{4,6},{6,4},{1,3},{3,1},{5,7},{7,5},{8,10},{10,8},{12,... | collective-permute-start | bytes 3145736 | tf_op jit(solution)/shard_map/ppermute | solution.py:21
  278.3 324.9 %reduce-scatter.12.cloned.1.call-start = ((), (), s32[]{:S(2)}) async-start(), calls=%async_computation.12 | async-start | bytes 2621440 | tf_op jit(solution)/shard_map/reduce_scatter | solution.py:469
  307.3 40.6 %collective-permute-start.27 = (bf16[2048,512]{1,0:T(8,128)(2,1)}, bf16[2048,512]{1,0:T(8,128)(2,1)}, u32[]{:S(2)}, u32[]{:S(2)}) collective-permute-start(bf16[2048,512]{1,0:T(8,128)(2,1)} %all-gather.9.cloned.1.call-done), channel_id=1, source_target_pairs={{0,1},{1,0},{2,3},{3,2},{4,5},{5,4},{6,7},{7,6},{8,9},{9,8},{10,11... | collective-permute-start | bytes 6291464 | tf_op jit(solution)/shard_map/ppermute | solution.py:17
  307.3 25.9 %collective-permute-start.21 = (bf16[256,2048]{1,0:T(8,128)(2,1)}, bf16[256,2048]{1,0:T(8,128)(2,1)}, u32[]{:S(2)}, u32[]{:S(2)}) collective-permute-start(bf16[256,2048]{1,0:T(8,128)(2,1)} %get-tuple-element.97), channel_id=1, source_target_pairs={{0,4},{2,6},{4,0},{6,2},{1,5},{3,7},{5,1},{7,3},{8,12},{10,14},{12... | collective-permute-start | bytes 3145736 | tf_op jit(solution)/shard_map/ppermute | solution.py:21
  332.4 23.6 %collective-permute-start.33 = (bf16[512,2048]{1,0:T(8,128)(2,1)S(1)}, bf16[512,2048]{1,0:T(8,128)(2,1)S(1)}, u32[]{:S(2)}, u32[]{:S(2)}) collective-permute-start(bf16[512,2048]{1,0:T(8,128)(2,1)S(1)} %copy-done.21), channel_id=1, source_target_pairs={{0,1},{1,0},{2,3},{3,2},{4,5},{5,4},{6,7},{7,6},{8,9},{9,8},{10,11... | collective-permute-start | bytes 6291464 | tf_op jit(solution)/shard_map/ppermute | solution.py:17
  392.4 213.7 %reduce-scatter.14.cloned.1.call-start = ((), (), s32[]{:S(2)}) async-start(), calls=%async_computation.13 | async-start | bytes 2621440 | tf_op jit(solution)/shard_map/reduce_scatter | solution.py:469
  400.3 42.5 %collective-permute-start.89 = (bf16[512,2048]{1,0:T(8,128)(2,1)S(1)}, bf16[512,2048]{1,0:T(8,128)(2,1)S(1)}, u32[]{:S(2)}, u32[]{:S(2)}) collective-permute-start(bf16[512,2048]{1,0:T(8,128)(2,1)S(1)} %slice.667), channel_id=1, source_target_pairs={{0,1},{1,0},{2,3},{3,2},{4,5},{5,4},{6,7},{7,6},{8,9},{9,8},{10,11... | collective-permute-start | bytes 6291464 | tf_op jit(solution)/shard_map/ppermute | solution.py:17
  419.7 25.3 %collective-permute-start.39 = (bf16[256,2048]{1,0:T(8,128)(2,1)}, bf16[256,2048]{1,0:T(8,128)(2,1)}, u32[]{:S(2)}, u32[]{:S(2)}) collective-permute-start(bf16[256,2048]{1,0:T(8,128)(2,1)} %get-tuple-element.95), channel_id=1, source_target_pairs={{0,4},{2,6},{4,0},{6,2},{1,5},{3,7},{5,1},{7,3},{8,12},{10,14},{12... | collective-permute-start | bytes 3145736 | tf_op jit(solution)/shard_map/ppermute | solution.py:21
  444.9 212.1 %reduce-scatter.8.cloned.1.call-start = ((), (), s32[]{:S(2)}) async-start(), calls=%async_computation.10 | async-start | bytes 2621440 | tf_op jit(solution)/shard_map/reduce_scatter | solution.py:469
  500.8 200.2 %reduce-scatter.10.cloned.1.call-start = ((), (), s32[]{:S(2)}) async-start(), calls=%async_computation.11 | async-start | bytes 2621440 | tf_op jit(solution)/shard_map/reduce_scatter | solution.py:469
  503.2 25.9 %collective-permute-start.45 = (bf16[256,2048]{1,0:T(8,128)(2,1)}, bf16[256,2048]{1,0:T(8,128)(2,1)}, u32[]{:S(2)}, u32[]{:S(2)}) collective-permute-start(bf16[256,2048]{1,0:T(8,128)(2,1)} %pad_maximum_fusion.13), channel_id=1, source_target_pairs={{0,4},{2,6},{4,0},{6,2},{1,5},{3,7},{5,1},{7,3},{8,12},{10,14},{12... | collective-permute-start | bytes 3145736 | tf_op jit(solution)/shard_map/ppermute | solution.py:21
  506.0 25.7 %collective-permute-start.43 = (bf16[256,2048]{1,0:T(8,128)(2,1)}, bf16[256,2048]{1,0:T(8,128)(2,1)}, u32[]{:S(2)}, u32[]{:S(2)}) collective-permute-start(bf16[256,2048]{1,0:T(8,128)(2,1)} %pad_maximum_fusion.12), channel_id=1, source_target_pairs={{0,2},{2,0},{4,6},{6,4},{1,3},{3,1},{5,7},{7,5},{8,10},{10,8},{12,... | collective-permute-start | bytes 3145736 | tf_op jit(solution)/shard_map/ppermute | solution.py:21
  515.2 57.9 %collective-permute-start.79 = (bf16[512,2048]{1,0:T(8,128)(2,1)S(1)}, bf16[512,2048]{1,0:T(8,128)(2,1)S(1)}, u32[]{:S(2)}, u32[]{:S(2)}) collective-permute-start(bf16[512,2048]{1,0:T(8,128)(2,1)S(1)} %slice.669), channel_id=1, source_target_pairs={{0,1},{1,0},{2,3},{3,2},{4,5},{5,4},{6,7},{7,6},{8,9},{9,8},{10,11... | collective-permute-start | bytes 6291464 | tf_op jit(solution)/shard_map/ppermute | solution.py:17
  539.1 28.7 %collective-permute-start.47 = (bf16[1,64,2048]{2,1,0:T(8,128)(2,1)S(1)}, bf16[1,64,2048]{2,1,0:T(8,128)(2,1)S(1)}, u32[]{:S(2)}, u32[]{:S(2)}) collective-permute-start(bf16[1,64,2048]{2,1,0:T(8,128)(2,1)S(1)} %get-tuple-element.153), channel_id=1, source_target_pairs={{0,16},{8,24},{16,0},{24,8},{1,17},{9,25},{17,1},{25,9},{2,18},{10... | collective-permute-start | bytes 786440 | tf_op jit(solution)/shard_map/ppermute | solution.py:66
  541.5 26.3 %collective-permute-start.48 = (bf16[1,64,2048]{2,1,0:T(8,128)(2,1)S(1)}, bf16[1,64,2048]{2,1,0:T(8,128)(2,1)S(1)}, u32[]{:S(2)}, u32[]{:S(2)}) collective-permute-start(bf16[1,64,2048]{2,1,0:T(8,128)(2,1)S(1)} %get-tuple-element.152), channel_id=1, source_target_pairs={{0,8},{8,16},{16,24},{24,0},{1,9},{9,17},{17,25},{25,1},{2,10},{10... | collective-permute-start | bytes 786440 | tf_op jit(solution)/shard_map/ppermute | solution.py:66
  575.2 194.7 %reduce-scatter.6.cloned.1.call-start = ((), (), s32[]{:S(2)}) async-start(), calls=%async_computation.9 | async-start | bytes 5242880 | tf_op jit(solution)/shard_map/reduce_scatter | solution.py:469
  601.9 36.8 %collective-permute-start.54 = (bf16[1024,2048]{1,0:T(8,128)(2,1)}, bf16[1024,2048]{1,0:T(8,128)(2,1)}, u32[]{:S(2)}, u32[]{:S(2)}) collective-permute-start(bf16[1024,2048]{1,0:T(8,128)(2,1)} %convolution_convert_fusion), channel_id=1, source_target_pairs={{0,1},{1,0},{2,3},{3,2},{4,5},{5,4},{6,7},{7,6},{8,9},{9,8},{10,11... | collective-permute-start | bytes 12582920 | tf_op jit(solution)/shard_map/ppermute | solution.py:17
  606.1 25.5 %collective-permute-start.90 = (bf16[512,512]{1,0:T(8,128)(2,1)}, bf16[512,512]{1,0:T(8,128)(2,1)S(1)}, u32[]{:S(2)}, u32[]{:S(2)}) collective-permute-start(bf16[512,512]{1,0:T(8,128)(2,1)} %reduce-scatter.14.cloned.1.call-done), channel_id=1, source_target_pairs={{0,2},{2,0},{4,6},{6,4},{1,3},{3,1},{5,7},{7,5},{8,10},{10,8},{12,... | collective-permute-start | bytes 1572872 | tf_op jit(solution)/shard_map/ppermute | solution.py:21
  630.9 36.2 %collective-permute-start.93 = (bf16[256,512]{1,0:T(8,128)(2,1)S(1)}, bf16[256,512]{1,0:T(8,128)(2,1)}, u32[]{:S(2)}, u32[]{:S(2)}) collective-permute-start(bf16[256,512]{1,0:T(8,128)(2,1)S(1)} %slice.540), channel_id=1, source_target_pairs={{0,2},{2,0},{4,6},{6,4},{1,3},{3,1},{5,7},{7,5},{8,10},{10,8},{12,... | collective-permute-start | bytes 786440 | tf_op jit(solution)/shard_map/ppermute | solution.py:21
  632.2 35.4 %collective-permute-start.92 = (bf16[256,512]{1,0:T(8,128)(2,1)}, bf16[256,512]{1,0:T(8,128)(2,1)}, u32[]{:S(2)}, u32[]{:S(2)}) collective-permute-start(bf16[256,512]{1,0:T(8,128)(2,1)} %slice.539), channel_id=1, source_target_pairs={{0,4},{2,6},{4,0},{6,2},{1,5},{3,7},{5,1},{7,3},{8,12},{10,14},{12... | collective-permute-start | bytes 786440 | tf_op jit(solution)/shard_map/ppermute | solution.py:21
  664.7 37.6 %collective-permute-start.58 = (bf16[256,2048]{1,0:T(8,128)(2,1)}, bf16[256,2048]{1,0:T(8,128)(2,1)S(1)}, u32[]{:S(2)}, u32[]{:S(2)}) collective-permute-start(bf16[256,2048]{1,0:T(8,128)(2,1)} %pad_maximum_fusion.16), channel_id=1, source_target_pairs={{0,4},{2,6},{4,0},{6,2},{1,5},{3,7},{5,1},{7,3},{8,12},{10,14},{12... | collective-permute-start | bytes 3145736 | tf_op jit(solution)/shard_map/ppermute | solution.py:21
  667.1 35.2 %collective-permute-start.56 = (bf16[256,2048]{1,0:T(8,128)(2,1)}, bf16[256,2048]{1,0:T(8,128)(2,1)}, u32[]{:S(2)}, u32[]{:S(2)}) collective-permute-start(bf16[256,2048]{1,0:T(8,128)(2,1)} %pad_maximum_fusion.15), channel_id=1, source_target_pairs={{0,2},{2,0},{4,6},{6,4},{1,3},{3,1},{5,7},{7,5},{8,10},{10,8},{12,... | collective-permute-start | bytes 3145736 | tf_op jit(solution)/shard_map/ppermute | solution.py:21
  675.1 23.6 %collective-permute-start.78 = (bf16[256,512]{1,0:T(8,128)(2,1)S(1)}, bf16[256,512]{1,0:T(8,128)(2,1)S(1)}, u32[]{:S(2)}, u32[]{:S(2)}) collective-permute-start(bf16[256,512]{1,0:T(8,128)(2,1)S(1)} %slice.528), channel_id=1, source_target_pairs={{0,2},{2,0},{4,6},{6,4},{1,3},{3,1},{5,7},{7,5},{8,10},{10,8},{12,... | collective-permute-start | bytes 786440 | tf_op jit(solution)/shard_map/ppermute | solution.py:21
  675.7 24.3 %collective-permute-start.77 = (bf16[256,512]{1,0:T(8,128)(2,1)S(1)}, bf16[256,512]{1,0:T(8,128)(2,1)S(1)}, u32[]{:S(2)}, u32[]{:S(2)}) collective-permute-start(bf16[256,512]{1,0:T(8,128)(2,1)S(1)} %slice.527), channel_id=1, source_target_pairs={{0,4},{2,6},{4,0},{6,2},{1,5},{3,7},{5,1},{7,3},{8,12},{10,14},{12... | collective-permute-start | bytes 786440 | tf_op jit(solution)/shard_map/ppermute | solution.py:21
  712.9 47.8 %collective-permute-start.83 = (bf16[256,512]{1,0:T(8,128)(2,1)S(1)}, bf16[256,512]{1,0:T(8,128)(2,1)S(1)}, u32[]{:S(2)}, u32[]{:S(2)}) collective-permute-start(bf16[256,512]{1,0:T(8,128)(2,1)S(1)} %slice.532), channel_id=1, source_target_pairs={{0,2},{2,0},{4,6},{6,4},{1,3},{3,1},{5,7},{7,5},{8,10},{10,8},{12,... | collective-permute-start | bytes 786440 | tf_op jit(solution)/shard_map/ppermute | solution.py:21
  714.4 46.3 %collective-permute-start.82 = (bf16[256,512]{1,0:T(8,128)(2,1)S(1)}, bf16[256,512]{1,0:T(8,128)(2,1)S(1)}, u32[]{:S(2)}, u32[]{:S(2)}) collective-permute-start(bf16[256,512]{1,0:T(8,128)(2,1)S(1)} %slice.531), channel_id=1, source_target_pairs={{0,4},{2,6},{4,0},{6,2},{1,5},{3,7},{5,1},{7,3},{8,12},{10,14},{12... | collective-permute-start | bytes 786440 | tf_op jit(solution)/shard_map/ppermute | solution.py:21
  770.6 23.7 %collective-permute-start.72 = (bf16[512,1024]{1,0:T(8,128)(2,1)}, bf16[512,1024]{1,0:T(8,128)(2,1)S(1)}, u32[]{:S(2)}, u32[]{:S(2)}) collective-permute-start(bf16[512,1024]{1,0:T(8,128)(2,1)} %reduce-scatter.6.cloned.1.call-done), channel_id=1, source_target_pairs={{0,4},{2,6},{4,0},{6,2},{1,5},{3,7},{5,1},{7,3},{8,12},{10,14},{12... | collective-permute-start | bytes 3145736 | tf_op jit(solution)/shard_map/ppermute | solution.py:21
  (111 other events, 1447.2 us)
Sparse Core Ops, SparseCore 0:
  11.2 143.0 all-gather.4
  156.4 44.2 all-gather.6
  226.1 48.9 all-gather.8
  278.4 49.0 all-gather.10
  392.5 46.0 reduce-scatter.11
  445.1 45.5 reduce-scatter.13
  501.0 49.9 reduce-scatter.7
  575.3 41.9 reduce-scatter.9
  620.2 76.0 reduce-scatter.5

commit v3 on v2

--- a/solution.py
+++ b/solution.py
@@ -538,8 +538,8 @@
     normed = lax.optimization_barrier(normed)
     dy_rows = jnp.concatenate((dy_own,) + spread(after(dy_own, arrived)), axis=0)
     output_own = gather_cols(after(rows_of(output_weight, VAL), arrived))
-    expand_own = gather_rows(after(cols_of(expand_weight, part), dy_own))
-    reduce_own = gather_cols(after(rows_of(reduce_weight, part), dy_rows))
+    expand_own = gather_rows(after(cols_of(expand_weight, part), normed))
+    reduce_own = gather_cols(after(rows_of(reduce_weight, part), normed))
 
     last = natural[:, rows - 1]
     ends = jnp.cumsum(spans, axis=1).reshape(form + (-1,))

time: 824 us -> 822 us (level)
  starting transfers between devices: 119 us -> 106 us
    ppermute x12, starting transfers between devices: 34.5 us -> 20.9 us  [turn(): lax.ppermute(value, 'seq', [(source, (source + steps) % count) for source...]
    all_gather x2, waiting for transfers between devices: 15.9 us -> 28 us  [gather_cols(): return lax.all_gather(weight, 'seq', axis=1, tiled=True)]
    unnamed x142 -> x128, local copies, waits for them, and re-layouts: 44.8 us -> 44.3 us
where the time goes in v3:
time: 822 us; the launch traced here: 812 us
  waiting for transfers between devices  356 us (43%)
  matrix products  111 us (14%)
  local copies, waits for them, and re-layouts  106 us (13%)
  starting transfers between devices  106 us (13%)
  other arithmetic  74.7 us (9%)
  Pallas kernels  43 us (5%)
  between operations  15.9 us (2%)
    ppermute x61, waiting for transfers between devices, swap_batch(): lax.ppermute(value, 'batch', [(place, place ^ mask) for place in range(4)])  217 us
    ppermute x12, waiting for transfers between devices, turn(): lax.ppermute(value, 'seq', [(source, (source + steps) % count) for source...  92.9 us
    ppermute x61, starting transfers between devices, swap_batch(): lax.ppermute(value, 'batch', [(place, place ^ mask) for place in range(4)])  69 us
    dot_general x8, matrix products, contract_cols(): lax.dot_general(left, right, (((1,), (1,)), ((), ())), preferred_element_...  45.5 us
    unnamed x128, local copies, waits for them, and re-layouts  44.3 us
    dot_general x5, matrix products, contract_rows(): lax.dot_general(left, right, (((0,), (0,)), ((), ())), preferred_element_...  43.6 us
    pallas_call x2, Pallas kernels, by_block(): pl.pallas_call(kernel, grid=(4,), in_specs=[block_spec(v, at in shared, l...  43 us
    all_gather x2, waiting for transfers between devices, gather_cols(): return lax.all_gather(weight, 'seq', axis=1, tiled=True)  28 us
  transfers between devices with their start and end apart: 103, of which 50 were waited for; matrix products, arithmetic and copies ran while one was open for 32% of the time, Pallas kernels for 5%

profile of v3, /device:TPU:0, one launch (start us, length us, event | category | flops | bytes accessed | tf_op | source)
XLA Modules:
  0.0 812.4 jit_solution(12558701973356125441)
XLA Ops:
  15.0 3.9 collective-permute-start.2
  23.7 9.0 %collective-permute-done.2 = bf16[136,2048]{1,0:T(8,128)(2,1)S(1)} collective-permute-done((bf16[136,2048]{1,0:T(8,128)(2,1)}, bf16[136,2048]{1,0:T(8,128)(2,1)S(1)}, u32[]{:S(2)}, u32[]{:S(2)}) %collective-permute-start.2) | collective-permute-done | bytes 557088 | tf_op jit(solution)/shard_map/ppermute | solution.py:21
  32.6 11.2 %collective-permute-done.1 = bf16[136,2048]{1,0:T(8,128)(2,1)} collective-permute-done((bf16[136,2048]{1,0:T(8,128)(2,1)}, bf16[136,2048]{1,0:T(8,128)(2,1)}, u32[]{:S(2)}, u32[]{:S(2)}) %collective-permute-start.1) | collective-permute-done | bytes 557088 | tf_op jit(solution)/shard_map/ppermute | solution.py:21
  51.6 12.4 %collective-permute-done.3 = bf16[1,72,2048]{2,1,0:T(8,128)(2,1)S(1)} collective-permute-done((bf16[1,72,2048]{2,1,0:T(8,128)(2,1)S(1)}, bf16[1,72,2048]{2,1,0:T(8,128)(2,1)S(1)}, u32[]{:S(2)}, u32[]{:S(2)}) %collective-permute-start.3) | collective-permute-done | bytes 294944 | tf_op jit(solution)/shard_map/ppermute | solution.py:66
  64.0 21.0 %collective-permute-done.4 = bf16[1,72,2048]{2,1,0:T(8,128)(2,1)S(1)} collective-permute-done((bf16[1,72,2048]{2,1,0:T(8,128)(2,1)S(1)}, bf16[1,72,2048]{2,1,0:T(8,128)(2,1)S(1)}, u32[]{:S(2)}, u32[]{:S(2)}) %collective-permute-start.4) | collective-permute-done | bytes 294944 | tf_op jit(solution)/shard_map/ppermute | solution.py:66
  94.1 18.3 %collective-permute-done.6 = bf16[256,2048]{1,0:T(8,128)(2,1)} collective-permute-done((bf16[256,2048]{1,0:T(8,128)(2,1)}, bf16[256,2048]{1,0:T(8,128)(2,1)}, u32[]{:S(2)}, u32[]{:S(2)}) %collective-permute-start.6) | collective-permute-done | bytes 1048608 | tf_op jit(solution)/shard_map/ppermute | solution.py:21
  121.2 4.3 collective-permute-done.8
  131.6 5.5 multiply_sine_fusion
  147.9 6.4 all-gather.5.cloned.1.call-done.weight
  154.3 24.4 %shard_map.297 = (bf16[2,4,4,64,256]{4,3,2,1,0:T(8,128)(2,1)}, bf16[2,4,4,64,256]{4,3,2,1,0:T(8,128)(2,1)}, bf16[2,4,4,64,512]{4,3,2,1,0:T(8,128)(2,1)}, bf16[4,...) custom-call(bf16[2,4,4,64,2048]{4,3,2,1,0:T(8,128)(2,1)} %bitcast.13, ...), custom_call_target="tpu_custom_call" | custom-call | tf_op jit(solution)/shard_map/pallas_call | solution.py:326
  187.4 13.3 %all-gather.7.cloned.1.call-done = bf16[512,2048]{1,0:T(8,128)(2,1)} async-done(((bf16[512,512]{1,0:T(8,128)(2,1)}), bf16[512,2048]{1,0:T(8,128)(2,1)}) %all-gather.7.cloned.1.call-update) | async-done | bytes 2097168 | tf_op jit(solution)/shard_map/all_gather | solution.py:466
  202.1 6.9 collective-permute-start.27
  211.2 4.4 collective-permute-done.26
  215.7 10.9 %collective-permute-done.27 = bf16[1,64,2048]{2,1,0:T(8,128)(2,1)S(1)} collective-permute-done((bf16[1,64,2048]{2,1,0:T(8,128)(2,1)S(1)}, bf16[1,64,2048]{2,1,0:T(8,128)(2,1)S(1)}, u32[]{:S(2)}, u32[]{:S(2)}) %collective-permute-start.27) | collective-permute-done | bytes 262176 | tf_op jit(solution)/shard_map/ppermute | solution.py:66
  228.5 10.4 %all-gather.11.cloned.1.call-start = ((), (), s32[]{:S(2)}) async-start(), calls=%async_computation.8 | async-start | bytes 2621440 | tf_op jit(solution)/shard_map/all_gather | solution.py:466
  250.4 12.7 %collective-permute-done.16 = bf16[128,2048]{1,0:T(8,128)(2,1)S(1)} collective-permute-done((bf16[128,2048]{1,0:T(8,128)(2,1)S(1)}, bf16[128,2048]{1,0:T(8,128)(2,1)S(1)}, u32[]{:S(2)}, u32[]{:S(2)}) %collective-permute-start.16) | collective-permute-done | bytes 524320 | tf_op jit(solution)/shard_map/ppermute | solution.py:21
  276.9 13.9 %collective-permute-done.19 = bf16[256,2048]{1,0:T(8,128)(2,1)} collective-permute-done((bf16[256,2048]{1,0:T(8,128)(2,1)}, bf16[256,2048]{1,0:T(8,128)(2,1)}, u32[]{:S(2)}, u32[]{:S(2)}) %collective-permute-start.19) | collective-permute-done | bytes 1048608 | tf_op jit(solution)/shard_map/ppermute | solution.py:21
  293.3 3.4 fusion.91
  309.6 14.7 %all-gather.11.cloned.1.call-done = bf16[512,2048]{1,0:T(8,128)(2,1)} async-done(((bf16[512,512]{1,0:T(8,128)(2,1)}), bf16[512,2048]{1,0:T(8,128)(2,1)}) %all-gather.11.cloned.1.call-update) | async-done | bytes 2097168 | tf_op jit(solution)/shard_map/all_gather | solution.py:466
  334.5 6.7 collective-permute-done.22
  341.2 3.5 collective-permute-done.23
  346.7 6.1 multiply_convert_fusion
  353.0 9.5 %convert_reduce_fusion = (f32[1024]{0:T(1024)S(1)}, bf16[1024,1024]{1,0:T(8,128)(2,1)S(1)}) fusion(f32[1024,1024]{1,0:T(8,128)S(1)} %get-tuple-element.212, f32[1024]{0:T(1024)S(1)} %pad_maximum_fusion.19, bf16[1024,2048]{1,0:T(8,128)(2,1)} %constant_dynamic-update-slice_fusion.25, bf16[1024,2048]{1,0:T(8,128)(2,1)S(1)} %constant_dynamic-update-slice_fusion.30), kind=kOutput, calls=%fused_computation.20 | convolution fusion | flops 4308597760 | bytes 14688256 | tf_op jit(solution)/shard_map/dot_general | solution.py:99
  363.8 4.6 fusion.95
  373.5 8.6 %collective-permute-done.34 = bf16[128,2048]{1,0:T(8,128)(2,1)S(1)} collective-permute-done((bf16[128,2048]{1,0:T(8,128)(2,1)S(1)}, bf16[128,2048]{1,0:T(8,128)(2,1)S(1)}, u32[]{:S(2)}, u32[]{:S(2)}) %collective-permute-start.34) | collective-permute-done | bytes 524320 | tf_op jit(solution)/shard_map/ppermute | solution.py:21
  390.1 7.5 fusion.96
  398.0 9.7 %collective-permute-done.37 = bf16[256,2048]{1,0:T(8,128)(2,1)} collective-permute-done((bf16[256,2048]{1,0:T(8,128)(2,1)}, bf16[256,2048]{1,0:T(8,128)(2,1)}, u32[]{:S(2)}, u32[]{:S(2)}) %collective-permute-start.37) | collective-permute-done | bytes 1048608 | tf_op jit(solution)/shard_map/ppermute | solution.py:21
  409.9 3.9 multiply_reduce_fusion
  418.6 20.6 %collective-permute-done.38 = bf16[256,2048]{1,0:T(8,128)(2,1)S(1)} collective-permute-done((bf16[256,2048]{1,0:T(8,128)(2,1)}, bf16[256,2048]{1,0:T(8,128)(2,1)S(1)}, u32[]{:S(2)}, u32[]{:S(2)}) %collective-permute-start.38) | collective-permute-done | bytes 1048608 | tf_op jit(solution)/shard_map/ppermute | solution.py:21
  460.4 4.9 convolution_convert_fusion.5
  472.2 18.6 %shard_map.298 = (bf16[2,4,4,64,1536]{4,3,2,1,0:T(8,128)(2,1)}, f32[2,512]{1,0:T(2,128)}) custom-call(bf16[4,4,64,512]{3,2,1,0:T(8,128)(2,1)} %bitcast.112, bf16[4,4,64,512]{3,2,1,0:T(8,128)(2,1)} %bitcast.117, f32[2,4,4,64,512]{4,3,2,1,0:T(8,128)} %get-tuple-element.74.gate, f32[2,4,4,64,512]{4,3,2,1,0:T(8,128)} %get-tuple-element.75.unit, ...), custom_call_target="tpu_custom_call" | custom-call | tf_op jit(solution)/shard_map/pallas_call | solution.py:326
  490.8 10.0 %convolution_convert_fusion.1 = bf16[2048,512]{1,0:T(8,128)(2,1)} fusion(bf16[2048,2048]{1,0:T(8,128)(2,1)} %constant_dynamic-update-slice_fusion.2, bf16[2048,1536]{1,0:T(8,128)(2,1)} %bitcast.140), kind=kOutput, calls=%fused_computation.26 | convolution fusion | flops 4296015872 | bytes 12582912 | tf_op jit(solution)/shard_map/dot_general | solution.py:95
  507.6 7.1 fusion.75
  515.1 14.0 %collective-permute-done.45 = bf16[256,2048]{1,0:T(8,128)(2,1)} collective-permute-done((bf16[256,2048]{1,0:T(8,128)(2,1)}, bf16[256,2048]{1,0:T(8,128)(2,1)}, u32[]{:S(2)}, u32[]{:S(2)}) %collective-permute-start.45) | collective-permute-done | bytes 1048608 | tf_op jit(solution)/shard_map/ppermute | solution.py:21
  537.1 3.9 collective-permute-start.47
  541.0 7.9 collective-permute-done.46
  548.9 17.7 %collective-permute-done.47 = bf16[1,64,2048]{2,1,0:T(8,128)(2,1)S(1)} collective-permute-done((bf16[1,64,2048]{2,1,0:T(8,128)(2,1)S(1)}, bf16[1,64,2048]{2,1,0:T(8,128)(2,1)S(1)}, u32[]{:S(2)}, u32[]{:S(2)}) %collective-permute-start.47) | collective-permute-done | bytes 262176 | tf_op jit(solution)/shard_map/ppermute | solution.py:66
  573.6 14.4 %fusion.11 = bf16[2048,1024]{1,0:T(8,128)(2,1)} fusion(bf16[2048,2048]{1,0:T(8,128)(2,1)} %constant_dynamic-update-slice_fusion.2, bf16[2048,1536]{1,0:T(8,128)(2,1)} %bitcast.141), kind=kOutput, calls=%fused_computation.24 | convolution fusion | flops 8592031744 | bytes 16777216 | tf_op jit(solution)/shard_map/dot_general | solution.py:95
  589.1 11.1 %convolution_convert_fusion = bf16[1024,2048]{1,0:T(8,128)(2,1)} fusion(bf16[2048,1536]{1,0:T(8,128)(2,1)} %all-gather.5.cloned.1.call-done.weight, bf16[2048,1536]{1,0:T(8,128)(2,1)} %bitcast.142), kind=kOutput, calls=%fused_computation.23 | convolution fusion | flops 6444548096 | bytes 13631488 | tf_op jit(solution)/shard_map/dot_general | solution.py:99
  611.0 6.9 collective-permute-done.86
  620.1 9.1 %collective-permute-done.91 = bf16[512,512]{1,0:T(8,128)(2,1)S(1)} collective-permute-done((bf16[512,512]{1,0:T(8,128)(2,1)S(1)}, bf16[512,512]{1,0:T(8,128)(2,1)S(1)}, u32[]{:S(2)}, u32[]{:S(2)}) %collective-permute-start.91) | collective-permute-done | bytes 524320 | tf_op jit(solution)/shard_map/ppermute | solution.py:21
  637.1 3.9 convert_element_type.356
  646.0 9.3 %fusion.94 = (bf16[768,2048]{1,0:T(8,128)(2,1)}, f32[768,2048]{1,0:T(8,128)}) fusion(f32[1024,2048]{1,0:T(8,128)S(1)} %convert_element_type.356, bf16[2048,1536]{1,0:T(8,128)(2,1)S(1)} %bitcast.111, bf16[2048,1536]{1,0:T(8,128)(2,1)} %bitcast.144), kind=kOutput, calls=%fused_computation.345 | convolution fusion | flops 4834983936 | bytes 24379392 | tf_op jit(solution)/shard_map/dot_general | solution.py:99
  676.9 20.1 %collective-permute-done.78 = bf16[256,512]{1,0:T(8,128)(2,1)S(1)} collective-permute-done((bf16[256,512]{1,0:T(8,128)(2,1)S(1)}, bf16[256,512]{1,0:T(8,128)(2,1)S(1)}, u32[]{:S(2)}, u32[]{:S(2)}) %collective-permute-start.78) | collective-permute-done | bytes 262176 | tf_op jit(solution)/shard_map/ppermute | solution.py:21
  716.9 17.5 %collective-permute-done.60 = bf16[1,64,2048]{2,1,0:T(8,128)(2,1)S(1)} collective-permute-done((bf16[1,64,2048]{2,1,0:T(8,128)(2,1)S(1)}, bf16[1,64,2048]{2,1,0:T(8,128)(2,1)S(1)}, u32[]{:S(2)}, u32[]{:S(2)}) %collective-permute-start.60) | collective-permute-done | bytes 262176 | tf_op jit(solution)/shard_map/ppermute | solution.py:66
  741.4 3.3 collective-permute-done.64
  773.2 17.3 %collective-permute-done.71 = bf16[512,1024]{1,0:T(8,128)(2,1)S(1)} collective-permute-done((bf16[512,1024]{1,0:T(8,128)(2,1)}, bf16[512,1024]{1,0:T(8,128)(2,1)S(1)}, u32[]{:S(2)}, u32[]{:S(2)}) %collective-permute-start.71) | collective-permute-done | bytes 1048608 | tf_op jit(solution)/shard_map/ppermute | solution.py:21
  794.9 7.2 collective-permute-done.73
  (539 shorter events, 304.8 us)
Async XLA Ops:
  7.2 147.0 %all-gather.5.cloned.1.call-start = ((), (), s32[]{:S(2)}) async-start(), calls=%async_computation.5 | async-start | bytes 7864320 | tf_op jit(solution)/shard_map/all_gather | solution.py:463
  11.0 189.6 %all-gather.7.cloned.1.call-start = ((), (), s32[]{:S(2)}) async-start(), calls=%async_computation.6 | async-start | bytes 2621440 | tf_op jit(solution)/shard_map/all_gather | solution.py:466
  18.9 24.9 %collective-permute-start.1 = (bf16[136,2048]{1,0:T(8,128)(2,1)}, bf16[136,2048]{1,0:T(8,128)(2,1)}, u32[]{:S(2)}, u32[]{:S(2)}) collective-permute-start(bf16[136,2048]{1,0:T(8,128)(2,1)} %get-tuple-element.181), channel_id=1, source_target_pairs={{0,4},{2,6},{4,0},{6,2},{1,5},{3,7},{5,1},{7,3},{8,12},{10,14},{12... | collective-permute-start | bytes 1671176 | tf_op jit(solution)/shard_map/ppermute | solution.py:21
  19.4 24.7 %collective-permute-start = (bf16[136,2048]{1,0:T(8,128)(2,1)}, bf16[136,2048]{1,0:T(8,128)(2,1)}, u32[]{:S(2)}, u32[]{:S(2)}) collective-permute-start(bf16[136,2048]{1,0:T(8,128)(2,1)} %get-tuple-element.180), channel_id=1, source_target_pairs={{0,2},{2,0},{4,6},{6,4},{1,3},{3,1},{5,7},{7,5},{8,10},{10,8},{12,... | collective-permute-start | bytes 1671176 | tf_op jit(solution)/shard_map/ppermute | solution.py:21
  47.6 37.4 %collective-permute-start.4 = (bf16[1,72,2048]{2,1,0:T(8,128)(2,1)S(1)}, bf16[1,72,2048]{2,1,0:T(8,128)(2,1)S(1)}, u32[]{:S(2)}, u32[]{:S(2)}) collective-permute-start(bf16[1,72,2048]{2,1,0:T(8,128)(2,1)S(1)} %get-tuple-element.129), channel_id=1, source_target_pairs={{0,16},{8,24},{16,0},{24,8},{1,17},{9,25},{17,1},{25,9},{2,18},{10... | collective-permute-start | bytes 884744 | tf_op jit(solution)/shard_map/ppermute | solution.py:66
  50.2 36.0 %collective-permute-start.5 = (bf16[1,72,2048]{2,1,0:T(8,128)(2,1)S(1)}, bf16[1,72,2048]{2,1,0:T(8,128)(2,1)S(1)}, u32[]{:S(2)}, u32[]{:S(2)}) collective-permute-start(bf16[1,72,2048]{2,1,0:T(8,128)(2,1)S(1)} %get-tuple-element.128), channel_id=1, source_target_pairs={{0,24},{8,0},{16,8},{24,16},{1,25},{9,1},{17,9},{25,17},{2,26},{10... | collective-permute-start | bytes 884744 | tf_op jit(solution)/shard_map/ppermute | solution.py:66
  87.9 24.5 %collective-permute-start.6 = (bf16[256,2048]{1,0:T(8,128)(2,1)}, bf16[256,2048]{1,0:T(8,128)(2,1)}, u32[]{:S(2)}, u32[]{:S(2)}) collective-permute-start(bf16[256,2048]{1,0:T(8,128)(2,1)} %multiply_convert_fusion.1), channel_id=1, source_target_pairs={{0,2},{2,0},{4,6},{6,4},{1,3},{3,1},{5,7},{7,5},{8,10},{10,8},{12,... | collective-permute-start | bytes 3145736 | tf_op jit(solution)/shard_map/ppermute | solution.py:21
  89.4 25.7 %collective-permute-start.7 = (bf16[256,2048]{1,0:T(8,128)(2,1)}, bf16[256,2048]{1,0:T(8,128)(2,1)}, u32[]{:S(2)}, u32[]{:S(2)}) collective-permute-start(bf16[256,2048]{1,0:T(8,128)(2,1)} %multiply_convert_fusion.1), channel_id=1, source_target_pairs={{0,4},{2,6},{4,0},{6,2},{1,5},{3,7},{5,1},{7,3},{8,12},{10,14},{12... | collective-permute-start | bytes 3145736 | tf_op jit(solution)/shard_map/ppermute | solution.py:21
  89.9 48.6 %collective-permute-start.10 = (bf16[256,2048]{1,0:T(8,128)(2,1)}, bf16[256,2048]{1,0:T(8,128)(2,1)}, u32[]{:S(2)}, u32[]{:S(2)}) collective-permute-start(bf16[256,2048]{1,0:T(8,128)(2,1)} %multiply_convert_fusion.1), channel_id=1, source_target_pairs={{0,1},{1,0},{2,3},{3,2},{4,5},{5,4},{6,7},{7,6},{8,9},{9,8},{10,11... | collective-permute-start | bytes 3145736 | tf_op jit(solution)/shard_map/ppermute | solution.py:17
  116.5 24.3 %collective-permute-start.11 = (bf16[256,2048]{1,0:T(8,128)(2,1)}, bf16[256,2048]{1,0:T(8,128)(2,1)}, u32[]{:S(2)}, u32[]{:S(2)}) collective-permute-start(bf16[256,2048]{1,0:T(8,128)(2,1)} %collective-permute-done.6), channel_id=1, source_target_pairs={{0,1},{1,0},{2,3},{3,2},{4,5},{5,4},{6,7},{7,6},{8,9},{9,8},{10,11... | collective-permute-start | bytes 3145736 | tf_op jit(solution)/shard_map/ppermute | solution.py:17
  130.0 173.5 %all-gather.9.cloned.1.call-start = ((), (), s32[]{:S(2)}) async-start(), calls=%async_computation.7 | async-start | bytes 2621440 | tf_op jit(solution)/shard_map/all_gather | solution.py:463
  200.7 40.0 %collective-permute-start.15 = (bf16[512,2048]{1,0:T(8,128)(2,1)}, bf16[512,2048]{1,0:T(8,128)(2,1)}, u32[]{:S(2)}, u32[]{:S(2)}) collective-permute-start(bf16[512,2048]{1,0:T(8,128)(2,1)} %all-gather.7.cloned.1.call-done), channel_id=1, source_target_pairs={{0,1},{1,0},{2,3},{3,2},{4,5},{5,4},{6,7},{7,6},{8,9},{9,8},{10,11... | collective-permute-start | bytes 6291464 | tf_op jit(solution)/shard_map/ppermute | solution.py:17
  202.1 24.4 %collective-permute-start.27 = (bf16[1,64,2048]{2,1,0:T(8,128)(2,1)S(1)}, bf16[1,64,2048]{2,1,0:T(8,128)(2,1)S(1)}, u32[]{:S(2)}, u32[]{:S(2)}) collective-permute-start(bf16[1,64,2048]{2,1,0:T(8,128)(2,1)S(1)} %get-tuple-element.161), channel_id=1, source_target_pairs={{0,16},{8,24},{16,0},{24,8},{1,17},{9,25},{17,1},{25,9},{2,18},{10... | collective-permute-start | bytes 786440 | tf_op jit(solution)/shard_map/ppermute | solution.py:66
  226.6 44.1 %collective-permute-start.29 = (bf16[256,2048]{1,0:T(8,128)(2,1)S(1)}, bf16[256,2048]{1,0:T(8,128)(2,1)}, u32[]{:S(2)}, u32[]{:S(2)}) collective-permute-start(bf16[256,2048]{1,0:T(8,128)(2,1)S(1)} %bitcast.106), channel_id=1, source_target_pairs={{0,2},{2,0},{4,6},{6,4},{1,3},{3,1},{5,7},{7,5},{8,10},{10,8},{12,... | collective-permute-start | bytes 3145736 | tf_op jit(solution)/shard_map/ppermute | solution.py:21
  226.9 47.8 %collective-permute-start.30 = (bf16[256,2048]{1,0:T(8,128)(2,1)S(1)}, bf16[256,2048]{1,0:T(8,128)(2,1)}, u32[]{:S(2)}, u32[]{:S(2)}) collective-permute-start(bf16[256,2048]{1,0:T(8,128)(2,1)S(1)} %bitcast.107), channel_id=1, source_target_pairs={{0,4},{2,6},{4,0},{6,2},{1,5},{3,7},{5,1},{7,3},{8,12},{10,14},{12... | collective-permute-start | bytes 3145736 | tf_op jit(solution)/shard_map/ppermute | solution.py:21
  228.5 95.8 %all-gather.11.cloned.1.call-start = ((), (), s32[]{:S(2)}) async-start(), calls=%async_computation.8 | async-start | bytes 2621440 | tf_op jit(solution)/shard_map/all_gather | solution.py:466
  264.4 26.4 %collective-permute-start.19 = (bf16[256,2048]{1,0:T(8,128)(2,1)}, bf16[256,2048]{1,0:T(8,128)(2,1)}, u32[]{:S(2)}, u32[]{:S(2)}) collective-permute-start(bf16[256,2048]{1,0:T(8,128)(2,1)} %pad_maximum_fusion.9), channel_id=1, source_target_pairs={{0,4},{2,6},{4,0},{6,2},{1,5},{3,7},{5,1},{7,3},{8,12},{10,14},{12... | collective-permute-start | bytes 3145736 | tf_op jit(solution)/shard_map/ppermute | solution.py:21
  266.8 26.4 %collective-permute-start.17 = (bf16[256,2048]{1,0:T(8,128)(2,1)}, bf16[256,2048]{1,0:T(8,128)(2,1)}, u32[]{:S(2)}, u32[]{:S(2)}) collective-permute-start(bf16[256,2048]{1,0:T(8,128)(2,1)} %pad_maximum_fusion.8), channel_id=1, source_target_pairs={{0,2},{2,0},{4,6},{6,4},{1,3},{3,1},{5,7},{7,5},{8,10},{10,8},{12,... | collective-permute-start | bytes 3145736 | tf_op jit(solution)/shard_map/ppermute | solution.py:21
  269.3 332.1 %reduce-scatter.12.cloned.1.call-start = ((), (), s32[]{:S(2)}) async-start(), calls=%async_computation.12 | async-start | bytes 2621440 | tf_op jit(solution)/shard_map/reduce_scatter | solution.py:469
  272.9 32.9 %collective-permute-start.31 = (bf16[128,2048]{1,0:T(8,128)(2,1)}, bf16[128,2048]{1,0:T(8,128)(2,1)}, u32[]{:S(2)}, u32[]{:S(2)}) collective-permute-start(bf16[128,2048]{1,0:T(8,128)(2,1)} %slice.477), channel_id=1, source_target_pairs={{0,4},{2,6},{4,0},{6,2},{1,5},{3,7},{5,1},{7,3},{8,12},{10,14},{12... | collective-permute-start | bytes 1572872 | tf_op jit(solution)/shard_map/ppermute | solution.py:21
  276.5 31.1 %collective-permute-start.32 = (bf16[128,2048]{1,0:T(8,128)(2,1)}, bf16[128,2048]{1,0:T(8,128)(2,1)}, u32[]{:S(2)}, u32[]{:S(2)}) collective-permute-start(bf16[128,2048]{1,0:T(8,128)(2,1)} %slice.478), channel_id=1, source_target_pairs={{0,2},{2,0},{4,6},{6,4},{1,3},{3,1},{5,7},{7,5},{8,10},{10,8},{12,... | collective-permute-start | bytes 1572872 | tf_op jit(solution)/shard_map/ppermute | solution.py:21
  298.9 27.4 %collective-permute-start.20 = (bf16[256,2048]{1,0:T(8,128)(2,1)}, bf16[256,2048]{1,0:T(8,128)(2,1)}, u32[]{:S(2)}, u32[]{:S(2)}) collective-permute-start(bf16[256,2048]{1,0:T(8,128)(2,1)} %get-tuple-element.97), channel_id=1, source_target_pairs={{0,2},{2,0},{4,6},{6,4},{1,3},{3,1},{5,7},{7,5},{8,10},{10,8},{12,... | collective-permute-start | bytes 3145736 | tf_op jit(solution)/shard_map/ppermute | solution.py:21
  301.7 27.5 %collective-permute-start.21 = (bf16[256,2048]{1,0:T(8,128)(2,1)}, bf16[256,2048]{1,0:T(8,128)(2,1)}, u32[]{:S(2)}, u32[]{:S(2)}) collective-permute-start(bf16[256,2048]{1,0:T(8,128)(2,1)} %get-tuple-element.97), channel_id=1, source_target_pairs={{0,4},{2,6},{4,0},{6,2},{1,5},{3,7},{5,1},{7,3},{8,12},{10,14},{12... | collective-permute-start | bytes 3145736 | tf_op jit(solution)/shard_map/ppermute | solution.py:21
  303.5 41.3 %collective-permute-start.24 = (bf16[2048,512]{1,0:T(8,128)(2,1)}, bf16[2048,512]{1,0:T(8,128)(2,1)}, u32[]{:S(2)}, u32[]{:S(2)}) collective-permute-start(bf16[2048,512]{1,0:T(8,128)(2,1)} %all-gather.9.cloned.1.call-done), channel_id=1, source_target_pairs={{0,1},{1,0},{2,3},{3,2},{4,5},{5,4},{6,7},{7,6},{8,9},{9,8},{10,11... | collective-permute-start | bytes 6291464 | tf_op jit(solution)/shard_map/ppermute | solution.py:17
  329.2 23.6 %collective-permute-start.33 = (bf16[512,2048]{1,0:T(8,128)(2,1)S(1)}, bf16[512,2048]{1,0:T(8,128)(2,1)S(1)}, u32[]{:S(2)}, u32[]{:S(2)}) collective-permute-start(bf16[512,2048]{1,0:T(8,128)(2,1)S(1)} %copy-done.16), channel_id=1, source_target_pairs={{0,1},{1,0},{2,3},{3,2},{4,5},{5,4},{6,7},{7,6},{8,9},{9,8},{10,11... | collective-permute-start | bytes 6291464 | tf_op jit(solution)/shard_map/ppermute | solution.py:17
  383.8 23.9 %collective-permute-start.37 = (bf16[256,2048]{1,0:T(8,128)(2,1)}, bf16[256,2048]{1,0:T(8,128)(2,1)}, u32[]{:S(2)}, u32[]{:S(2)}) collective-permute-start(bf16[256,2048]{1,0:T(8,128)(2,1)} %pad_maximum_fusion.11), channel_id=1, source_target_pairs={{0,4},{2,6},{4,0},{6,2},{1,5},{3,7},{5,1},{7,3},{8,12},{10,14},{12... | collective-permute-start | bytes 3145736 | tf_op jit(solution)/shard_map/ppermute | solution.py:21
  390.0 214.4 %reduce-scatter.14.cloned.1.call-start = ((), (), s32[]{:S(2)}) async-start(), calls=%async_computation.13 | async-start | bytes 2621440 | tf_op jit(solution)/shard_map/reduce_scatter | solution.py:469
  397.9 43.8 %collective-permute-start.89 = (bf16[512,2048]{1,0:T(8,128)(2,1)S(1)}, bf16[512,2048]{1,0:T(8,128)(2,1)S(1)}, u32[]{:S(2)}, u32[]{:S(2)}) collective-permute-start(bf16[512,2048]{1,0:T(8,128)(2,1)S(1)} %slice.667), channel_id=1, source_target_pairs={{0,1},{1,0},{2,3},{3,2},{4,5},{5,4},{6,7},{7,6},{8,9},{9,8},{10,11... | collective-permute-start | bytes 6291464 | tf_op jit(solution)/shard_map/ppermute | solution.py:17
  418.1 25.8 %collective-permute-start.39 = (bf16[256,2048]{1,0:T(8,128)(2,1)}, bf16[256,2048]{1,0:T(8,128)(2,1)}, u32[]{:S(2)}, u32[]{:S(2)}) collective-permute-start(bf16[256,2048]{1,0:T(8,128)(2,1)} %get-tuple-element.95), channel_id=1, source_target_pairs={{0,4},{2,6},{4,0},{6,2},{1,5},{3,7},{5,1},{7,3},{8,12},{10,14},{12... | collective-permute-start | bytes 3145736 | tf_op jit(solution)/shard_map/ppermute | solution.py:21
  443.8 211.6 %reduce-scatter.8.cloned.1.call-start = ((), (), s32[]{:S(2)}) async-start(), calls=%async_computation.10 | async-start | bytes 2621440 | tf_op jit(solution)/shard_map/reduce_scatter | solution.py:469
  500.8 198.4 %reduce-scatter.10.cloned.1.call-start = ((), (), s32[]{:S(2)}) async-start(), calls=%async_computation.11 | async-start | bytes 2621440 | tf_op jit(solution)/shard_map/reduce_scatter | solution.py:469
  503.2 25.9 %collective-permute-start.45 = (bf16[256,2048]{1,0:T(8,128)(2,1)}, bf16[256,2048]{1,0:T(8,128)(2,1)}, u32[]{:S(2)}, u32[]{:S(2)}) collective-permute-start(bf16[256,2048]{1,0:T(8,128)(2,1)} %pad_maximum_fusion.13), channel_id=1, source_target_pairs={{0,4},{2,6},{4,0},{6,2},{1,5},{3,7},{5,1},{7,3},{8,12},{10,14},{12... | collective-permute-start | bytes 3145736 | tf_op jit(solution)/shard_map/ppermute | solution.py:21
  506.1 25.6 %collective-permute-start.43 = (bf16[256,2048]{1,0:T(8,128)(2,1)}, bf16[256,2048]{1,0:T(8,128)(2,1)}, u32[]{:S(2)}, u32[]{:S(2)}) collective-permute-start(bf16[256,2048]{1,0:T(8,128)(2,1)} %pad_maximum_fusion.12), channel_id=1, source_target_pairs={{0,2},{2,0},{4,6},{6,4},{1,3},{3,1},{5,7},{7,5},{8,10},{10,8},{12,... | collective-permute-start | bytes 3145736 | tf_op jit(solution)/shard_map/ppermute | solution.py:21
  515.0 56.4 %collective-permute-start.79 = (bf16[512,2048]{1,0:T(8,128)(2,1)S(1)}, bf16[512,2048]{1,0:T(8,128)(2,1)S(1)}, u32[]{:S(2)}, u32[]{:S(2)}) collective-permute-start(bf16[512,2048]{1,0:T(8,128)(2,1)S(1)} %slice.669), channel_id=1, source_target_pairs={{0,1},{1,0},{2,3},{3,2},{4,5},{5,4},{6,7},{7,6},{8,9},{9,8},{10,11... | collective-permute-start | bytes 6291464 | tf_op jit(solution)/shard_map/ppermute | solution.py:17
  537.1 29.6 %collective-permute-start.47 = (bf16[1,64,2048]{2,1,0:T(8,128)(2,1)S(1)}, bf16[1,64,2048]{2,1,0:T(8,128)(2,1)S(1)}, u32[]{:S(2)}, u32[]{:S(2)}) collective-permute-start(bf16[1,64,2048]{2,1,0:T(8,128)(2,1)S(1)} %get-tuple-element.153), channel_id=1, source_target_pairs={{0,16},{8,24},{16,0},{24,8},{1,17},{9,25},{17,1},{25,9},{2,18},{10... | collective-permute-start | bytes 786440 | tf_op jit(solution)/shard_map/ppermute | solution.py:66
  541.0 25.7 %collective-permute-start.48 = (bf16[1,64,2048]{2,1,0:T(8,128)(2,1)S(1)}, bf16[1,64,2048]{2,1,0:T(8,128)(2,1)S(1)}, u32[]{:S(2)}, u32[]{:S(2)}) collective-permute-start(bf16[1,64,2048]{2,1,0:T(8,128)(2,1)S(1)} %get-tuple-element.152), channel_id=1, source_target_pairs={{0,8},{8,16},{16,24},{24,0},{1,9},{9,17},{17,25},{25,1},{2,10},{10... | collective-permute-start | bytes 786440 | tf_op jit(solution)/shard_map/ppermute | solution.py:66
  573.5 194.7 %reduce-scatter.6.cloned.1.call-start = ((), (), s32[]{:S(2)}) async-start(), calls=%async_computation.9 | async-start | bytes 5242880 | tf_op jit(solution)/shard_map/reduce_scatter | solution.py:469
  600.2 36.8 %collective-permute-start.54 = (bf16[1024,2048]{1,0:T(8,128)(2,1)}, bf16[1024,2048]{1,0:T(8,128)(2,1)}, u32[]{:S(2)}, u32[]{:S(2)}) collective-permute-start(bf16[1024,2048]{1,0:T(8,128)(2,1)} %convolution_convert_fusion), channel_id=1, source_target_pairs={{0,1},{1,0},{2,3},{3,2},{4,5},{5,4},{6,7},{7,6},{8,9},{9,8},{10,11... | collective-permute-start | bytes 12582920 | tf_op jit(solution)/shard_map/ppermute | solution.py:17
  604.4 25.5 %collective-permute-start.90 = (bf16[512,512]{1,0:T(8,128)(2,1)}, bf16[512,512]{1,0:T(8,128)(2,1)S(1)}, u32[]{:S(2)}, u32[]{:S(2)}) collective-permute-start(bf16[512,512]{1,0:T(8,128)(2,1)} %reduce-scatter.14.cloned.1.call-done), channel_id=1, source_target_pairs={{0,2},{2,0},{4,6},{6,4},{1,3},{3,1},{5,7},{7,5},{8,10},{10,8},{12,... | collective-permute-start | bytes 1572872 | tf_op jit(solution)/shard_map/ppermute | solution.py:21
  629.2 35.0 %collective-permute-start.93 = (bf16[256,512]{1,0:T(8,128)(2,1)S(1)}, bf16[256,512]{1,0:T(8,128)(2,1)}, u32[]{:S(2)}, u32[]{:S(2)}) collective-permute-start(bf16[256,512]{1,0:T(8,128)(2,1)S(1)} %slice.540), channel_id=1, source_target_pairs={{0,2},{2,0},{4,6},{6,4},{1,3},{3,1},{5,7},{7,5},{8,10},{10,8},{12,... | collective-permute-start | bytes 786440 | tf_op jit(solution)/shard_map/ppermute | solution.py:21
  630.6 34.1 %collective-permute-start.92 = (bf16[256,512]{1,0:T(8,128)(2,1)}, bf16[256,512]{1,0:T(8,128)(2,1)}, u32[]{:S(2)}, u32[]{:S(2)}) collective-permute-start(bf16[256,512]{1,0:T(8,128)(2,1)} %slice.539), channel_id=1, source_target_pairs={{0,4},{2,6},{4,0},{6,2},{1,5},{3,7},{5,1},{7,3},{8,12},{10,14},{12... | collective-permute-start | bytes 786440 | tf_op jit(solution)/shard_map/ppermute | solution.py:21
  661.9 38.7 %collective-permute-start.58 = (bf16[256,2048]{1,0:T(8,128)(2,1)}, bf16[256,2048]{1,0:T(8,128)(2,1)}, u32[]{:S(2)}, u32[]{:S(2)}) collective-permute-start(bf16[256,2048]{1,0:T(8,128)(2,1)} %pad_maximum_fusion.16), channel_id=1, source_target_pairs={{0,4},{2,6},{4,0},{6,2},{1,5},{3,7},{5,1},{7,3},{8,12},{10,14},{12... | collective-permute-start | bytes 3145736 | tf_op jit(solution)/shard_map/ppermute | solution.py:21
  664.2 36.4 %collective-permute-start.56 = (bf16[256,2048]{1,0:T(8,128)(2,1)}, bf16[256,2048]{1,0:T(8,128)(2,1)}, u32[]{:S(2)}, u32[]{:S(2)}) collective-permute-start(bf16[256,2048]{1,0:T(8,128)(2,1)} %pad_maximum_fusion.15), channel_id=1, source_target_pairs={{0,2},{2,0},{4,6},{6,4},{1,3},{3,1},{5,7},{7,5},{8,10},{10,8},{12,... | collective-permute-start | bytes 3145736 | tf_op jit(solution)/shard_map/ppermute | solution.py:21
  673.3 23.7 %collective-permute-start.78 = (bf16[256,512]{1,0:T(8,128)(2,1)S(1)}, bf16[256,512]{1,0:T(8,128)(2,1)S(1)}, u32[]{:S(2)}, u32[]{:S(2)}) collective-permute-start(bf16[256,512]{1,0:T(8,128)(2,1)S(1)} %slice.528), channel_id=1, source_target_pairs={{0,2},{2,0},{4,6},{6,4},{1,3},{3,1},{5,7},{7,5},{8,10},{10,8},{12,... | collective-permute-start | bytes 786440 | tf_op jit(solution)/shard_map/ppermute | solution.py:21
  673.9 24.3 %collective-permute-start.77 = (bf16[256,512]{1,0:T(8,128)(2,1)S(1)}, bf16[256,512]{1,0:T(8,128)(2,1)S(1)}, u32[]{:S(2)}, u32[]{:S(2)}) collective-permute-start(bf16[256,512]{1,0:T(8,128)(2,1)S(1)} %slice.527), channel_id=1, source_target_pairs={{0,4},{2,6},{4,0},{6,2},{1,5},{3,7},{5,1},{7,3},{8,12},{10,14},{12... | collective-permute-start | bytes 786440 | tf_op jit(solution)/shard_map/ppermute | solution.py:21
  711.2 47.9 %collective-permute-start.83 = (bf16[256,512]{1,0:T(8,128)(2,1)S(1)}, bf16[256,512]{1,0:T(8,128)(2,1)S(1)}, u32[]{:S(2)}, u32[]{:S(2)}) collective-permute-start(bf16[256,512]{1,0:T(8,128)(2,1)S(1)} %slice.532), channel_id=1, source_target_pairs={{0,2},{2,0},{4,6},{6,4},{1,3},{3,1},{5,7},{7,5},{8,10},{10,8},{12,... | collective-permute-start | bytes 786440 | tf_op jit(solution)/shard_map/ppermute | solution.py:21
  712.7 46.4 %collective-permute-start.82 = (bf16[256,512]{1,0:T(8,128)(2,1)S(1)}, bf16[256,512]{1,0:T(8,128)(2,1)S(1)}, u32[]{:S(2)}, u32[]{:S(2)}) collective-permute-start(bf16[256,512]{1,0:T(8,128)(2,1)S(1)} %slice.531), channel_id=1, source_target_pairs={{0,4},{2,6},{4,0},{6,2},{1,5},{3,7},{5,1},{7,3},{8,12},{10,14},{12... | collective-permute-start | bytes 786440 | tf_op jit(solution)/shard_map/ppermute | solution.py:21
  768.9 23.7 %collective-permute-start.72 = (bf16[512,1024]{1,0:T(8,128)(2,1)}, bf16[512,1024]{1,0:T(8,128)(2,1)S(1)}, u32[]{:S(2)}, u32[]{:S(2)}) collective-permute-start(bf16[512,1024]{1,0:T(8,128)(2,1)} %reduce-scatter.6.cloned.1.call-done), channel_id=1, source_target_pairs={{0,4},{2,6},{4,0},{6,2},{1,5},{3,7},{5,1},{7,3},{8,12},{10,14},{12... | collective-permute-start | bytes 3145736 | tf_op jit(solution)/shard_map/ppermute | solution.py:21
  (104 other events, 1409.0 us)
Sparse Core Ops, SparseCore 0:
  11.2 143.0 all-gather.4
  156.4 44.2 all-gather.6
  228.6 48.9 all-gather.8
  279.6 44.6 all-gather.10
  390.1 43.8 reduce-scatter.11
  443.9 45.0 reduce-scatter.13
  501.0 48.0 reduce-scatter.7
  573.6 41.9 reduce-scatter.9
  618.5 76.0 reduce-scatter.5

commit v4 on v3

--- a/solution.py
+++ b/solution.py
@@ -26,9 +26,11 @@
 
 
 def spread(piece):
-    middle = piece.shape[0] // 2
-    first = swap_batch(piece, 1)
-    second = swap_batch(piece, 2)
+    return relay(swap_batch(piece, 1), swap_batch(piece, 2))
+
+
+def relay(first, second):
+    middle = first.shape[0] // 2
     upper = swap_batch(first[:middle], 2)
     lower = swap_batch(second[middle:], 1)
     return first, second, jnp.concatenate([upper, lower], axis=0)
@@ -424,16 +426,17 @@
             result = lax.dynamic_update_slice_in_dim(result, moved, (block - steps) % 4, 0)
         return result
 
-    def give_back(value, dtype):
-        if not within:
-            return both_rows(value, swap_core(value)).astype(dtype)
+    def send_back(value):
         value = value.reshape(4, size, width)
-        held = jnp.zeros((4, size, width), value.dtype)
-        for steps in range(4):
-            moved = lax.dynamic_index_in_dim(value, (block - steps) % 4, 0, True)
-            if steps:
-                moved = turn(moved, -steps)
-            held = lax.dynamic_update_slice_in_dim(held, moved, (block + steps) % 4, 0)
+        parts = [
+            lax.dynamic_index_in_dim(value, (block - steps) % 4, 0, True) for steps in range(4)
+        ]
+        return parts[:1] + [turn(parts[steps], -steps) for steps in (1, 2, 3)]
+
+    def place_back(parts, dtype):
+        held = jnp.zeros((4, size, width), parts[0].dtype)
+        for steps, part in enumerate(parts):
+            held = lax.dynamic_update_slice_in_dim(held, part, (block + steps) % 4, 0)
         own = []
         for slot in range(4):
             moved = lax.dynamic_index_in_dim(held, place ^ slot, 0, False)
@@ -668,7 +671,10 @@
 
     expanded = fold(slot_products(dot, after(active, grad_branch), reduce_both))
     output_rows = (residual + expanded + outputbias).astype(BF16)
-    layer_output = give_back(output_rows, BF16)
+    if within:
+        layer_output = place_back(send_back(output_rows), BF16)
+    else:
+        layer_output = both_rows(output_rows, swap_core(output_rows))
 
     grad_gated_both = contract_cols(grad_branch, output_both).astype(BF16)
     grad_gated_own = grad_gated_both[:, :VAL].reshape(segment.shape[1:] + (VAL,))
@@ -731,7 +737,15 @@
     grad_rows = grad_residual + inverse * (
         grad_scaled - scaled * jnp.mean(grad_scaled * scaled, axis=-1, keepdims=True)
     )
-    tokens_grad = give_back(grad_rows.astype(BF16) if within else grad_rows, F32)
+    grad_rows, first_grad = lax.optimization_barrier((grad_rows, first_grad))
+    first_near = swap_batch(first_grad, 1), swap_batch(first_grad, 2)
+    if within:
+        parts = send_back(grad_rows.astype(BF16))
+        *parts, first, second = lax.optimization_barrier(tuple(parts) + first_near)
+        first_near = first, second
+        tokens_grad = place_back(parts, F32)
+    else:
+        tokens_grad = both_rows(grad_rows, swap_core(grad_rows))
 
     by_width = [prescale_grad, postscale_grad, postshift_grad, outputbias_grad]
     over_cores = swap_core(jnp.concatenate([hiddenbias_grad[part:]] + by_width))
@@ -753,7 +767,7 @@
     expand_pieces = all_pieces(expand_grad)
     output_pieces = all_pieces(output_grad)
     gate_pieces = all_pieces(gate_grad)
-    first_pieces = all_pieces(first_grad)
+    first_pieces = (first_grad,) + relay(*first_near)
     return (
         layer_output[None],
         tokens_grad[None],

time: 822 us -> 810 us (0.985)
  other arithmetic: 74.7 us -> 65.3 us
    unnamed x128 -> x130, local copies, waits for them, and re-layouts: 44.3 us -> 45.3 us
  transfers between devices with their start and end apart: 103 -> 103, of which waited for: 50 -> 53; matrix products, arithmetic and copies ran while one was open for 32% -> 31% of each run, Pallas kernels for 5% -> 5%
where the time goes in v4:
time: 810 us; the launch traced here: 800 us
  waiting for transfers between devices  359 us (44%)
  matrix products  111 us (14%)
  local copies, waits for them, and re-layouts  104 us (13%)
  starting transfers between devices  102 us (13%)
  other arithmetic  65.3 us (8%)
  Pallas kernels  43 us (5%)
  between operations  16 us (2%)
    ppermute x61, waiting for transfers between devices, swap_batch(): lax.ppermute(value, 'batch', [(place, place ^ mask) for place in range(4)])  217 us
    ppermute x12, waiting for transfers between devices, turn(): lax.ppermute(value, 'seq', [(source, (source + steps) % count) for source...  93.1 us
    ppermute x61, starting transfers between devices, swap_batch(): lax.ppermute(value, 'batch', [(place, place ^ mask) for place in range(4)])  65.5 us
    dot_general x8, matrix products, contract_cols(): lax.dot_general(left, right, (((1,), (1,)), ((), ())), preferred_element_...  45.5 us
    unnamed x130, local copies, waits for them, and re-layouts  45.3 us
    dot_general x5, matrix products, contract_rows(): lax.dot_general(left, right, (((0,), (0,)), ((), ())), preferred_element_...  43.7 us
    pallas_call x2, Pallas kernels, by_block(): pl.pallas_call(kernel, grid=(4,), in_specs=[block_spec(v, at in shared, l...  43 us
    all_gather x2, waiting for transfers between devices, gather_cols(): return lax.all_gather(weight, 'seq', axis=1, tiled=True)  28 us
  transfers between devices with their start and end apart: 103, of which 53 were waited for; matrix products, arithmetic and copies ran while one was open for 31% of the time, Pallas kernels for 5%

profile of v4, /device:TPU:0, one launch (start us, length us, event | category | flops | bytes accessed | tf_op | source)
XLA Modules:
  0.0 800.1 jit_solution(8202099510139404877)
XLA Ops:
  15.0 3.9 collective-permute-start.2
  23.7 9.0 %collective-permute-done.2 = bf16[136,2048]{1,0:T(8,128)(2,1)S(1)} collective-permute-done((bf16[136,2048]{1,0:T(8,128)(2,1)}, bf16[136,2048]{1,0:T(8,128)(2,1)S(1)}, u32[]{:S(2)}, u32[]{:S(2)}) %collective-permute-start.2) | collective-permute-done | bytes 557088 | tf_op jit(solution)/shard_map/ppermute | solution.py:21
  32.6 11.2 %collective-permute-done.1 = bf16[136,2048]{1,0:T(8,128)(2,1)} collective-permute-done((bf16[136,2048]{1,0:T(8,128)(2,1)}, bf16[136,2048]{1,0:T(8,128)(2,1)}, u32[]{:S(2)}, u32[]{:S(2)}) %collective-permute-start.1) | collective-permute-done | bytes 557088 | tf_op jit(solution)/shard_map/ppermute | solution.py:21
  51.6 12.4 %collective-permute-done.3 = bf16[1,72,2048]{2,1,0:T(8,128)(2,1)S(1)} collective-permute-done((bf16[1,72,2048]{2,1,0:T(8,128)(2,1)S(1)}, bf16[1,72,2048]{2,1,0:T(8,128)(2,1)S(1)}, u32[]{:S(2)}, u32[]{:S(2)}) %collective-permute-start.3) | collective-permute-done | bytes 294944 | tf_op jit(solution)/shard_map/ppermute | solution.py:68
  64.0 21.0 %collective-permute-done.4 = bf16[1,72,2048]{2,1,0:T(8,128)(2,1)S(1)} collective-permute-done((bf16[1,72,2048]{2,1,0:T(8,128)(2,1)S(1)}, bf16[1,72,2048]{2,1,0:T(8,128)(2,1)S(1)}, u32[]{:S(2)}, u32[]{:S(2)}) %collective-permute-start.4) | collective-permute-done | bytes 294944 | tf_op jit(solution)/shard_map/ppermute | solution.py:68
  94.1 18.3 %collective-permute-done.6 = bf16[256,2048]{1,0:T(8,128)(2,1)} collective-permute-done((bf16[256,2048]{1,0:T(8,128)(2,1)}, bf16[256,2048]{1,0:T(8,128)(2,1)}, u32[]{:S(2)}, u32[]{:S(2)}) %collective-permute-start.6) | collective-permute-done | bytes 1048608 | tf_op jit(solution)/shard_map/ppermute | solution.py:21
  121.2 4.3 collective-permute-done.8
  131.6 5.5 multiply_sine_fusion
  147.9 6.3 all-gather.5.cloned.1.call-done.weight
  154.3 24.4 %shard_map.297 = (bf16[2,4,4,64,256]{4,3,2,1,0:T(8,128)(2,1)}, bf16[2,4,4,64,256]{4,3,2,1,0:T(8,128)(2,1)}, bf16[2,4,4,64,512]{4,3,2,1,0:T(8,128)(2,1)}, bf16[4,...) custom-call(bf16[2,4,4,64,2048]{4,3,2,1,0:T(8,128)(2,1)} %bitcast.13, ...), custom_call_target="tpu_custom_call" | custom-call | tf_op jit(solution)/shard_map/pallas_call | solution.py:328
  187.4 13.3 %all-gather.7.cloned.1.call-done = bf16[512,2048]{1,0:T(8,128)(2,1)} async-done(((bf16[512,512]{1,0:T(8,128)(2,1)}), bf16[512,2048]{1,0:T(8,128)(2,1)}) %all-gather.7.cloned.1.call-update) | async-done | bytes 2097168 | tf_op jit(solution)/shard_map/all_gather | solution.py:469
  202.1 6.9 collective-permute-start.27
  211.3 4.4 collective-permute-done.26
  215.7 10.9 %collective-permute-done.27 = bf16[1,64,2048]{2,1,0:T(8,128)(2,1)S(1)} collective-permute-done((bf16[1,64,2048]{2,1,0:T(8,128)(2,1)S(1)}, bf16[1,64,2048]{2,1,0:T(8,128)(2,1)S(1)}, u32[]{:S(2)}, u32[]{:S(2)}) %collective-permute-start.27) | collective-permute-done | bytes 262176 | tf_op jit(solution)/shard_map/ppermute | solution.py:68
  228.5 10.4 %all-gather.11.cloned.1.call-start = ((), (), s32[]{:S(2)}) async-start(), calls=%async_computation.8 | async-start | bytes 2621440 | tf_op jit(solution)/shard_map/all_gather | solution.py:469
  250.4 12.7 %collective-permute-done.16 = bf16[128,2048]{1,0:T(8,128)(2,1)S(1)} collective-permute-done((bf16[128,2048]{1,0:T(8,128)(2,1)S(1)}, bf16[128,2048]{1,0:T(8,128)(2,1)S(1)}, u32[]{:S(2)}, u32[]{:S(2)}) %collective-permute-start.16) | collective-permute-done | bytes 524320 | tf_op jit(solution)/shard_map/ppermute | solution.py:21
  276.9 13.9 %collective-permute-done.19 = bf16[256,2048]{1,0:T(8,128)(2,1)} collective-permute-done((bf16[256,2048]{1,0:T(8,128)(2,1)}, bf16[256,2048]{1,0:T(8,128)(2,1)}, u32[]{:S(2)}, u32[]{:S(2)}) %collective-permute-start.19) | collective-permute-done | bytes 1048608 | tf_op jit(solution)/shard_map/ppermute | solution.py:21
  309.6 14.7 %all-gather.11.cloned.1.call-done = bf16[512,2048]{1,0:T(8,128)(2,1)} async-done(((bf16[512,512]{1,0:T(8,128)(2,1)}), bf16[512,2048]{1,0:T(8,128)(2,1)}) %all-gather.11.cloned.1.call-update) | async-done | bytes 2097168 | tf_op jit(solution)/shard_map/all_gather | solution.py:469
  334.6 6.7 collective-permute-done.22
  346.7 6.1 multiply_convert_fusion
  353.0 9.5 %convert_reduce_fusion = (f32[1024]{0:T(1024)S(1)}, bf16[1024,1024]{1,0:T(8,128)(2,1)S(1)}) fusion(f32[1024,1024]{1,0:T(8,128)S(1)} %get-tuple-element.228, f32[1024]{0:T(1024)S(1)} %pad_maximum_fusion.19, bf16[1024,2048]{1,0:T(8,128)(2,1)} %constant_dynamic-update-slice_fusion.25, bf16[1024,2048]{1,0:T(8,128)(2,1)S(1)} %constant_dynamic-update-slice_fusion.30), kind=kOutput, calls=%fused_computation.20 | convolution fusion | flops 4308597760 | bytes 14688256 | tf_op jit(solution)/shard_map/dot_general | solution.py:101
  363.9 4.6 fusion.95
  373.6 8.6 %collective-permute-done.34 = bf16[128,2048]{1,0:T(8,128)(2,1)S(1)} collective-permute-done((bf16[128,2048]{1,0:T(8,128)(2,1)S(1)}, bf16[128,2048]{1,0:T(8,128)(2,1)S(1)}, u32[]{:S(2)}, u32[]{:S(2)}) %collective-permute-start.34) | collective-permute-done | bytes 524320 | tf_op jit(solution)/shard_map/ppermute | solution.py:21
  390.1 7.5 fusion.96
  398.0 9.7 %collective-permute-done.37 = bf16[256,2048]{1,0:T(8,128)(2,1)} collective-permute-done((bf16[256,2048]{1,0:T(8,128)(2,1)}, bf16[256,2048]{1,0:T(8,128)(2,1)}, u32[]{:S(2)}, u32[]{:S(2)}) %collective-permute-start.37) | collective-permute-done | bytes 1048608 | tf_op jit(solution)/shard_map/ppermute | solution.py:21
  409.9 3.9 multiply_reduce_fusion
  418.7 20.6 %collective-permute-done.38 = bf16[256,2048]{1,0:T(8,128)(2,1)S(1)} collective-permute-done((bf16[256,2048]{1,0:T(8,128)(2,1)}, bf16[256,2048]{1,0:T(8,128)(2,1)S(1)}, u32[]{:S(2)}, u32[]{:S(2)}) %collective-permute-start.38) | collective-permute-done | bytes 1048608 | tf_op jit(solution)/shard_map/ppermute | solution.py:21
  460.3 4.9 convolution_convert_fusion.5
  472.2 18.6 %shard_map.298 = (bf16[2,4,4,64,1536]{4,3,2,1,0:T(8,128)(2,1)}, f32[2,512]{1,0:T(2,128)}) custom-call(bf16[4,4,64,512]{3,2,1,0:T(8,128)(2,1)} %bitcast.113, bf16[4,4,64,512]{3,2,1,0:T(8,128)(2,1)} %bitcast.118, f32[2,4,4,64,512]{4,3,2,1,0:T(8,128)} %get-tuple-element.82.gate, f32[2,4,4,64,512]{4,3,2,1,0:T(8,128)} %get-tuple-element.83.unit, ...), custom_call_target="tpu_custom_call" | custom-call | tf_op jit(solution)/shard_map/pallas_call | solution.py:328
  490.8 10.0 %convolution_convert_fusion.1 = bf16[2048,512]{1,0:T(8,128)(2,1)} fusion(bf16[2048,2048]{1,0:T(8,128)(2,1)} %constant_dynamic-update-slice_fusion.2, bf16[2048,1536]{1,0:T(8,128)(2,1)} %bitcast.141), kind=kOutput, calls=%fused_computation.26 | convolution fusion | flops 4296015872 | bytes 12582912 | tf_op jit(solution)/shard_map/dot_general | solution.py:97
  507.6 7.1 fusion.75
  515.1 14.0 %collective-permute-done.45 = bf16[256,2048]{1,0:T(8,128)(2,1)} collective-permute-done((bf16[256,2048]{1,0:T(8,128)(2,1)}, bf16[256,2048]{1,0:T(8,128)(2,1)}, u32[]{:S(2)}, u32[]{:S(2)}) %collective-permute-start.45) | collective-permute-done | bytes 1048608 | tf_op jit(solution)/shard_map/ppermute | solution.py:21
  536.9 4.2 collective-permute-start.47
  541.1 7.8 collective-permute-done.46
  549.0 17.8 %collective-permute-done.47 = bf16[1,64,2048]{2,1,0:T(8,128)(2,1)S(1)} collective-permute-done((bf16[1,64,2048]{2,1,0:T(8,128)(2,1)S(1)}, bf16[1,64,2048]{2,1,0:T(8,128)(2,1)S(1)}, u32[]{:S(2)}, u32[]{:S(2)}) %collective-permute-start.47) | collective-permute-done | bytes 262176 | tf_op jit(solution)/shard_map/ppermute | solution.py:68
  573.6 14.4 %fusion.11 = bf16[2048,1024]{1,0:T(8,128)(2,1)} fusion(bf16[2048,2048]{1,0:T(8,128)(2,1)} %constant_dynamic-update-slice_fusion.2, bf16[2048,1536]{1,0:T(8,128)(2,1)} %bitcast.142), kind=kOutput, calls=%fused_computation.24 | convolution fusion | flops 8592031744 | bytes 16777216 | tf_op jit(solution)/shard_map/dot_general | solution.py:97
  589.1 11.1 %convolution_convert_fusion = bf16[1024,2048]{1,0:T(8,128)(2,1)} fusion(bf16[2048,1536]{1,0:T(8,128)(2,1)} %all-gather.5.cloned.1.call-done.weight, bf16[2048,1536]{1,0:T(8,128)(2,1)} %bitcast.143), kind=kOutput, calls=%fused_computation.23 | convolution fusion | flops 6444548096 | bytes 13631488 | tf_op jit(solution)/shard_map/dot_general | solution.py:101
  611.1 6.9 collective-permute-done.86
  620.1 9.1 %collective-permute-done.91 = bf16[512,512]{1,0:T(8,128)(2,1)S(1)} collective-permute-done((bf16[512,512]{1,0:T(8,128)(2,1)S(1)}, bf16[512,512]{1,0:T(8,128)(2,1)S(1)}, u32[]{:S(2)}, u32[]{:S(2)}) %collective-permute-start.91) | collective-permute-done | bytes 524320 | tf_op jit(solution)/shard_map/ppermute | solution.py:21
  642.0 3.8 convert_element_type.356
  650.9 9.3 %fusion.94 = (bf16[768,2048]{1,0:T(8,128)(2,1)}, f32[768,2048]{1,0:T(8,128)}) fusion(f32[1024,2048]{1,0:T(8,128)S(1)} %convert_element_type.356, bf16[2048,1536]{1,0:T(8,128)(2,1)S(1)} %bitcast.111, bf16[2048,1536]{1,0:T(8,128)(2,1)} %bitcast.145), kind=kOutput, calls=%fused_computation.346 | convolution fusion | flops 4834983936 | bytes 24379392 | tf_op jit(solution)/shard_map/dot_general | solution.py:101
  680.8 23.2 %collective-permute-done.78 = bf16[256,512]{1,0:T(8,128)(2,1)S(1)} collective-permute-done((bf16[256,512]{1,0:T(8,128)(2,1)S(1)}, bf16[256,512]{1,0:T(8,128)(2,1)S(1)}, u32[]{:S(2)}, u32[]{:S(2)}) %collective-permute-start.78) | collective-permute-done | bytes 262176 | tf_op jit(solution)/shard_map/ppermute | solution.py:21
  711.5 4.3 collective-permute-done.81
  735.6 3.9 collective-permute-done.72
  746.9 6.9 collective-permute-done.59
  753.8 10.7 %collective-permute-done.60 = bf16[1,64,2048]{2,1,0:T(8,128)(2,1)S(1)} collective-permute-done((bf16[1,64,2048]{2,1,0:T(8,128)(2,1)S(1)}, bf16[1,64,2048]{2,1,0:T(8,128)(2,1)S(1)}, u32[]{:S(2)}, u32[]{:S(2)}) %collective-permute-start.60) | collective-permute-done | bytes 262176 | tf_op jit(solution)/shard_map/ppermute | solution.py:68
  770.5 5.2 collective-permute-done.66
  781.0 7.6 collective-permute-done.73
  (542 shorter events, 302.7 us)
Async XLA Ops:
  7.2 147.0 %all-gather.5.cloned.1.call-start = ((), (), s32[]{:S(2)}) async-start(), calls=%async_computation.5 | async-start | bytes 7864320 | tf_op jit(solution)/shard_map/all_gather | solution.py:466
  11.0 189.6 %all-gather.7.cloned.1.call-start = ((), (), s32[]{:S(2)}) async-start(), calls=%async_computation.6 | async-start | bytes 2621440 | tf_op jit(solution)/shard_map/all_gather | solution.py:469
  18.9 24.9 %collective-permute-start.1 = (bf16[136,2048]{1,0:T(8,128)(2,1)}, bf16[136,2048]{1,0:T(8,128)(2,1)}, u32[]{:S(2)}, u32[]{:S(2)}) collective-permute-start(bf16[136,2048]{1,0:T(8,128)(2,1)} %get-tuple-element.197), channel_id=1, source_target_pairs={{0,4},{2,6},{4,0},{6,2},{1,5},{3,7},{5,1},{7,3},{8,12},{10,14},{12... | collective-permute-start | bytes 1671176 | tf_op jit(solution)/shard_map/ppermute | solution.py:21
  19.4 24.7 %collective-permute-start = (bf16[136,2048]{1,0:T(8,128)(2,1)}, bf16[136,2048]{1,0:T(8,128)(2,1)}, u32[]{:S(2)}, u32[]{:S(2)}) collective-permute-start(bf16[136,2048]{1,0:T(8,128)(2,1)} %get-tuple-element.196), channel_id=1, source_target_pairs={{0,2},{2,0},{4,6},{6,4},{1,3},{3,1},{5,7},{7,5},{8,10},{10,8},{12,... | collective-permute-start | bytes 1671176 | tf_op jit(solution)/shard_map/ppermute | solution.py:21
  47.6 37.4 %collective-permute-start.4 = (bf16[1,72,2048]{2,1,0:T(8,128)(2,1)S(1)}, bf16[1,72,2048]{2,1,0:T(8,128)(2,1)S(1)}, u32[]{:S(2)}, u32[]{:S(2)}) collective-permute-start(bf16[1,72,2048]{2,1,0:T(8,128)(2,1)S(1)} %get-tuple-element.145), channel_id=1, source_target_pairs={{0,16},{8,24},{16,0},{24,8},{1,17},{9,25},{17,1},{25,9},{2,18},{10... | collective-permute-start | bytes 884744 | tf_op jit(solution)/shard_map/ppermute | solution.py:68
  50.2 36.0 %collective-permute-start.5 = (bf16[1,72,2048]{2,1,0:T(8,128)(2,1)S(1)}, bf16[1,72,2048]{2,1,0:T(8,128)(2,1)S(1)}, u32[]{:S(2)}, u32[]{:S(2)}) collective-permute-start(bf16[1,72,2048]{2,1,0:T(8,128)(2,1)S(1)} %get-tuple-element.144), channel_id=1, source_target_pairs={{0,24},{8,0},{16,8},{24,16},{1,25},{9,1},{17,9},{25,17},{2,26},{10... | collective-permute-start | bytes 884744 | tf_op jit(solution)/shard_map/ppermute | solution.py:68
  87.9 24.5 %collective-permute-start.6 = (bf16[256,2048]{1,0:T(8,128)(2,1)}, bf16[256,2048]{1,0:T(8,128)(2,1)}, u32[]{:S(2)}, u32[]{:S(2)}) collective-permute-start(bf16[256,2048]{1,0:T(8,128)(2,1)} %multiply_convert_fusion.1), channel_id=1, source_target_pairs={{0,2},{2,0},{4,6},{6,4},{1,3},{3,1},{5,7},{7,5},{8,10},{10,8},{12,... | collective-permute-start | bytes 3145736 | tf_op jit(solution)/shard_map/ppermute | solution.py:21
  89.4 25.7 %collective-permute-start.7 = (bf16[256,2048]{1,0:T(8,128)(2,1)}, bf16[256,2048]{1,0:T(8,128)(2,1)}, u32[]{:S(2)}, u32[]{:S(2)}) collective-permute-start(bf16[256,2048]{1,0:T(8,128)(2,1)} %multiply_convert_fusion.1), channel_id=1, source_target_pairs={{0,4},{2,6},{4,0},{6,2},{1,5},{3,7},{5,1},{7,3},{8,12},{10,14},{12... | collective-permute-start | bytes 3145736 | tf_op jit(solution)/shard_map/ppermute | solution.py:21
  89.9 48.6 %collective-permute-start.10 = (bf16[256,2048]{1,0:T(8,128)(2,1)}, bf16[256,2048]{1,0:T(8,128)(2,1)}, u32[]{:S(2)}, u32[]{:S(2)}) collective-permute-start(bf16[256,2048]{1,0:T(8,128)(2,1)} %multiply_convert_fusion.1), channel_id=1, source_target_pairs={{0,1},{1,0},{2,3},{3,2},{4,5},{5,4},{6,7},{7,6},{8,9},{9,8},{10,11... | collective-permute-start | bytes 3145736 | tf_op jit(solution)/shard_map/ppermute | solution.py:17
  116.5 24.3 %collective-permute-start.11 = (bf16[256,2048]{1,0:T(8,128)(2,1)}, bf16[256,2048]{1,0:T(8,128)(2,1)}, u32[]{:S(2)}, u32[]{:S(2)}) collective-permute-start(bf16[256,2048]{1,0:T(8,128)(2,1)} %collective-permute-done.6), channel_id=1, source_target_pairs={{0,1},{1,0},{2,3},{3,2},{4,5},{5,4},{6,7},{7,6},{8,9},{9,8},{10,11... | collective-permute-start | bytes 3145736 | tf_op jit(solution)/shard_map/ppermute | solution.py:17
  130.0 173.5 %all-gather.9.cloned.1.call-start = ((), (), s32[]{:S(2)}) async-start(), calls=%async_computation.7 | async-start | bytes 2621440 | tf_op jit(solution)/shard_map/all_gather | solution.py:466
  200.7 40.0 %collective-permute-start.15 = (bf16[512,2048]{1,0:T(8,128)(2,1)}, bf16[512,2048]{1,0:T(8,128)(2,1)}, u32[]{:S(2)}, u32[]{:S(2)}) collective-permute-start(bf16[512,2048]{1,0:T(8,128)(2,1)} %all-gather.7.cloned.1.call-done), channel_id=1, source_target_pairs={{0,1},{1,0},{2,3},{3,2},{4,5},{5,4},{6,7},{7,6},{8,9},{9,8},{10,11... | collective-permute-start | bytes 6291464 | tf_op jit(solution)/shard_map/ppermute | solution.py:17
  202.1 24.4 %collective-permute-start.27 = (bf16[1,64,2048]{2,1,0:T(8,128)(2,1)S(1)}, bf16[1,64,2048]{2,1,0:T(8,128)(2,1)S(1)}, u32[]{:S(2)}, u32[]{:S(2)}) collective-permute-start(bf16[1,64,2048]{2,1,0:T(8,128)(2,1)S(1)} %get-tuple-element.177), channel_id=1, source_target_pairs={{0,16},{8,24},{16,0},{24,8},{1,17},{9,25},{17,1},{25,9},{2,18},{10... | collective-permute-start | bytes 786440 | tf_op jit(solution)/shard_map/ppermute | solution.py:68
  226.6 44.1 %collective-permute-start.29 = (bf16[256,2048]{1,0:T(8,128)(2,1)S(1)}, bf16[256,2048]{1,0:T(8,128)(2,1)}, u32[]{:S(2)}, u32[]{:S(2)}) collective-permute-start(bf16[256,2048]{1,0:T(8,128)(2,1)S(1)} %bitcast.106), channel_id=1, source_target_pairs={{0,2},{2,0},{4,6},{6,4},{1,3},{3,1},{5,7},{7,5},{8,10},{10,8},{12,... | collective-permute-start | bytes 3145736 | tf_op jit(solution)/shard_map/ppermute | solution.py:21
  226.9 47.8 %collective-permute-start.30 = (bf16[256,2048]{1,0:T(8,128)(2,1)S(1)}, bf16[256,2048]{1,0:T(8,128)(2,1)}, u32[]{:S(2)}, u32[]{:S(2)}) collective-permute-start(bf16[256,2048]{1,0:T(8,128)(2,1)S(1)} %bitcast.107), channel_id=1, source_target_pairs={{0,4},{2,6},{4,0},{6,2},{1,5},{3,7},{5,1},{7,3},{8,12},{10,14},{12... | collective-permute-start | bytes 3145736 | tf_op jit(solution)/shard_map/ppermute | solution.py:21
  228.5 95.8 %all-gather.11.cloned.1.call-start = ((), (), s32[]{:S(2)}) async-start(), calls=%async_computation.8 | async-start | bytes 2621440 | tf_op jit(solution)/shard_map/all_gather | solution.py:469
  264.4 26.4 %collective-permute-start.19 = (bf16[256,2048]{1,0:T(8,128)(2,1)}, bf16[256,2048]{1,0:T(8,128)(2,1)}, u32[]{:S(2)}, u32[]{:S(2)}) collective-permute-start(bf16[256,2048]{1,0:T(8,128)(2,1)} %pad_maximum_fusion.9), channel_id=1, source_target_pairs={{0,4},{2,6},{4,0},{6,2},{1,5},{3,7},{5,1},{7,3},{8,12},{10,14},{12... | collective-permute-start | bytes 3145736 | tf_op jit(solution)/shard_map/ppermute | solution.py:21
  266.9 26.4 %collective-permute-start.17 = (bf16[256,2048]{1,0:T(8,128)(2,1)}, bf16[256,2048]{1,0:T(8,128)(2,1)}, u32[]{:S(2)}, u32[]{:S(2)}) collective-permute-start(bf16[256,2048]{1,0:T(8,128)(2,1)} %pad_maximum_fusion.8), channel_id=1, source_target_pairs={{0,2},{2,0},{4,6},{6,4},{1,3},{3,1},{5,7},{7,5},{8,10},{10,8},{12,... | collective-permute-start | bytes 3145736 | tf_op jit(solution)/shard_map/ppermute | solution.py:21
  269.4 332.1 %reduce-scatter.12.cloned.1.call-start = ((), (), s32[]{:S(2)}) async-start(), calls=%async_computation.12 | async-start | bytes 2621440 | tf_op jit(solution)/shard_map/reduce_scatter | solution.py:472
  272.9 32.9 %collective-permute-start.31 = (bf16[128,2048]{1,0:T(8,128)(2,1)}, bf16[128,2048]{1,0:T(8,128)(2,1)}, u32[]{:S(2)}, u32[]{:S(2)}) collective-permute-start(bf16[128,2048]{1,0:T(8,128)(2,1)} %slice.477), channel_id=1, source_target_pairs={{0,4},{2,6},{4,0},{6,2},{1,5},{3,7},{5,1},{7,3},{8,12},{10,14},{12... | collective-permute-start | bytes 1572872 | tf_op jit(solution)/shard_map/ppermute | solution.py:21
  276.6 31.1 %collective-permute-start.32 = (bf16[128,2048]{1,0:T(8,128)(2,1)}, bf16[128,2048]{1,0:T(8,128)(2,1)}, u32[]{:S(2)}, u32[]{:S(2)}) collective-permute-start(bf16[128,2048]{1,0:T(8,128)(2,1)} %slice.478), channel_id=1, source_target_pairs={{0,2},{2,0},{4,6},{6,4},{1,3},{3,1},{5,7},{7,5},{8,10},{10,8},{12,... | collective-permute-start | bytes 1572872 | tf_op jit(solution)/shard_map/ppermute | solution.py:21
  298.9 27.4 %collective-permute-start.20 = (bf16[256,2048]{1,0:T(8,128)(2,1)}, bf16[256,2048]{1,0:T(8,128)(2,1)}, u32[]{:S(2)}, u32[]{:S(2)}) collective-permute-start(bf16[256,2048]{1,0:T(8,128)(2,1)} %get-tuple-element.113), channel_id=1, source_target_pairs={{0,2},{2,0},{4,6},{6,4},{1,3},{3,1},{5,7},{7,5},{8,10},{10,8},{12,... | collective-permute-start | bytes 3145736 | tf_op jit(solution)/shard_map/ppermute | solution.py:21
  301.8 27.5 %collective-permute-start.21 = (bf16[256,2048]{1,0:T(8,128)(2,1)}, bf16[256,2048]{1,0:T(8,128)(2,1)}, u32[]{:S(2)}, u32[]{:S(2)}) collective-permute-start(bf16[256,2048]{1,0:T(8,128)(2,1)} %get-tuple-element.113), channel_id=1, source_target_pairs={{0,4},{2,6},{4,0},{6,2},{1,5},{3,7},{5,1},{7,3},{8,12},{10,14},{12... | collective-permute-start | bytes 3145736 | tf_op jit(solution)/shard_map/ppermute | solution.py:21
  303.5 41.3 %collective-permute-start.24 = (bf16[2048,512]{1,0:T(8,128)(2,1)}, bf16[2048,512]{1,0:T(8,128)(2,1)}, u32[]{:S(2)}, u32[]{:S(2)}) collective-permute-start(bf16[2048,512]{1,0:T(8,128)(2,1)} %all-gather.9.cloned.1.call-done), channel_id=1, source_target_pairs={{0,1},{1,0},{2,3},{3,2},{4,5},{5,4},{6,7},{7,6},{8,9},{9,8},{10,11... | collective-permute-start | bytes 6291464 | tf_op jit(solution)/shard_map/ppermute | solution.py:17
  329.2 23.6 %collective-permute-start.33 = (bf16[512,2048]{1,0:T(8,128)(2,1)S(1)}, bf16[512,2048]{1,0:T(8,128)(2,1)S(1)}, u32[]{:S(2)}, u32[]{:S(2)}) collective-permute-start(bf16[512,2048]{1,0:T(8,128)(2,1)S(1)} %copy-done.17), channel_id=1, source_target_pairs={{0,1},{1,0},{2,3},{3,2},{4,5},{5,4},{6,7},{7,6},{8,9},{9,8},{10,11... | collective-permute-start | bytes 6291464 | tf_op jit(solution)/shard_map/ppermute | solution.py:17
  383.8 23.9 %collective-permute-start.37 = (bf16[256,2048]{1,0:T(8,128)(2,1)}, bf16[256,2048]{1,0:T(8,128)(2,1)}, u32[]{:S(2)}, u32[]{:S(2)}) collective-permute-start(bf16[256,2048]{1,0:T(8,128)(2,1)} %pad_maximum_fusion.11), channel_id=1, source_target_pairs={{0,4},{2,6},{4,0},{6,2},{1,5},{3,7},{5,1},{7,3},{8,12},{10,14},{12... | collective-permute-start | bytes 3145736 | tf_op jit(solution)/shard_map/ppermute | solution.py:21
  386.3 23.6 %collective-permute-start.35 = (bf16[256,2048]{1,0:T(8,128)(2,1)}, bf16[256,2048]{1,0:T(8,128)(2,1)}, u32[]{:S(2)}, u32[]{:S(2)}) collective-permute-start(bf16[256,2048]{1,0:T(8,128)(2,1)} %pad_maximum_fusion.10), channel_id=1, source_target_pairs={{0,2},{2,0},{4,6},{6,4},{1,3},{3,1},{5,7},{7,5},{8,10},{10,8},{12,... | collective-permute-start | bytes 3145736 | tf_op jit(solution)/shard_map/ppermute | solution.py:21
  390.0 214.4 %reduce-scatter.14.cloned.1.call-start = ((), (), s32[]{:S(2)}) async-start(), calls=%async_computation.13 | async-start | bytes 2621440 | tf_op jit(solution)/shard_map/reduce_scatter | solution.py:472
  397.9 43.7 %collective-permute-start.89 = (bf16[512,2048]{1,0:T(8,128)(2,1)S(1)}, bf16[512,2048]{1,0:T(8,128)(2,1)S(1)}, u32[]{:S(2)}, u32[]{:S(2)}) collective-permute-start(bf16[512,2048]{1,0:T(8,128)(2,1)S(1)} %slice.656), channel_id=1, source_target_pairs={{0,1},{1,0},{2,3},{3,2},{4,5},{5,4},{6,7},{7,6},{8,9},{9,8},{10,11... | collective-permute-start | bytes 6291464 | tf_op jit(solution)/shard_map/ppermute | solution.py:17
  418.1 25.8 %collective-permute-start.39 = (bf16[256,2048]{1,0:T(8,128)(2,1)}, bf16[256,2048]{1,0:T(8,128)(2,1)}, u32[]{:S(2)}, u32[]{:S(2)}) collective-permute-start(bf16[256,2048]{1,0:T(8,128)(2,1)} %get-tuple-element.111), channel_id=1, source_target_pairs={{0,4},{2,6},{4,0},{6,2},{1,5},{3,7},{5,1},{7,3},{8,12},{10,14},{12... | collective-permute-start | bytes 3145736 | tf_op jit(solution)/shard_map/ppermute | solution.py:21
  443.8 216.5 %reduce-scatter.8.cloned.1.call-start = ((), (), s32[]{:S(2)}) async-start(), calls=%async_computation.10 | async-start | bytes 2621440 | tf_op jit(solution)/shard_map/reduce_scatter | solution.py:472
  500.8 178.4 %reduce-scatter.10.cloned.1.call-start = ((), (), s32[]{:S(2)}) async-start(), calls=%async_computation.11 | async-start | bytes 2621440 | tf_op jit(solution)/shard_map/reduce_scatter | solution.py:472
  503.2 25.9 %collective-permute-start.45 = (bf16[256,2048]{1,0:T(8,128)(2,1)}, bf16[256,2048]{1,0:T(8,128)(2,1)}, u32[]{:S(2)}, u32[]{:S(2)}) collective-permute-start(bf16[256,2048]{1,0:T(8,128)(2,1)} %pad_maximum_fusion.13), channel_id=1, source_target_pairs={{0,4},{2,6},{4,0},{6,2},{1,5},{3,7},{5,1},{7,3},{8,12},{10,14},{12... | collective-permute-start | bytes 3145736 | tf_op jit(solution)/shard_map/ppermute | solution.py:21
  506.2 25.6 %collective-permute-start.43 = (bf16[256,2048]{1,0:T(8,128)(2,1)}, bf16[256,2048]{1,0:T(8,128)(2,1)}, u32[]{:S(2)}, u32[]{:S(2)}) collective-permute-start(bf16[256,2048]{1,0:T(8,128)(2,1)} %pad_maximum_fusion.12), channel_id=1, source_target_pairs={{0,2},{2,0},{4,6},{6,4},{1,3},{3,1},{5,7},{7,5},{8,10},{10,8},{12,... | collective-permute-start | bytes 3145736 | tf_op jit(solution)/shard_map/ppermute | solution.py:21
  515.0 56.4 %collective-permute-start.79 = (bf16[512,2048]{1,0:T(8,128)(2,1)S(1)}, bf16[512,2048]{1,0:T(8,128)(2,1)S(1)}, u32[]{:S(2)}, u32[]{:S(2)}) collective-permute-start(bf16[512,2048]{1,0:T(8,128)(2,1)S(1)} %slice.658), channel_id=1, source_target_pairs={{0,1},{1,0},{2,3},{3,2},{4,5},{5,4},{6,7},{7,6},{8,9},{9,8},{10,11... | collective-permute-start | bytes 6291464 | tf_op jit(solution)/shard_map/ppermute | solution.py:17
  536.9 29.8 %collective-permute-start.47 = (bf16[1,64,2048]{2,1,0:T(8,128)(2,1)S(1)}, bf16[1,64,2048]{2,1,0:T(8,128)(2,1)S(1)}, u32[]{:S(2)}, u32[]{:S(2)}) collective-permute-start(bf16[1,64,2048]{2,1,0:T(8,128)(2,1)S(1)} %get-tuple-element.169), channel_id=1, source_target_pairs={{0,16},{8,24},{16,0},{24,8},{1,17},{9,25},{17,1},{25,9},{2,18},{10... | collective-permute-start | bytes 786440 | tf_op jit(solution)/shard_map/ppermute | solution.py:68
  541.1 25.6 %collective-permute-start.48 = (bf16[1,64,2048]{2,1,0:T(8,128)(2,1)S(1)}, bf16[1,64,2048]{2,1,0:T(8,128)(2,1)S(1)}, u32[]{:S(2)}, u32[]{:S(2)}) collective-permute-start(bf16[1,64,2048]{2,1,0:T(8,128)(2,1)S(1)} %get-tuple-element.168), channel_id=1, source_target_pairs={{0,8},{8,16},{16,24},{24,0},{1,9},{9,17},{17,25},{25,1},{2,10},{10... | collective-permute-start | bytes 786440 | tf_op jit(solution)/shard_map/ppermute | solution.py:68
  573.6 166.1 %reduce-scatter.6.cloned.1.call-start = ((), (), s32[]{:S(2)}) async-start(), calls=%async_computation.9 | async-start | bytes 5242880 | tf_op jit(solution)/shard_map/reduce_scatter | solution.py:472
  600.3 41.7 %collective-permute-start.54 = (bf16[1024,2048]{1,0:T(8,128)(2,1)}, bf16[1024,2048]{1,0:T(8,128)(2,1)}, u32[]{:S(2)}, u32[]{:S(2)}) collective-permute-start(bf16[1024,2048]{1,0:T(8,128)(2,1)} %convolution_convert_fusion), channel_id=1, source_target_pairs={{0,1},{1,0},{2,3},{3,2},{4,5},{5,4},{6,7},{7,6},{8,9},{9,8},{10,11... | collective-permute-start | bytes 12582920 | tf_op jit(solution)/shard_map/ppermute | solution.py:17
  604.4 25.5 %collective-permute-start.90 = (bf16[512,512]{1,0:T(8,128)(2,1)}, bf16[512,512]{1,0:T(8,128)(2,1)S(1)}, u32[]{:S(2)}, u32[]{:S(2)}) collective-permute-start(bf16[512,512]{1,0:T(8,128)(2,1)} %reduce-scatter.14.cloned.1.call-done), channel_id=1, source_target_pairs={{0,2},{2,0},{4,6},{6,4},{1,3},{3,1},{5,7},{7,5},{8,10},{10,8},{12,... | collective-permute-start | bytes 1572872 | tf_op jit(solution)/shard_map/ppermute | solution.py:21
  606.3 22.9 %collective-permute-start.91 = (bf16[512,512]{1,0:T(8,128)(2,1)S(1)}, bf16[512,512]{1,0:T(8,128)(2,1)S(1)}, u32[]{:S(2)}, u32[]{:S(2)}) collective-permute-start(bf16[512,512]{1,0:T(8,128)(2,1)S(1)} %copy-done.31), channel_id=1, source_target_pairs={{0,4},{2,6},{4,0},{6,2},{1,5},{3,7},{5,1},{7,3},{8,12},{10,14},{12... | collective-permute-start | bytes 1572872 | tf_op jit(solution)/shard_map/ppermute | solution.py:21
  667.5 49.3 %collective-permute-start.58 = (bf16[256,2048]{1,0:T(8,128)(2,1)}, bf16[256,2048]{1,0:T(8,128)(2,1)S(1)}, u32[]{:S(2)}, u32[]{:S(2)}) collective-permute-start(bf16[256,2048]{1,0:T(8,128)(2,1)} %pad_maximum_fusion.16), channel_id=1, source_target_pairs={{0,4},{2,6},{4,0},{6,2},{1,5},{3,7},{5,1},{7,3},{8,12},{10,14},{12... | collective-permute-start | bytes 3145736 | tf_op jit(solution)/shard_map/ppermute | solution.py:21
  669.3 47.5 %collective-permute-start.56 = (bf16[256,2048]{1,0:T(8,128)(2,1)}, bf16[256,2048]{1,0:T(8,128)(2,1)S(1)}, u32[]{:S(2)}, u32[]{:S(2)}) collective-permute-start(bf16[256,2048]{1,0:T(8,128)(2,1)} %pad_maximum_fusion.15), channel_id=1, source_target_pairs={{0,2},{2,0},{4,6},{6,4},{1,3},{3,1},{5,7},{7,5},{8,10},{10,8},{12,... | collective-permute-start | bytes 3145736 | tf_op jit(solution)/shard_map/ppermute | solution.py:21
  676.8 27.1 %collective-permute-start.78 = (bf16[256,512]{1,0:T(8,128)(2,1)S(1)}, bf16[256,512]{1,0:T(8,128)(2,1)S(1)}, u32[]{:S(2)}, u32[]{:S(2)}) collective-permute-start(bf16[256,512]{1,0:T(8,128)(2,1)S(1)} %slice.517), channel_id=1, source_target_pairs={{0,2},{2,0},{4,6},{6,4},{1,3},{3,1},{5,7},{7,5},{8,10},{10,8},{12,... | collective-permute-start | bytes 786440 | tf_op jit(solution)/shard_map/ppermute | solution.py:21
  677.5 28.3 %collective-permute-start.77 = (bf16[256,512]{1,0:T(8,128)(2,1)S(1)}, bf16[256,512]{1,0:T(8,128)(2,1)}, u32[]{:S(2)}, u32[]{:S(2)}) collective-permute-start(bf16[256,512]{1,0:T(8,128)(2,1)S(1)} %slice.516), channel_id=1, source_target_pairs={{0,4},{2,6},{4,0},{6,2},{1,5},{3,7},{5,1},{7,3},{8,12},{10,14},{12... | collective-permute-start | bytes 786440 | tf_op jit(solution)/shard_map/ppermute | solution.py:21
  679.3 36.8 %collective-permute-start.80 = (bf16[512,512]{1,0:T(8,128)(2,1)}, bf16[512,512]{1,0:T(8,128)(2,1)S(1)}, u32[]{:S(2)}, u32[]{:S(2)}) collective-permute-start(bf16[512,512]{1,0:T(8,128)(2,1)} %reduce-scatter.10.cloned.1.call-done), channel_id=1, source_target_pairs={{0,2},{2,0},{4,6},{6,4},{1,3},{3,1},{5,7},{7,5},{8,10},{10,8},{12,... | collective-permute-start | bytes 1572872 | tf_op jit(solution)/shard_map/ppermute | solution.py:21
  739.6 25.0 %collective-permute-start.62 = (bf16[512,1024]{1,0:T(8,128)(2,1)}, bf16[512,1024]{1,0:T(8,128)(2,1)S(1)}, u32[]{:S(2)}, u32[]{:S(2)}) collective-permute-start(bf16[512,1024]{1,0:T(8,128)(2,1)} %reduce-scatter.6.cloned.1.call-done), channel_id=1, source_target_pairs={{0,2},{2,0},{4,6},{6,4},{1,3},{3,1},{5,7},{7,5},{8,10},{10,8},{12,... | collective-permute-start | bytes 3145736 | tf_op jit(solution)/shard_map/ppermute | solution.py:21
  741.5 23.1 %collective-permute-start.63 = (bf16[512,1024]{1,0:T(8,128)(2,1)}, bf16[512,1024]{1,0:T(8,128)(2,1)S(1)}, u32[]{:S(2)}, u32[]{:S(2)}) collective-permute-start(bf16[512,1024]{1,0:T(8,128)(2,1)} %reduce-scatter.6.cloned.1.call-done), channel_id=1, source_target_pairs={{0,4},{2,6},{4,0},{6,2},{1,5},{3,7},{5,1},{7,3},{8,12},{10,14},{12... | collective-permute-start | bytes 3145736 | tf_op jit(solution)/shard_map/ppermute | solution.py:21
  (105 other events, 1342.9 us)
Sparse Core Ops, SparseCore 0:
  11.2 143.0 all-gather.4
  156.4 44.2 all-gather.6
  228.6 48.9 all-gather.8
  279.6 44.6 all-gather.10
  390.1 43.9 reduce-scatter.11
  443.9 45.1 reduce-scatter.13
  501.0 48.1 reduce-scatter.7
  573.7 41.9 reduce-scatter.9
  618.6 76.0 reduce-scatter.5

commit v5 on v4

--- a/solution.py
+++ b/solution.py
@@ -754,7 +754,8 @@
         lax.dynamic_update_slice(jnp.zeros((4 * part,), F32), piece, (place * part,))
         for piece in (over_cores[:part], groupscale_grad, groupshift_grad)
     ]
-    sums = total(jnp.concatenate([over_cores[part:]] + spaced))
+    sums = jnp.concatenate([over_cores[part:]] + spaced)
+    sums = total(after(sums, *first_near))
     cuts = [width * at for at in range(1, 5)] + [4 * width + 4 * part, 4 * width + 8 * part]
     prescale_sum, postscale_sum, postshift_sum, outputbias_sum, hiddenbias_sum, scale_sum, shift_sum = (
         jnp.split(sums, cuts)

time: 810 us -> 818 us (level)
    ppermute x4, waiting for transfers between devices: 9.59 us -> 24.4 us  [total(): lax.ppermute(value, axis, [(place, place ^ step) for place in range(count)])]
    ppermute x61, waiting for transfers between devices: 217 us -> 205 us  [swap_batch(): lax.ppermute(value, 'batch', [(place, place ^ mask) for place in range(4)])]
    unnamed x130 -> x138, local copies, waits for them, and re-layouts: 45.3 us -> 48.6 us
  transfers between devices with their start and end apart: 103 -> 103, of which waited for: 53 -> 49; matrix products, arithmetic and copies ran while one was open for 31% -> 31% of each run, Pallas kernels for 5% -> 5%
where the time goes in v5:
time: 818 us; the launch traced here: 809 us
  waiting for transfers between devices  363 us (44%)
  matrix products  111 us (14%)
  local copies, waits for them, and re-layouts  107 us (13%)
  starting transfers between devices  107 us (13%)
  other arithmetic  62.7 us (8%)
  Pallas kernels  42.9 us (5%)
  between operations  16 us (2%)
    ppermute x61, waiting for transfers between devices, swap_batch(): lax.ppermute(value, 'batch', [(place, place ^ mask) for place in range(4)])  205 us
    ppermute x12, waiting for transfers between devices, turn(): lax.ppermute(value, 'seq', [(source, (source + steps) % count) for source...  95.4 us
    ppermute x61, starting transfers between devices, swap_batch(): lax.ppermute(value, 'batch', [(place, place ^ mask) for place in range(4)])  67.2 us
    unnamed x138, local copies, waits for them, and re-layouts  48.6 us
    dot_general x8, matrix products, contract_cols(): lax.dot_general(left, right, (((1,), (1,)), ((), ())), preferred_element_...  45.2 us
    dot_general x5, matrix products, contract_rows(): lax.dot_general(left, right, (((0,), (0,)), ((), ())), preferred_element_...  43.7 us
    pallas_call x2, Pallas kernels, by_block(): pl.pallas_call(kernel, grid=(4,), in_specs=[block_spec(v, at in shared, l...  42.9 us
    all_gather x2, waiting for transfers between devices, gather_cols(): return lax.all_gather(weight, 'seq', axis=1, tiled=True)  28 us
  transfers between devices with their start and end apart: 103, of which 49 were waited for; matrix products, arithmetic and copies ran while one was open for 31% of the time, Pallas kernels for 5%

profile of v5, /device:TPU:0, one launch (start us, length us, event | category | flops | bytes accessed | tf_op | source)
XLA Modules:
  0.0 808.7 jit_solution(355493127244788723)
XLA Ops:
  15.0 3.9 collective-permute-start.2
  23.7 9.0 %collective-permute-done.2 = bf16[136,2048]{1,0:T(8,128)(2,1)S(1)} collective-permute-done((bf16[136,2048]{1,0:T(8,128)(2,1)}, bf16[136,2048]{1,0:T(8,128)(2,1)S(1)}, u32[]{:S(2)}, u32[]{:S(2)}) %collective-permute-start.2) | collective-permute-done | bytes 557088 | tf_op jit(solution)/shard_map/ppermute | solution.py:21
  32.6 11.2 %collective-permute-done.1 = bf16[136,2048]{1,0:T(8,128)(2,1)} collective-permute-done((bf16[136,2048]{1,0:T(8,128)(2,1)}, bf16[136,2048]{1,0:T(8,128)(2,1)}, u32[]{:S(2)}, u32[]{:S(2)}) %collective-permute-start.1) | collective-permute-done | bytes 557088 | tf_op jit(solution)/shard_map/ppermute | solution.py:21
  51.6 12.4 %collective-permute-done.3 = bf16[1,72,2048]{2,1,0:T(8,128)(2,1)S(1)} collective-permute-done((bf16[1,72,2048]{2,1,0:T(8,128)(2,1)S(1)}, bf16[1,72,2048]{2,1,0:T(8,128)(2,1)S(1)}, u32[]{:S(2)}, u32[]{:S(2)}) %collective-permute-start.3) | collective-permute-done | bytes 294944 | tf_op jit(solution)/shard_map/ppermute | solution.py:68
  64.0 21.0 %collective-permute-done.4 = bf16[1,72,2048]{2,1,0:T(8,128)(2,1)S(1)} collective-permute-done((bf16[1,72,2048]{2,1,0:T(8,128)(2,1)S(1)}, bf16[1,72,2048]{2,1,0:T(8,128)(2,1)S(1)}, u32[]{:S(2)}, u32[]{:S(2)}) %collective-permute-start.4) | collective-permute-done | bytes 294944 | tf_op jit(solution)/shard_map/ppermute | solution.py:68
  94.1 18.3 %collective-permute-done.6 = bf16[256,2048]{1,0:T(8,128)(2,1)} collective-permute-done((bf16[256,2048]{1,0:T(8,128)(2,1)}, bf16[256,2048]{1,0:T(8,128)(2,1)}, u32[]{:S(2)}, u32[]{:S(2)}) %collective-permute-start.6) | collective-permute-done | bytes 1048608 | tf_op jit(solution)/shard_map/ppermute | solution.py:21
  121.2 4.3 collective-permute-done.8
  131.6 5.5 multiply_sine_fusion
  147.8 6.4 all-gather.5.cloned.1.call-done.weight
  154.3 24.4 %shard_map.297 = (bf16[2,4,4,64,256]{4,3,2,1,0:T(8,128)(2,1)}, bf16[2,4,4,64,256]{4,3,2,1,0:T(8,128)(2,1)}, bf16[2,4,4,64,512]{4,3,2,1,0:T(8,128)(2,1)}, bf16[4,...) custom-call(bf16[2,4,4,64,2048]{4,3,2,1,0:T(8,128)(2,1)} %bitcast.13, ...), custom_call_target="tpu_custom_call" | custom-call | tf_op jit(solution)/shard_map/pallas_call | solution.py:328
  187.4 13.3 %all-gather.7.cloned.1.call-done = bf16[512,2048]{1,0:T(8,128)(2,1)} async-done(((bf16[512,512]{1,0:T(8,128)(2,1)}), bf16[512,2048]{1,0:T(8,128)(2,1)}) %all-gather.7.cloned.1.call-update) | async-done | bytes 2097168 | tf_op jit(solution)/shard_map/all_gather | solution.py:469
  202.1 6.8 collective-permute-start.27
  211.2 4.4 collective-permute-done.26
  215.6 10.9 %collective-permute-done.27 = bf16[1,64,2048]{2,1,0:T(8,128)(2,1)S(1)} collective-permute-done((bf16[1,64,2048]{2,1,0:T(8,128)(2,1)S(1)}, bf16[1,64,2048]{2,1,0:T(8,128)(2,1)S(1)}, u32[]{:S(2)}, u32[]{:S(2)}) %collective-permute-start.27) | collective-permute-done | bytes 262176 | tf_op jit(solution)/shard_map/ppermute | solution.py:68
  228.4 10.4 %all-gather.11.cloned.1.call-start = ((), (), s32[]{:S(2)}) async-start(), calls=%async_computation.8 | async-start | bytes 2621440 | tf_op jit(solution)/shard_map/all_gather | solution.py:469
  250.3 12.7 %collective-permute-done.16 = bf16[128,2048]{1,0:T(8,128)(2,1)S(1)} collective-permute-done((bf16[128,2048]{1,0:T(8,128)(2,1)S(1)}, bf16[128,2048]{1,0:T(8,128)(2,1)S(1)}, u32[]{:S(2)}, u32[]{:S(2)}) %collective-permute-start.16) | collective-permute-done | bytes 524320 | tf_op jit(solution)/shard_map/ppermute | solution.py:21
  276.8 13.9 %collective-permute-done.19 = bf16[256,2048]{1,0:T(8,128)(2,1)} collective-permute-done((bf16[256,2048]{1,0:T(8,128)(2,1)}, bf16[256,2048]{1,0:T(8,128)(2,1)}, u32[]{:S(2)}, u32[]{:S(2)}) %collective-permute-start.19) | collective-permute-done | bytes 1048608 | tf_op jit(solution)/shard_map/ppermute | solution.py:21
  309.5 14.7 %all-gather.11.cloned.1.call-done = bf16[512,2048]{1,0:T(8,128)(2,1)} async-done(((bf16[512,512]{1,0:T(8,128)(2,1)}), bf16[512,2048]{1,0:T(8,128)(2,1)}) %all-gather.11.cloned.1.call-update) | async-done | bytes 2097168 | tf_op jit(solution)/shard_map/all_gather | solution.py:469
  334.5 6.7 collective-permute-done.22
  346.6 6.1 multiply_convert_fusion
  352.9 9.5 %convert_reduce_fusion = (f32[1024]{0:T(1024)S(1)}, bf16[1024,1024]{1,0:T(8,128)(2,1)S(1)}) fusion(f32[1024,1024]{1,0:T(8,128)S(1)} %get-tuple-element.230, f32[1024]{0:T(1024)S(1)} %pad_maximum_fusion.19, bf16[1024,2048]{1,0:T(8,128)(2,1)} %constant_dynamic-update-slice_fusion.25, bf16[1024,2048]{1,0:T(8,128)(2,1)S(1)} %constant_dynamic-update-slice_fusion.30), kind=kOutput, calls=%fused_computation.20 | convolution fusion | flops 4308597760 | bytes 14688256 | tf_op jit(solution)/shard_map/dot_general | solution.py:101
  363.8 4.6 fusion.94
  373.5 8.6 %collective-permute-done.34 = bf16[128,2048]{1,0:T(8,128)(2,1)S(1)} collective-permute-done((bf16[128,2048]{1,0:T(8,128)(2,1)S(1)}, bf16[128,2048]{1,0:T(8,128)(2,1)S(1)}, u32[]{:S(2)}, u32[]{:S(2)}) %collective-permute-start.34) | collective-permute-done | bytes 524320 | tf_op jit(solution)/shard_map/ppermute | solution.py:21
  390.0 7.5 fusion.95
  397.9 9.7 %collective-permute-done.37 = bf16[256,2048]{1,0:T(8,128)(2,1)} collective-permute-done((bf16[256,2048]{1,0:T(8,128)(2,1)}, bf16[256,2048]{1,0:T(8,128)(2,1)}, u32[]{:S(2)}, u32[]{:S(2)}) %collective-permute-start.37) | collective-permute-done | bytes 1048608 | tf_op jit(solution)/shard_map/ppermute | solution.py:21
  409.9 3.9 multiply_reduce_fusion
  418.6 20.6 %collective-permute-done.38 = bf16[256,2048]{1,0:T(8,128)(2,1)S(1)} collective-permute-done((bf16[256,2048]{1,0:T(8,128)(2,1)}, bf16[256,2048]{1,0:T(8,128)(2,1)S(1)}, u32[]{:S(2)}, u32[]{:S(2)}) %collective-permute-start.38) | collective-permute-done | bytes 1048608 | tf_op jit(solution)/shard_map/ppermute | solution.py:21
  460.3 4.9 convolution_convert_fusion.5
  472.1 18.6 %shard_map.298 = (bf16[2,4,4,64,1536]{4,3,2,1,0:T(8,128)(2,1)}, f32[2,512]{1,0:T(2,128)}) custom-call(bf16[4,4,64,512]{3,2,1,0:T(8,128)(2,1)} %bitcast.115, bf16[4,4,64,512]{3,2,1,0:T(8,128)(2,1)} %bitcast.120, f32[2,4,4,64,512]{4,3,2,1,0:T(8,128)} %get-tuple-element.83.gate, f32[2,4,4,64,512]{4,3,2,1,0:T(8,128)} %get-tuple-element.84.unit, ...), custom_call_target="tpu_custom_call" | custom-call | tf_op jit(solution)/shard_map/pallas_call | solution.py:328
  490.7 10.0 %convolution_convert_fusion.1 = bf16[2048,512]{1,0:T(8,128)(2,1)} fusion(bf16[2048,2048]{1,0:T(8,128)(2,1)} %constant_dynamic-update-slice_fusion.2, bf16[2048,1536]{1,0:T(8,128)(2,1)} %bitcast.143), kind=kOutput, calls=%fused_computation.26 | convolution fusion | flops 4296015872 | bytes 12582912 | tf_op jit(solution)/shard_map/dot_general | solution.py:97
  507.5 7.1 fusion.74
  515.0 14.0 %collective-permute-done.45 = bf16[256,2048]{1,0:T(8,128)(2,1)} collective-permute-done((bf16[256,2048]{1,0:T(8,128)(2,1)}, bf16[256,2048]{1,0:T(8,128)(2,1)}, u32[]{:S(2)}, u32[]{:S(2)}) %collective-permute-start.45) | collective-permute-done | bytes 1048608 | tf_op jit(solution)/shard_map/ppermute | solution.py:21
  537.0 4.0 collective-permute-start.47
  541.0 7.8 collective-permute-done.46
  548.8 17.8 %collective-permute-done.47 = bf16[1,64,2048]{2,1,0:T(8,128)(2,1)S(1)} collective-permute-done((bf16[1,64,2048]{2,1,0:T(8,128)(2,1)S(1)}, bf16[1,64,2048]{2,1,0:T(8,128)(2,1)S(1)}, u32[]{:S(2)}, u32[]{:S(2)}) %collective-permute-start.47) | collective-permute-done | bytes 262176 | tf_op jit(solution)/shard_map/ppermute | solution.py:68
  573.5 14.4 %fusion.11 = bf16[2048,1024]{1,0:T(8,128)(2,1)} fusion(bf16[2048,2048]{1,0:T(8,128)(2,1)} %constant_dynamic-update-slice_fusion.2, bf16[2048,1536]{1,0:T(8,128)(2,1)} %bitcast.144), kind=kOutput, calls=%fused_computation.24 | convolution fusion | flops 8592031744 | bytes 16777216 | tf_op jit(solution)/shard_map/dot_general | solution.py:97
  589.0 11.1 %convolution_convert_fusion = bf16[1024,2048]{1,0:T(8,128)(2,1)} fusion(bf16[2048,1536]{1,0:T(8,128)(2,1)} %all-gather.5.cloned.1.call-done.weight, bf16[2048,1536]{1,0:T(8,128)(2,1)} %bitcast.145), kind=kOutput, calls=%fused_computation.23 | convolution fusion | flops 6444548096 | bytes 13631488 | tf_op jit(solution)/shard_map/dot_general | solution.py:101
  610.9 6.9 collective-permute-done.86
  620.0 9.1 %collective-permute-done.91 = bf16[512,512]{1,0:T(8,128)(2,1)S(1)} collective-permute-done((bf16[512,512]{1,0:T(8,128)(2,1)S(1)}, bf16[512,512]{1,0:T(8,128)(2,1)S(1)}, u32[]{:S(2)}, u32[]{:S(2)}) %collective-permute-start.91) | collective-permute-done | bytes 524320 | tf_op jit(solution)/shard_map/ppermute | solution.py:21
  641.9 3.7 convert_element_type.356
  656.2 9.1 %fusion.93 = (bf16[768,2048]{1,0:T(8,128)(2,1)S(1)}, f32[768,2048]{1,0:T(8,128)S(1)}) fusion(f32[1024,2048]{1,0:T(8,128)} %copy-done.7, bf16[2048,1536]{1,0:T(8,128)(2,1)} %all-gather.5.cloned.1.call-done.weight, bf16[2048,1536]{1,0:T(8,128)(2,1)} %bitcast.147), kind=kOutput, calls=%fused_computation.345 | convolution fusion | flops 4834983936 | bytes 24379392 | tf_op jit(solution)/shard_map/dot_general | solution.py:101
  674.0 4.2 collective-permute-done.76
  682.9 24.8 %collective-permute-done.78 = bf16[256,512]{1,0:T(8,128)(2,1)S(1)} collective-permute-done((bf16[256,512]{1,0:T(8,128)(2,1)S(1)}, bf16[256,512]{1,0:T(8,128)(2,1)S(1)}, u32[]{:S(2)}, u32[]{:S(2)}) %collective-permute-start.78) | collective-permute-done | bytes 262176 | tf_op jit(solution)/shard_map/ppermute | solution.py:21
  734.2 5.3 collective-permute-done.59
  739.5 14.7 %collective-permute-done.60 = bf16[1,64,2048]{2,1,0:T(8,128)(2,1)S(1)} collective-permute-done((bf16[1,64,2048]{2,1,0:T(8,128)(2,1)S(1)}, bf16[1,64,2048]{2,1,0:T(8,128)(2,1)S(1)}, u32[]{:S(2)}, u32[]{:S(2)}) %collective-permute-start.60) | collective-permute-done | bytes 262176 | tf_op jit(solution)/shard_map/ppermute | solution.py:68
  759.7 9.5 %collective-permute-done.69 = f32[14336]{0:T(1024)S(1)} collective-permute-done((f32[14336]{0:T(1024)S(1)}, f32[14336]{0:T(1024)S(1)}, u32[]{:S(2)}, u32[]{:S(2)}) %collective-permute-start.69) | collective-permute-done | bytes 57376 | tf_op jit(solution)/shard_map/ppermute | solution.py:60
  770.7 10.0 %collective-permute-done.70 = f32[14336]{0:T(1024)S(1)} collective-permute-done((f32[14336]{0:T(1024)S(1)}, f32[14336]{0:T(1024)S(1)}, u32[]{:S(2)}, u32[]{:S(2)}) %collective-permute-start.70) | collective-permute-done | bytes 57376 | tf_op jit(solution)/shard_map/ppermute | solution.py:60
  792.5 4.6 collective-permute-done.74
  (551 shorter events, 300.4 us)
Async XLA Ops:
  7.2 147.0 %all-gather.5.cloned.1.call-start = ((), (), s32[]{:S(2)}) async-start(), calls=%async_computation.5 | async-start | bytes 7864320 | tf_op jit(solution)/shard_map/all_gather | solution.py:466
  11.0 189.6 %all-gather.7.cloned.1.call-start = ((), (), s32[]{:S(2)}) async-start(), calls=%async_computation.6 | async-start | bytes 2621440 | tf_op jit(solution)/shard_map/all_gather | solution.py:469
  18.9 24.9 %collective-permute-start.1 = (bf16[136,2048]{1,0:T(8,128)(2,1)}, bf16[136,2048]{1,0:T(8,128)(2,1)}, u32[]{:S(2)}, u32[]{:S(2)}) collective-permute-start(bf16[136,2048]{1,0:T(8,128)(2,1)} %get-tuple-element.199), channel_id=1, source_target_pairs={{0,4},{2,6},{4,0},{6,2},{1,5},{3,7},{5,1},{7,3},{8,12},{10,14},{12... | collective-permute-start | bytes 1671176 | tf_op jit(solution)/shard_map/ppermute | solution.py:21
  19.4 24.7 %collective-permute-start = (bf16[136,2048]{1,0:T(8,128)(2,1)}, bf16[136,2048]{1,0:T(8,128)(2,1)}, u32[]{:S(2)}, u32[]{:S(2)}) collective-permute-start(bf16[136,2048]{1,0:T(8,128)(2,1)} %get-tuple-element.198), channel_id=1, source_target_pairs={{0,2},{2,0},{4,6},{6,4},{1,3},{3,1},{5,7},{7,5},{8,10},{10,8},{12,... | collective-permute-start | bytes 1671176 | tf_op jit(solution)/shard_map/ppermute | solution.py:21
  47.6 37.4 %collective-permute-start.4 = (bf16[1,72,2048]{2,1,0:T(8,128)(2,1)S(1)}, bf16[1,72,2048]{2,1,0:T(8,128)(2,1)S(1)}, u32[]{:S(2)}, u32[]{:S(2)}) collective-permute-start(bf16[1,72,2048]{2,1,0:T(8,128)(2,1)S(1)} %get-tuple-element.147), channel_id=1, source_target_pairs={{0,16},{8,24},{16,0},{24,8},{1,17},{9,25},{17,1},{25,9},{2,18},{10... | collective-permute-start | bytes 884744 | tf_op jit(solution)/shard_map/ppermute | solution.py:68
  50.2 36.0 %collective-permute-start.5 = (bf16[1,72,2048]{2,1,0:T(8,128)(2,1)S(1)}, bf16[1,72,2048]{2,1,0:T(8,128)(2,1)S(1)}, u32[]{:S(2)}, u32[]{:S(2)}) collective-permute-start(bf16[1,72,2048]{2,1,0:T(8,128)(2,1)S(1)} %get-tuple-element.146), channel_id=1, source_target_pairs={{0,24},{8,0},{16,8},{24,16},{1,25},{9,1},{17,9},{25,17},{2,26},{10... | collective-permute-start | bytes 884744 | tf_op jit(solution)/shard_map/ppermute | solution.py:68
  87.9 24.5 %collective-permute-start.6 = (bf16[256,2048]{1,0:T(8,128)(2,1)}, bf16[256,2048]{1,0:T(8,128)(2,1)}, u32[]{:S(2)}, u32[]{:S(2)}) collective-permute-start(bf16[256,2048]{1,0:T(8,128)(2,1)} %multiply_convert_fusion.1), channel_id=1, source_target_pairs={{0,2},{2,0},{4,6},{6,4},{1,3},{3,1},{5,7},{7,5},{8,10},{10,8},{12,... | collective-permute-start | bytes 3145736 | tf_op jit(solution)/shard_map/ppermute | solution.py:21
  89.4 25.7 %collective-permute-start.7 = (bf16[256,2048]{1,0:T(8,128)(2,1)}, bf16[256,2048]{1,0:T(8,128)(2,1)}, u32[]{:S(2)}, u32[]{:S(2)}) collective-permute-start(bf16[256,2048]{1,0:T(8,128)(2,1)} %multiply_convert_fusion.1), channel_id=1, source_target_pairs={{0,4},{2,6},{4,0},{6,2},{1,5},{3,7},{5,1},{7,3},{8,12},{10,14},{12... | collective-permute-start | bytes 3145736 | tf_op jit(solution)/shard_map/ppermute | solution.py:21
  89.9 48.6 %collective-permute-start.10 = (bf16[256,2048]{1,0:T(8,128)(2,1)}, bf16[256,2048]{1,0:T(8,128)(2,1)}, u32[]{:S(2)}, u32[]{:S(2)}) collective-permute-start(bf16[256,2048]{1,0:T(8,128)(2,1)} %multiply_convert_fusion.1), channel_id=1, source_target_pairs={{0,1},{1,0},{2,3},{3,2},{4,5},{5,4},{6,7},{7,6},{8,9},{9,8},{10,11... | collective-permute-start | bytes 3145736 | tf_op jit(solution)/shard_map/ppermute | solution.py:17
  130.0 173.4 %all-gather.9.cloned.1.call-start = ((), (), s32[]{:S(2)}) async-start(), calls=%async_computation.7 | async-start | bytes 2621440 | tf_op jit(solution)/shard_map/all_gather | solution.py:466
  200.7 39.9 %collective-permute-start.15 = (bf16[512,2048]{1,0:T(8,128)(2,1)}, bf16[512,2048]{1,0:T(8,128)(2,1)}, u32[]{:S(2)}, u32[]{:S(2)}) collective-permute-start(bf16[512,2048]{1,0:T(8,128)(2,1)} %all-gather.7.cloned.1.call-done), channel_id=1, source_target_pairs={{0,1},{1,0},{2,3},{3,2},{4,5},{5,4},{6,7},{7,6},{8,9},{9,8},{10,11... | collective-permute-start | bytes 6291464 | tf_op jit(solution)/shard_map/ppermute | solution.py:17
  202.1 24.4 %collective-permute-start.27 = (bf16[1,64,2048]{2,1,0:T(8,128)(2,1)S(1)}, bf16[1,64,2048]{2,1,0:T(8,128)(2,1)S(1)}, u32[]{:S(2)}, u32[]{:S(2)}) collective-permute-start(bf16[1,64,2048]{2,1,0:T(8,128)(2,1)S(1)} %get-tuple-element.179), channel_id=1, source_target_pairs={{0,16},{8,24},{16,0},{24,8},{1,17},{9,25},{17,1},{25,9},{2,18},{10... | collective-permute-start | bytes 786440 | tf_op jit(solution)/shard_map/ppermute | solution.py:68
  226.5 44.1 %collective-permute-start.29 = (bf16[256,2048]{1,0:T(8,128)(2,1)S(1)}, bf16[256,2048]{1,0:T(8,128)(2,1)}, u32[]{:S(2)}, u32[]{:S(2)}) collective-permute-start(bf16[256,2048]{1,0:T(8,128)(2,1)S(1)} %bitcast.106), channel_id=1, source_target_pairs={{0,2},{2,0},{4,6},{6,4},{1,3},{3,1},{5,7},{7,5},{8,10},{10,8},{12,... | collective-permute-start | bytes 3145736 | tf_op jit(solution)/shard_map/ppermute | solution.py:21
  226.8 47.8 %collective-permute-start.30 = (bf16[256,2048]{1,0:T(8,128)(2,1)S(1)}, bf16[256,2048]{1,0:T(8,128)(2,1)}, u32[]{:S(2)}, u32[]{:S(2)}) collective-permute-start(bf16[256,2048]{1,0:T(8,128)(2,1)S(1)} %bitcast.107), channel_id=1, source_target_pairs={{0,4},{2,6},{4,0},{6,2},{1,5},{3,7},{5,1},{7,3},{8,12},{10,14},{12... | collective-permute-start | bytes 3145736 | tf_op jit(solution)/shard_map/ppermute | solution.py:21
  228.4 95.8 %all-gather.11.cloned.1.call-start = ((), (), s32[]{:S(2)}) async-start(), calls=%async_computation.8 | async-start | bytes 2621440 | tf_op jit(solution)/shard_map/all_gather | solution.py:469
  264.3 26.4 %collective-permute-start.19 = (bf16[256,2048]{1,0:T(8,128)(2,1)}, bf16[256,2048]{1,0:T(8,128)(2,1)}, u32[]{:S(2)}, u32[]{:S(2)}) collective-permute-start(bf16[256,2048]{1,0:T(8,128)(2,1)} %pad_maximum_fusion.9), channel_id=1, source_target_pairs={{0,4},{2,6},{4,0},{6,2},{1,5},{3,7},{5,1},{7,3},{8,12},{10,14},{12... | collective-permute-start | bytes 3145736 | tf_op jit(solution)/shard_map/ppermute | solution.py:21
  266.8 26.4 %collective-permute-start.17 = (bf16[256,2048]{1,0:T(8,128)(2,1)}, bf16[256,2048]{1,0:T(8,128)(2,1)}, u32[]{:S(2)}, u32[]{:S(2)}) collective-permute-start(bf16[256,2048]{1,0:T(8,128)(2,1)} %pad_maximum_fusion.8), channel_id=1, source_target_pairs={{0,2},{2,0},{4,6},{6,4},{1,3},{3,1},{5,7},{7,5},{8,10},{10,8},{12,... | collective-permute-start | bytes 3145736 | tf_op jit(solution)/shard_map/ppermute | solution.py:21
  269.3 332.1 %reduce-scatter.12.cloned.1.call-start = ((), (), s32[]{:S(2)}) async-start(), calls=%async_computation.12 | async-start | bytes 2621440 | tf_op jit(solution)/shard_map/reduce_scatter | solution.py:472
  272.8 32.9 %collective-permute-start.31 = (bf16[128,2048]{1,0:T(8,128)(2,1)}, bf16[128,2048]{1,0:T(8,128)(2,1)}, u32[]{:S(2)}, u32[]{:S(2)}) collective-permute-start(bf16[128,2048]{1,0:T(8,128)(2,1)} %slice.477), channel_id=1, source_target_pairs={{0,4},{2,6},{4,0},{6,2},{1,5},{3,7},{5,1},{7,3},{8,12},{10,14},{12... | collective-permute-start | bytes 1572872 | tf_op jit(solution)/shard_map/ppermute | solution.py:21
  276.5 31.1 %collective-permute-start.32 = (bf16[128,2048]{1,0:T(8,128)(2,1)}, bf16[128,2048]{1,0:T(8,128)(2,1)}, u32[]{:S(2)}, u32[]{:S(2)}) collective-permute-start(bf16[128,2048]{1,0:T(8,128)(2,1)} %slice.478), channel_id=1, source_target_pairs={{0,2},{2,0},{4,6},{6,4},{1,3},{3,1},{5,7},{7,5},{8,10},{10,8},{12,... | collective-permute-start | bytes 1572872 | tf_op jit(solution)/shard_map/ppermute | solution.py:21
  298.8 27.4 %collective-permute-start.20 = (bf16[256,2048]{1,0:T(8,128)(2,1)}, bf16[256,2048]{1,0:T(8,128)(2,1)}, u32[]{:S(2)}, u32[]{:S(2)}) collective-permute-start(bf16[256,2048]{1,0:T(8,128)(2,1)} %get-tuple-element.115), channel_id=1, source_target_pairs={{0,2},{2,0},{4,6},{6,4},{1,3},{3,1},{5,7},{7,5},{8,10},{10,8},{12,... | collective-permute-start | bytes 3145736 | tf_op jit(solution)/shard_map/ppermute | solution.py:21
  301.7 27.5 %collective-permute-start.21 = (bf16[256,2048]{1,0:T(8,128)(2,1)}, bf16[256,2048]{1,0:T(8,128)(2,1)}, u32[]{:S(2)}, u32[]{:S(2)}) collective-permute-start(bf16[256,2048]{1,0:T(8,128)(2,1)} %get-tuple-element.115), channel_id=1, source_target_pairs={{0,4},{2,6},{4,0},{6,2},{1,5},{3,7},{5,1},{7,3},{8,12},{10,14},{12... | collective-permute-start | bytes 3145736 | tf_op jit(solution)/shard_map/ppermute | solution.py:21
  303.4 41.3 %collective-permute-start.24 = (bf16[2048,512]{1,0:T(8,128)(2,1)}, bf16[2048,512]{1,0:T(8,128)(2,1)}, u32[]{:S(2)}, u32[]{:S(2)}) collective-permute-start(bf16[2048,512]{1,0:T(8,128)(2,1)} %all-gather.9.cloned.1.call-done), channel_id=1, source_target_pairs={{0,1},{1,0},{2,3},{3,2},{4,5},{5,4},{6,7},{7,6},{8,9},{9,8},{10,11... | collective-permute-start | bytes 6291464 | tf_op jit(solution)/shard_map/ppermute | solution.py:17
  389.9 214.3 %reduce-scatter.14.cloned.1.call-start = ((), (), s32[]{:S(2)}) async-start(), calls=%async_computation.13 | async-start | bytes 2621440 | tf_op jit(solution)/shard_map/reduce_scatter | solution.py:472
  397.9 43.7 %collective-permute-start.89 = (bf16[512,2048]{1,0:T(8,128)(2,1)S(1)}, bf16[512,2048]{1,0:T(8,128)(2,1)S(1)}, u32[]{:S(2)}, u32[]{:S(2)}) collective-permute-start(bf16[512,2048]{1,0:T(8,128)(2,1)S(1)} %slice.656), channel_id=1, source_target_pairs={{0,1},{1,0},{2,3},{3,2},{4,5},{5,4},{6,7},{7,6},{8,9},{9,8},{10,11... | collective-permute-start | bytes 6291464 | tf_op jit(solution)/shard_map/ppermute | solution.py:17
  418.0 25.7 %collective-permute-start.39 = (bf16[256,2048]{1,0:T(8,128)(2,1)}, bf16[256,2048]{1,0:T(8,128)(2,1)}, u32[]{:S(2)}, u32[]{:S(2)}) collective-permute-start(bf16[256,2048]{1,0:T(8,128)(2,1)} %get-tuple-element.113), channel_id=1, source_target_pairs={{0,4},{2,6},{4,0},{6,2},{1,5},{3,7},{5,1},{7,3},{8,12},{10,14},{12... | collective-permute-start | bytes 3145736 | tf_op jit(solution)/shard_map/ppermute | solution.py:21
  443.7 210.4 %reduce-scatter.8.cloned.1.call-start = ((), (), s32[]{:S(2)}) async-start(), calls=%async_computation.10 | async-start | bytes 2621440 | tf_op jit(solution)/shard_map/reduce_scatter | solution.py:472
  500.8 180.7 %reduce-scatter.10.cloned.1.call-start = ((), (), s32[]{:S(2)}) async-start(), calls=%async_computation.11 | async-start | bytes 2621440 | tf_op jit(solution)/shard_map/reduce_scatter | solution.py:472
  503.1 25.9 %collective-permute-start.45 = (bf16[256,2048]{1,0:T(8,128)(2,1)}, bf16[256,2048]{1,0:T(8,128)(2,1)}, u32[]{:S(2)}, u32[]{:S(2)}) collective-permute-start(bf16[256,2048]{1,0:T(8,128)(2,1)} %pad_maximum_fusion.13), channel_id=1, source_target_pairs={{0,4},{2,6},{4,0},{6,2},{1,5},{3,7},{5,1},{7,3},{8,12},{10,14},{12... | collective-permute-start | bytes 3145736 | tf_op jit(solution)/shard_map/ppermute | solution.py:21
  506.0 25.6 %collective-permute-start.43 = (bf16[256,2048]{1,0:T(8,128)(2,1)}, bf16[256,2048]{1,0:T(8,128)(2,1)}, u32[]{:S(2)}, u32[]{:S(2)}) collective-permute-start(bf16[256,2048]{1,0:T(8,128)(2,1)} %pad_maximum_fusion.12), channel_id=1, source_target_pairs={{0,2},{2,0},{4,6},{6,4},{1,3},{3,1},{5,7},{7,5},{8,10},{10,8},{12,... | collective-permute-start | bytes 3145736 | tf_op jit(solution)/shard_map/ppermute | solution.py:21
  515.0 56.4 %collective-permute-start.79 = (bf16[512,2048]{1,0:T(8,128)(2,1)S(1)}, bf16[512,2048]{1,0:T(8,128)(2,1)S(1)}, u32[]{:S(2)}, u32[]{:S(2)}) collective-permute-start(bf16[512,2048]{1,0:T(8,128)(2,1)S(1)} %slice.658), channel_id=1, source_target_pairs={{0,1},{1,0},{2,3},{3,2},{4,5},{5,4},{6,7},{7,6},{8,9},{9,8},{10,11... | collective-permute-start | bytes 6291464 | tf_op jit(solution)/shard_map/ppermute | solution.py:17
  537.0 29.6 %collective-permute-start.47 = (bf16[1,64,2048]{2,1,0:T(8,128)(2,1)S(1)}, bf16[1,64,2048]{2,1,0:T(8,128)(2,1)S(1)}, u32[]{:S(2)}, u32[]{:S(2)}) collective-permute-start(bf16[1,64,2048]{2,1,0:T(8,128)(2,1)S(1)} %get-tuple-element.171), channel_id=1, source_target_pairs={{0,16},{8,24},{16,0},{24,8},{1,17},{9,25},{17,1},{25,9},{2,18},{10... | collective-permute-start | bytes 786440 | tf_op jit(solution)/shard_map/ppermute | solution.py:68
  541.0 25.6 %collective-permute-start.48 = (bf16[1,64,2048]{2,1,0:T(8,128)(2,1)S(1)}, bf16[1,64,2048]{2,1,0:T(8,128)(2,1)S(1)}, u32[]{:S(2)}, u32[]{:S(2)}) collective-permute-start(bf16[1,64,2048]{2,1,0:T(8,128)(2,1)S(1)} %get-tuple-element.170), channel_id=1, source_target_pairs={{0,8},{8,16},{16,24},{24,0},{1,9},{9,17},{17,25},{25,1},{2,10},{10... | collective-permute-start | bytes 786440 | tf_op jit(solution)/shard_map/ppermute | solution.py:68
  573.4 151.7 %reduce-scatter.6.cloned.1.call-start = ((), (), s32[]{:S(2)}) async-start(), calls=%async_computation.9 | async-start | bytes 5242880 | tf_op jit(solution)/shard_map/reduce_scatter | solution.py:472
  600.1 41.7 %collective-permute-start.54 = (bf16[1024,2048]{1,0:T(8,128)(2,1)}, bf16[1024,2048]{1,0:T(8,128)(2,1)}, u32[]{:S(2)}, u32[]{:S(2)}) collective-permute-start(bf16[1024,2048]{1,0:T(8,128)(2,1)} %convolution_convert_fusion), channel_id=1, source_target_pairs={{0,1},{1,0},{2,3},{3,2},{4,5},{5,4},{6,7},{7,6},{8,9},{9,8},{10,11... | collective-permute-start | bytes 12582920 | tf_op jit(solution)/shard_map/ppermute | solution.py:17
  604.3 25.5 %collective-permute-start.90 = (bf16[512,512]{1,0:T(8,128)(2,1)}, bf16[512,512]{1,0:T(8,128)(2,1)S(1)}, u32[]{:S(2)}, u32[]{:S(2)}) collective-permute-start(bf16[512,512]{1,0:T(8,128)(2,1)} %reduce-scatter.14.cloned.1.call-done), channel_id=1, source_target_pairs={{0,2},{2,0},{4,6},{6,4},{1,3},{3,1},{5,7},{7,5},{8,10},{10,8},{12,... | collective-permute-start | bytes 1572872 | tf_op jit(solution)/shard_map/ppermute | solution.py:21
  654.1 25.5 %collective-permute-start.75 = (bf16[512,512]{1,0:T(8,128)(2,1)}, bf16[512,512]{1,0:T(8,128)(2,1)S(1)}, u32[]{:S(2)}, u32[]{:S(2)}) collective-permute-start(bf16[512,512]{1,0:T(8,128)(2,1)} %reduce-scatter.8.cloned.1.call-done), channel_id=1, source_target_pairs={{0,2},{2,0},{4,6},{6,4},{1,3},{3,1},{5,7},{7,5},{8,10},{10,8},{12,... | collective-permute-start | bytes 1572872 | tf_op jit(solution)/shard_map/ppermute | solution.py:21
  671.1 51.5 %collective-permute-start.58 = (bf16[256,2048]{1,0:T(8,128)(2,1)}, bf16[256,2048]{1,0:T(8,128)(2,1)S(1)}, u32[]{:S(2)}, u32[]{:S(2)}) collective-permute-start(bf16[256,2048]{1,0:T(8,128)(2,1)} %pad_maximum_fusion.16), channel_id=1, source_target_pairs={{0,4},{2,6},{4,0},{6,2},{1,5},{3,7},{5,1},{7,3},{8,12},{10,14},{12... | collective-permute-start | bytes 3145736 | tf_op jit(solution)/shard_map/ppermute | solution.py:21
  673.6 49.0 %collective-permute-start.56 = (bf16[256,2048]{1,0:T(8,128)(2,1)}, bf16[256,2048]{1,0:T(8,128)(2,1)S(1)}, u32[]{:S(2)}, u32[]{:S(2)}) collective-permute-start(bf16[256,2048]{1,0:T(8,128)(2,1)} %pad_maximum_fusion.15), channel_id=1, source_target_pairs={{0,2},{2,0},{4,6},{6,4},{1,3},{3,1},{5,7},{7,5},{8,10},{10,8},{12,... | collective-permute-start | bytes 3145736 | tf_op jit(solution)/shard_map/ppermute | solution.py:21
  678.3 29.4 %collective-permute-start.78 = (bf16[256,512]{1,0:T(8,128)(2,1)S(1)}, bf16[256,512]{1,0:T(8,128)(2,1)S(1)}, u32[]{:S(2)}, u32[]{:S(2)}) collective-permute-start(bf16[256,512]{1,0:T(8,128)(2,1)S(1)} %slice.517), channel_id=1, source_target_pairs={{0,2},{2,0},{4,6},{6,4},{1,3},{3,1},{5,7},{7,5},{8,10},{10,8},{12,... | collective-permute-start | bytes 786440 | tf_op jit(solution)/shard_map/ppermute | solution.py:21
  679.6 29.8 %collective-permute-start.77 = (bf16[256,512]{1,0:T(8,128)(2,1)S(1)}, bf16[256,512]{1,0:T(8,128)(2,1)}, u32[]{:S(2)}, u32[]{:S(2)}) collective-permute-start(bf16[256,512]{1,0:T(8,128)(2,1)S(1)} %slice.516), channel_id=1, source_target_pairs={{0,4},{2,6},{4,0},{6,2},{1,5},{3,7},{5,1},{7,3},{8,12},{10,14},{12... | collective-permute-start | bytes 786440 | tf_op jit(solution)/shard_map/ppermute | solution.py:21
  681.5 37.5 %collective-permute-start.80 = (bf16[512,512]{1,0:T(8,128)(2,1)}, bf16[512,512]{1,0:T(8,128)(2,1)S(1)}, u32[]{:S(2)}, u32[]{:S(2)}) collective-permute-start(bf16[512,512]{1,0:T(8,128)(2,1)} %reduce-scatter.10.cloned.1.call-done), channel_id=1, source_target_pairs={{0,2},{2,0},{4,6},{6,4},{1,3},{3,1},{5,7},{7,5},{8,10},{10,8},{12,... | collective-permute-start | bytes 1572872 | tf_op jit(solution)/shard_map/ppermute | solution.py:21
  725.1 29.1 %collective-permute-start.62 = (bf16[512,1024]{1,0:T(8,128)(2,1)}, bf16[512,1024]{1,0:T(8,128)(2,1)S(1)}, u32[]{:S(2)}, u32[]{:S(2)}) collective-permute-start(bf16[512,1024]{1,0:T(8,128)(2,1)} %reduce-scatter.6.cloned.1.call-done), channel_id=1, source_target_pairs={{0,2},{2,0},{4,6},{6,4},{1,3},{3,1},{5,7},{7,5},{8,10},{10,8},{12,... | collective-permute-start | bytes 3145736 | tf_op jit(solution)/shard_map/ppermute | solution.py:21
  726.6 27.6 %collective-permute-start.63 = (bf16[512,1024]{1,0:T(8,128)(2,1)}, bf16[512,1024]{1,0:T(8,128)(2,1)S(1)}, u32[]{:S(2)}, u32[]{:S(2)}) collective-permute-start(bf16[512,1024]{1,0:T(8,128)(2,1)} %reduce-scatter.6.cloned.1.call-done), channel_id=1, source_target_pairs={{0,4},{2,6},{4,0},{6,2},{1,5},{3,7},{5,1},{7,3},{8,12},{10,14},{12... | collective-permute-start | bytes 3145736 | tf_op jit(solution)/shard_map/ppermute | solution.py:21
  754.5 31.5 %collective-permute-start.66 = (bf16[64,2048]{1,0:T(8,128)(2,1)S(1)}, bf16[64,2048]{1,0:T(8,128)(2,1)S(1)}, u32[]{:S(2)}, u32[]{:S(2)}) collective-permute-start(bf16[64,2048]{1,0:T(8,128)(2,1)S(1)} %get-tuple-element.157), channel_id=1, source_target_pairs={{0,6},{2,4},{4,2},{6,0},{1,7},{3,5},{5,3},{7,1},{8,14},{10,12},{12... | collective-permute-start | bytes 786440 | tf_op jit(solution)/shard_map/ppermute | solution.py:21
  755.3 33.7 %collective-permute-start.65 = (bf16[64,2048]{1,0:T(8,128)(2,1)S(1)}, bf16[64,2048]{1,0:T(8,128)(2,1)S(1)}, u32[]{:S(2)}, u32[]{:S(2)}) collective-permute-start(bf16[64,2048]{1,0:T(8,128)(2,1)S(1)} %get-tuple-element.158), channel_id=1, source_target_pairs={{0,4},{2,6},{4,0},{6,2},{1,5},{3,7},{5,1},{7,3},{8,12},{10,14},{12... | collective-permute-start | bytes 786440 | tf_op jit(solution)/shard_map/ppermute | solution.py:21
  756.7 32.3 %collective-permute-start.64 = (bf16[64,2048]{1,0:T(8,128)(2,1)S(1)}, bf16[64,2048]{1,0:T(8,128)(2,1)S(1)}, u32[]{:S(2)}, u32[]{:S(2)}) collective-permute-start(bf16[64,2048]{1,0:T(8,128)(2,1)S(1)} %get-tuple-element.156), channel_id=1, source_target_pairs={{0,2},{2,0},{4,6},{6,4},{1,3},{3,1},{5,7},{7,5},{8,10},{10,8},{12,... | collective-permute-start | bytes 786440 | tf_op jit(solution)/shard_map/ppermute | solution.py:21
  758.9 33.6 %collective-permute-start.73 = (bf16[256,1024]{1,0:T(8,128)(2,1)S(1)}, bf16[256,1024]{1,0:T(8,128)(2,1)S(1)}, u32[]{:S(2)}, u32[]{:S(2)}) collective-permute-start(bf16[256,1024]{1,0:T(8,128)(2,1)S(1)} %slice.432), channel_id=1, source_target_pairs={{0,4},{2,6},{4,0},{6,2},{1,5},{3,7},{5,1},{7,3},{8,12},{10,14},{12... | collective-permute-start | bytes 1572872 | tf_op jit(solution)/shard_map/ppermute | solution.py:21
  (109 other events, 1423.0 us)
Sparse Core Ops, SparseCore 0:
  11.2 143.0 all-gather.4
  156.4 44.2 all-gather.6
  228.5 48.9 all-gather.8
  279.5 44.6 all-gather.10
  390.1 43.9 reduce-scatter.11
  443.8 45.0 reduce-scatter.13
  500.9 48.0 reduce-scatter.7
  573.5 41.9 reduce-scatter.9
  618.4 76.0 reduce-scatter.5
